TPU v7x, 256 devices: a whole 4x4x8 slice. The times are simulated.
256 devices in a mesh: ctx: 32 (over z, y_hi, core), tp: 8 (over x, y_lo).
Axes of the slice: x: 4, y: 4 (y_hi: 2, y_lo: 2; y = y_hi * 2 + y_lo), z: 8, core: 2. Of those that a mesh axis runs over, the one named last changes fastest.
Arguments:
- queries: bfloat16 [4096, 8192], P('ctx', 'tp'), may hold values from -4.375 to 4.375
- stored_keys: bfloat16 [8192, 1024], P('ctx', 'tp'), may hold values from -4.375 to 4.375
- stored_values: bfloat16 [8192, 1024], P('ctx', 'tp'), may hold values from -6 to 6
- fresh_keys: bfloat16 [4096, 1024], P('ctx', 'tp'), may hold values from -6 to 6
- fresh_values: bfloat16 [4096, 1024], P('ctx', 'tp'), may hold values from -6 to 6
- cache_lengths: int32 [32], replicated, may hold values from 1 to 256, 5120 in all
- out_weight: bfloat16 [8192, 8192], P('tp', 'ctx'), may hold values from -0.0625 to 0.0625
Outputs:
- mixed: bfloat16 [4096, 8192], P('tp', 'ctx')
Inputs may be any that keep to these rules, and one draw needn't show every extreme that they name: `cache_lengths`: the longest shard holds exactly 256 used positions.
All inputs are finite; a program needn't handle non-finite values.
Results may differ from a plain program's by a relative error of at most 0.02.
Values may be sent and summed in bfloat16 or wider, within the bound.
No kernel may reach another device: no remote copies, remote signals or barrier semaphores. Data moves between devices by JAX's collectives and lax.ppermute only.
A program may use at most 192 MiB of HBM per device.

v0:
```python
import functools
import math

import jax
import jax.numpy as jnp
from jax import lax
from jax.experimental import pallas as pl
from jax.experimental.pallas import tpu as pltpu
from jax.sharding import Mesh
from jax.sharding import PartitionSpec as P

HEAD = 128
NZ, NY, NC, NX, NL = 8, 2, 2, 4, 2
NEG = -1e30
VMEM = 48 * 1024 * 1024
AXES = ("z", "yh", "core", "x", "yl")
TILE = 256
TAIL = 16
F32 = jnp.float32
BF16 = jnp.bfloat16


def permute(value, move):
    pairs = []
    for z in range(NZ):
        for yh in range(NY):
            for c in range(NC):
                for x in range(NX):
                    for yl in range(NL):
                        z2, yh2, c2, x2, yl2 = move(z, yh, c, x, yl)
                        source = ((z * NY + yh) * NC + c) * NX * NL + x * NL + yl
                        target = (((z2 % NZ) * NY + yh2) * NC + c2) * NX * NL + (x2 % NX) * NL + yl2
                        pairs.append((source, target))
    return lax.ppermute(value, AXES, pairs)


def shift_z(value, step):
    return permute(value, lambda z, yh, c, x, yl: (z + step, yh, c, x, yl))


def shift_x(value, step):
    return permute(value, lambda z, yh, c, x, yl: (z, yh, c, x + step, yl))


def swap(value, a=0, b=0, d=0):
    return permute(value, lambda z, yh, c, x, yl: (z, yh ^ a, c ^ b, x, yl ^ d))


def attend_kernel(shifts, first, last, rows, cache, fresh, meta, lens, q_ref, *refs):
    count = 2 * len(shifts)
    kv_refs, refs = refs[:count], refs[count:]
    if not first:
        acc_in, ml_in = refs[:2]
        refs = refs[2:]
    z, yh, core = meta[0], meta[1], meta[2]
    factor = math.log2(math.e) / math.sqrt(HEAD)
    group = rows // NZ
    strip = group // (NY * NC)
    for start in range(0, rows, TILE):
        q = q_ref[start : start + TILE, :]
        row = start + lax.broadcasted_iota(jnp.int32, (TILE, 1), 0)
        place = (row // group) * (NY * NC * fresh) + ((row % group) // strip) * fresh + z * strip + row % strip
        parts, top = [], None
        for index in range(count):
            zs = lax.rem(z + shifts[index // 2] + NZ, NZ)
            block = zs * NY * NC + yh * NC + (core if index % 2 == 0 else 1 - core)
            s = lax.dot_general(
                q, kv_refs[index][:, :HEAD], (((1,), (1,)), ((), ())), preferred_element_type=F32
            )
            col = lax.broadcasted_iota(jnp.int32, (1, cache), 1)
            stored = s[:, :cache] + jnp.where(col < lens[block], 0.0, NEG)
            col = lax.broadcasted_iota(jnp.int32, (1, fresh), 1)
            new = jnp.where(block * fresh + col <= place, s[:, cache:], NEG)
            s = jnp.concatenate([stored, new], 1)
            parts.append(s)
            for at in range(0, cache + fresh, HEAD):
                piece = s[:, at : at + HEAD]
                top = piece if top is None else jnp.maximum(top, piece)
        m = top.max(axis=1, keepdims=True)
        if first:
            l, acc = 0.0, 0.0
        else:
            before = ml_in[start : start + TILE, 0:1]
            m = jnp.maximum(m, before)
            alpha = jnp.exp2((before - m) * factor)
            l = ml_in[start : start + TILE, 64:65] * alpha
            acc = acc_in[start : start + TILE, :] * alpha
        for index in range(count):
            p = jnp.exp2((parts[index] - m) * factor)
            l = l + p.sum(axis=1, keepdims=True)
            acc = acc + jnp.dot(p.astype(BF16), kv_refs[index][:, HEAD:], preferred_element_type=F32)
        if not last:
            acc_out, ml_out = refs
            acc_out[start : start + TILE, :] = acc
            lane = lax.broadcasted_iota(jnp.int32, (TILE, HEAD), 1)
            ml_out[start : start + TILE, :] = jnp.where(lane < 64, m, l)
            continue
        out_ref = refs[0]
        out = (acc / l).astype(BF16)
        lse = m * factor + jnp.log2(l)
        for at in range(0, TILE, group):
            out_ref[0, (start + at) // group, 0:group, :] = out[at : at + group, :]
        for at in range(0, TILE, 2 * group):
            line = jnp.broadcast_to(lse[at : at + 2 * group, :], (2 * group, HEAD)).T[0:1, :]
            high = line.astype(BF16).astype(F32)
            middle = (line - high).astype(BF16).astype(F32)
            low = line - high - middle
            which = lax.broadcasted_iota(jnp.int32, (TAIL, HEAD), 0)
            tail = jnp.where(which == 0, high, jnp.where(which == 1, middle, low)).astype(BF16)
            for half in range(2):
                out_ref[0, (start + at) // group + half, group : group + TAIL, :] = tail


def attend(meta, lens, q, kvs, shifts, state, last, cache, fresh):
    rows, width = q.shape
    heads = width // HEAD
    group = rows // NZ
    first = state is None
    span = cache + fresh
    whole = pl.BlockSpec((span, 2 * HEAD), lambda h, *_: (0, 0))
    per_head = pl.BlockSpec((rows, HEAD), lambda h, *_: (0, h))
    in_specs = [per_head] + [whole] * len(kvs)
    args = [q] + list(kvs)
    if not first:
        in_specs += [per_head, per_head]
        args += list(state)
    if last:
        pair = heads // NY
        out_specs = pl.BlockSpec((1, NZ, group + TAIL, HEAD), lambda h, *_: (h // pair, 0, 0, h % pair))
        out_shape = jax.ShapeDtypeStruct((NY, NZ, group + TAIL, pair * HEAD), BF16)
    else:
        out_specs = [per_head, per_head]
        out_shape = [jax.ShapeDtypeStruct((rows, width), F32)] * 2
    return pl.pallas_call(
        functools.partial(attend_kernel, tuple(shifts), first, last, rows, cache, fresh),
        grid_spec=pltpu.PrefetchScalarGridSpec(
            num_scalar_prefetch=2, grid=(heads,), in_specs=in_specs, out_specs=out_specs
        ),
        out_shape=out_shape,
        compiler_params=pltpu.CompilerParams(vmem_limit_bytes=VMEM),
        cost_estimate=pl.CostEstimate(
            flops=8 * rows * heads * HEAD * span * len(kvs),
            bytes_accessed=4 * rows * width,
            transcendentals=rows * heads * span * len(kvs),
        ),
    )(meta, lens, *args)


def combine_kernel(group, meta, pieces, out):
    x, yl = meta[3], meta[4]

    def one(t, _):
        spot = lax.rem(t // NL - x + NX, NX) * NL + lax.rem(t + yl, NL)
        for at in range(0, pieces.shape[2], HEAD):
            values, weights = [], []
            for half in range(NY):
                tail = pieces[half * NX * NL + t, group:, at : at + HEAD].astype(F32)
                line = tail[0:1, :] + tail[1:2, :] + tail[2:3, :]
                wide = jnp.broadcast_to(line, (HEAD, HEAD)).T
                weights.append(jnp.where(yl == 0, wide[:group, :], wide[group : 2 * group, :]))
                values.append(pieces[half * NX * NL + t, 0:group, at : at + HEAD].astype(F32))
            top = jnp.maximum(weights[0], weights[1])
            a, b = jnp.exp2(weights[0] - top), jnp.exp2(weights[1] - top)
            joined = (values[0] * a + values[1] * b) / (a + b)
            out[:, pl.ds(pl.multiple_of(spot * pieces.shape[2] + at, HEAD), HEAD)] = joined.astype(BF16)
        return 0

    lax.fori_loop(0, NX * NL, one, 0, unroll=True)


def combine(meta, pieces):
    group, width = pieces.shape[1] - TAIL, pieces.shape[2]
    return pl.pallas_call(
        functools.partial(combine_kernel, group),
        in_specs=[pl.BlockSpec(memory_space=pltpu.SMEM), pl.BlockSpec(memory_space=pltpu.VMEM)],
        out_specs=pl.BlockSpec(memory_space=pltpu.VMEM),
        out_shape=jax.ShapeDtypeStruct((group, NX * NL * width), BF16),
        compiler_params=pltpu.CompilerParams(vmem_limit_bytes=VMEM),
    )(meta, pieces)


def project_kernel(count, *refs):
    blocks, weights, (keep, send) = refs[:count], refs[count:-2], refs[-2:]
    depth = weights[0].shape[0]
    total = None
    for at, weight in enumerate(weights):
        a = jnp.concatenate([block[:, at * depth : (at + 1) * depth] for block in blocks], 0)
        term = jnp.dot(a, weight[...], preferred_element_type=F32)
        total = term if total is None else total + term

    @pl.when(pl.program_id(0) < 2)
    def _():
        keep[...] = total

    @pl.when(pl.program_id(0) >= 2)
    def _():
        send[...] = total.astype(BF16)


def project(blocks, weights):
    rows = blocks[0].shape[0] * len(blocks)
    depth, width = weights[0].shape
    tile = width // 4
    whole = pl.BlockSpec(blocks[0].shape, lambda j: (0, 0))
    column = pl.BlockSpec((depth, tile), lambda j: (0, j))
    return pl.pallas_call(
        functools.partial(project_kernel, len(blocks)),
        grid=(4,),
        in_specs=[whole] * len(blocks) + [column] * len(weights),
        out_specs=[
            pl.BlockSpec((rows, tile), lambda j: (0, jnp.minimum(j, 1))),
            pl.BlockSpec((rows, tile), lambda j: (0, jnp.maximum(j - 2, 0))),
        ],
        out_shape=[
            jax.ShapeDtypeStruct((rows, width // 2), F32),
            jax.ShapeDtypeStruct((rows, width // 2), BF16),
        ],
        compiler_params=pltpu.CompilerParams(vmem_limit_bytes=VMEM),
        cost_estimate=pl.CostEstimate(
            flops=2 * rows * depth * width * len(weights),
            bytes_accessed=8 * depth * width,
            transcendentals=0,
        ),
    )(*blocks, *weights)


def finish_kernel(order, strip, meta, *refs):
    out = refs[-1]
    width = out.shape[1]
    z = meta[0]
    parts = len(order)
    for part, shifts in enumerate(order):
        kept, core, far = refs[3 * part : 3 * part + 3]
        for at, shift in enumerate(shifts):
            zs = lax.rem(z + shift + NZ, NZ)
            for p in range(NY * NC):
                here = pl.ds((at * NY * NC + p) * strip, strip)
                total = kept[here, :width] + core[here, :width].astype(F32) + far[here, :].astype(F32)
                spot = pl.multiple_of((p * NZ + zs) * strip, strip)
                out[pl.ds(spot, strip), :] = total.astype(BF16)


def finish(meta, order, parts):
    strip = 16
    rows = sum(part[0].shape[0] for part in parts)
    flat = [array for part in parts for array in part]
    return pl.pallas_call(
        functools.partial(finish_kernel, order, strip),
        in_specs=[pl.BlockSpec(memory_space=pltpu.SMEM)] + [pl.BlockSpec(memory_space=pltpu.VMEM)] * len(flat),
        out_specs=pl.BlockSpec(memory_space=pltpu.VMEM),
        out_shape=jax.ShapeDtypeStruct((rows, parts[0][2].shape[1]), BF16),
        compiler_params=pltpu.CompilerParams(vmem_limit_bytes=VMEM),
    )(meta, *flat)


def shards(queries, stored_keys, stored_values, fresh_keys, fresh_values, cache_lengths, out_weight):
    cache, fresh = stored_keys.shape[0], fresh_keys.shape[0]
    z, yh, core, x, yl = [lax.axis_index(name) for name in AXES]
    meta = jnp.stack([z, yh, core, x, yl]).astype(jnp.int32)

    kv = jnp.concatenate(
        [
            jnp.concatenate([stored_keys, stored_values], 1),
            jnp.concatenate([fresh_keys, fresh_values], 1),
        ],
        0,
    )
    forth, back = [kv], [kv]
    for _ in range(3):
        forth.append(shift_z(forth[-1], 1))
        back.append(shift_z(back[-1], -1))
    forth.append(shift_z(forth[-1], 1))
    pair = lambda value: [value, swap(value, b=1)]

    half = queries.shape[1] // 2
    mine = lax.dynamic_slice_in_dim(queries, core * half, half, 1)
    theirs = lax.dynamic_slice_in_dim(queries, (1 - core) * half, half, 1)
    received = swap(theirs, b=1)
    strips = lambda value: value.reshape(NZ, 1, fresh // NZ, half)
    near = jnp.where(
        core == 0,
        jnp.concatenate([strips(mine), strips(received)], 1),
        jnp.concatenate([strips(received), strips(mine)], 1),
    )
    near = jnp.broadcast_to(near[:, None], (NZ, NY, NC, fresh // NZ, half))
    q = lax.all_to_all(
        near.reshape(NZ * NY, NC * fresh // NZ, half), ("z", "yh"), split_axis=0, concat_axis=0, tiled=True
    ).reshape(NY * NC * fresh, half)

    state = attend(
        meta, cache_lengths, q, pair(kv) + pair(forth[1]) + pair(back[1]), (0, -1, 1), None, False, cache, fresh
    )
    state = attend(
        meta, cache_lengths, q, pair(forth[2]) + pair(back[2]), (-2, 2), state, False, cache, fresh
    )
    state = attend(
        meta, cache_lengths, q, pair(forth[3]) + pair(back[3]), (-3, 3), state, False, cache, fresh
    )
    pieces = attend(meta, cache_lengths, q, pair(forth[4]), (-4,), state, True, cache, fresh)

    depth = out_weight.shape[0] // 4

    def rows_of(a, b):
        return lax.dynamic_slice_in_dim(out_weight, ((core ^ b) * 2 + (yh ^ a)) * depth, depth, 0)

    own = jnp.concatenate(
        [rows_of(0, 0), swap(rows_of(1, 0), a=1), swap(rows_of(0, 1), b=1), swap(rows_of(1, 1), a=1, b=1)], 1
    )
    twin = swap(own, d=1)
    own_f, twin_f = shift_x(own, 1), shift_x(twin, 1)
    own_b, twin_b = shift_x(own, -1), shift_x(twin, -1)
    own_2, twin_2 = shift_x(own_f, 1), shift_x(twin_b, -1)
    weights = [own, twin, own_b, twin_b, own_2, twin_2, own_f, twin_f]

    group, width = pieces.shape[2] , pieces.shape[3]
    pieces = lax.all_to_all(
        pieces.reshape(NY * NZ, group, width), ("yh", "x", "yl"), split_axis=0, concat_axis=0, tiled=True
    )
    a = combine(meta, pieces)
    forth, back = [a], [a]
    for _ in range(3):
        forth.append(shift_z(forth[-1], 1))
        back.append(shift_z(back[-1], -1))
    forth.append(shift_z(forth[-1], 1))

    def share(blocks):
        kept, sent = project(blocks, weights)
        near = swap(sent, b=1)
        width = kept.shape[1] // 2
        part = (kept[:, width:] + near[:, width:].astype(F32)).astype(BF16)
        return kept, near, swap(part, a=1)

    order = ((0, -1, 1, -2, 2), (-3, 3, -4))
    first = share([a, forth[1], back[1], forth[2], back[2]])
    second = share([forth[3], back[3], forth[4]])
    return finish(meta, order, (first, second))


def solution(mesh):
    split = Mesh(mesh.devices.reshape(NZ, NY, NC, NX, NL), AXES)
    ctx, tp = ("z", "yh", "core"), ("x", "yl")
    spec = P(ctx, tp)
    return jax.shard_map(
        shards,
        mesh=split,
        in_specs=(spec, spec, spec, spec, spec, P(), P(tp, ctx)),
        out_specs=P(tp, ctx),
        check_vma=False,
    )
```

profile of v0, /device:TPU:1, one launch (start us, length us, event | category | flops | bytes accessed | tf_op | source)
XLA Modules:
  0.0 166.0 jit_solution(261763429391051489)
XLA Ops:
  1.0 3.3 %collective-permute-start = (bf16[128,512]{1,0:T(8,128)(2,1)S(1)}, bf16[128,512]{1,0:T(8,128)(2,1)S(1)}, u32[]{:S(2)}, u32[]{:S(2)}) collective-permute-start(bf16[128,512]{1,0:T(8,128)(2,1)S(1)} %get-tuple-element.30), channel_id=1, source_target_pairs={{0,8},{1,9},{2,10},{3,11},{4,12},{5,13},{6,14},{7,15},{8,0},{9,1},... | collective-permute-start | bytes 393224 | tf_op jit(solution)/shard_map/ppermute | solution.py:34
  6.2 9.3 %all-to-all-start = ((bf16[16,32,512]{2,1,0:T(8,128)(2,1)}), bf16[16,32,512]{2,1,0:T(8,128)(2,1)S(1)}, u32[]{:S(2)}, u32[]{:S(2)}) async-start(bf16[16,32,512]{2,1,0:T(8,128)(2,1)} %bitcast.7), calls=%async_computation | async-start | bytes 1048576 | tf_op jit(solution)/shard_map/all_to_all | solution.py:286
  15.7 1.4 collective-permute-start.1
  18.4 15.6 %collective-permute-done.1.refs_2_ = bf16[384,256]{1,0:T(8,128)(2,1)S(1)} collective-permute-done((bf16[384,256]{1,0:T(8,128)(2,1)S(1)}, bf16[384,256]{1,0:T(8,128)(2,1)S(1)}, u32[]{:S(2)}, u32[]{:S(2)}) %collective-permute-start.1) | collective-permute-done | bytes 196640 | tf_op jit(solution)/shard_map/ppermute | solution.py:34
  34.1 4.1 %collective-permute-start.22 = (bf16[256,256]{1,0:T(8,128)(2,1)S(1)}, bf16[256,256]{1,0:T(8,128)(2,1)S(1)}, u32[]{:S(2)}, u32[]{:S(2)}) collective-permute-start(bf16[256,256]{1,0:T(8,128)(2,1)S(1)} %get-tuple-element.27), channel_id=1, source_target_pairs={{0,24},{1,25},{2,26},{3,27},{4,28},{5,29},{6,30},{7,31},{8,16},{9,... | collective-permute-start | bytes 393224 | tf_op jit(solution)/shard_map/ppermute | solution.py:34
  38.4 4.0 %collective-permute-done.22 = bf16[256,256]{1,0:T(8,128)(2,1)S(1)} collective-permute-done((bf16[256,256]{1,0:T(8,128)(2,1)S(1)}, bf16[256,256]{1,0:T(8,128)(2,1)S(1)}, u32[]{:S(2)}, u32[]{:S(2)}) %collective-permute-start.22) | collective-permute-done | bytes 131104 | tf_op jit(solution)/shard_map/ppermute | solution.py:34
  42.9 3.0 %collective-permute-start.8 = (bf16[384,256]{1,0:T(8,128)(2,1)S(1)}, bf16[384,256]{1,0:T(8,128)(2,1)S(1)}, u32[]{:S(2)}, u32[]{:S(2)}) collective-permute-start(bf16[384,256]{1,0:T(8,128)(2,1)S(1)} %collective-permute-done.7.refs_4_), channel_id=1, source_target_pairs={{0,224},{1,225},{2,226},{3,227},{4,228},{5,229},{6,230},{7,231},{8... | collective-permute-start | bytes 589832 | tf_op jit(solution)/shard_map/ppermute | solution.py:34
  47.0 3.0 %collective-permute-done.8.refs_2_ = bf16[384,256]{1,0:T(8,128)(2,1)S(1)} collective-permute-done((bf16[384,256]{1,0:T(8,128)(2,1)S(1)}, bf16[384,256]{1,0:T(8,128)(2,1)S(1)}, u32[]{:S(2)}, u32[]{:S(2)}) %collective-permute-start.8) | collective-permute-done | bytes 196640 | tf_op jit(solution)/shard_map/ppermute | solution.py:34
  50.9 3.4 %collective-permute-start.9 = (bf16[384,256]{1,0:T(8,128)(2,1)S(1)}, bf16[384,256]{1,0:T(8,128)(2,1)}, u32[]{:S(2)}, u32[]{:S(2)}) collective-permute-start(bf16[384,256]{1,0:T(8,128)(2,1)S(1)} %collective-permute-done.8.refs_2_), channel_id=1, source_target_pairs={{0,224},{1,225},{2,226},{3,227},{4,228},{5,229},{6,230},{7,231},{8... | collective-permute-start | bytes 589832 | tf_op jit(solution)/shard_map/ppermute | solution.py:34
  54.7 9.9 %shard_map.73 = (f32[512,512]{1,0:T(8,128)S(1)}, f32[512,512]{1,0:T(8,128)S(1)}) custom-call(s32[5]{0:T(128)S(1)} %stack.23.meta, s32[32]{0:T(128)S(1)} %copy-done.1, bf16[512,512]{1,0:T(8,128)(2,1)S(1)} %bitcast.10, bf16[384,256]{1,0:T(8,128)(2,1)S(1)} %maximum_maximum_fusion.refs_0_, bf16[384,256]{1,0:T(8,128)(2,1)S(1)} %collective-permute-done.13.refs_1_, ...), custom_call_target="tpu_custom_call" | custom-call | flops 4831838208 | bytes 1048576 | tf_op jit(solution)/shard_map/pallas_call | solution.py:134
  65.4 9.5 %shard_map.74 = (f32[512,512]{1,0:T(8,128)S(1)}, f32[512,512]{1,0:T(8,128)S(1)}) custom-call(s32[5]{0:T(128)S(1)} %stack.23.meta, s32[32]{0:T(128)S(1)} %copy-done.1, bf16[512,512]{1,0:T(8,128)(2,1)S(1)} %bitcast.11, bf16[384,256]{1,0:T(8,128)(2,1)S(1)} %collective-permute-done.2.refs_0_, bf16[384,256]{1,0:T(8,128)(2,1)} %collective-permute-done.11.refs_1_, ...), custom_call_target="tpu_custom_call" | custom-call | flops 3221225472 | bytes 1048576 | tf_op jit(solution)/shard_map/pallas_call | solution.py:134
  75.0 9.5 %shard_map.75 = (f32[512,512]{1,0:T(8,128)S(1)}, f32[512,512]{1,0:T(8,128)S(1)}) custom-call(s32[5]{0:T(128)S(1)} %stack.23.meta, s32[32]{0:T(128)S(1)} %copy-done.1, bf16[512,512]{1,0:T(8,128)(2,1)S(1)} %bitcast.12, bf16[384,256]{1,0:T(8,128)(2,1)S(1)} %collective-permute-done.3.refs_0_, bf16[384,256]{1,0:T(8,128)(2,1)S(1)} %collective-permute-done.6.refs_1_, ...), custom_call_target="tpu_custom_call" | custom-call | flops 3221225472 | bytes 1048576 | tf_op jit(solution)/shard_map/pallas_call | solution.py:134
  84.5 8.3 %shard_map.76 = bf16[2,8,80,256]{3,2,1,0:T(8,128)(2,1)} custom-call(s32[5]{0:T(128)S(1)} %stack.23.meta, s32[32]{0:T(128)S(1)} %copy-done.1, bf16[512,512]{1,0:T(8,128)(2,1)S(1)} %bitcast.13, bf16[384,256]{1,0:T(8,128)(2,1)} %collective-permute-done.4.refs_0_, bf16[384,256]{1,0:T(8,128)(2,1)S(1)} %collective-permute-done.5.refs_1_, ...), custom_call_target="tpu_custom_call" | custom-call | flops 1610612736 | bytes 1048576 | tf_op jit(solution)/shard_map/pallas_call | solution.py:134
  92.8 6.1 %all-to-all-start.1 = ((bf16[16,80,256]{2,1,0:T(8,128)(2,1)}), bf16[16,80,256]{2,1,0:T(8,128)(2,1)S(1)}, u32[]{:S(2)}, u32[]{:S(2)}) async-start(bf16[16,80,256]{2,1,0:T(8,128)(2,1)} %bitcast.9), calls=%async_computation.1 | async-start | bytes 1310720 | tf_op jit(solution)/shard_map/all_to_all | solution.py:316
  98.9 2.6 %collective-permute-start.24 = (bf16[256,1024]{1,0:T(8,128)(2,1)S(1)}, bf16[256,1024]{1,0:T(8,128)(2,1)S(1)}, u32[]{:S(2)}, u32[]{:S(2)}) collective-permute-start(bf16[256,1024]{1,0:T(8,128)(2,1)S(1)} %pad_maximum_fusion.refs_5_.refs_3_), channel_id=1, source_target_pairs={{0,6},{1,7},{2,0},{3,1},{4,2},{5,3},{6,4},{7,5},{8,14},{9,15},{10,... | collective-permute-start | bytes 1572872 | tf_op jit(solution)/shard_map/ppermute | solution.py:34
  101.5 2.7 %collective-permute-start.25 = (bf16[256,1024]{1,0:T(8,128)(2,1)S(1)}, bf16[256,1024]{1,0:T(8,128)(2,1)S(1)}, u32[]{:S(2)}, u32[]{:S(2)}) collective-permute-start(bf16[256,1024]{1,0:T(8,128)(2,1)S(1)} %collective-permute-done.23.refs_6_.refs_4_), channel_id=1, source_target_pairs={{0,6},{1,7},{2,0},{3,1},{4,2},{5,3},{6,4},{7,5},{8,14},{9,15},{10,... | collective-permute-start | bytes 1572872 | tf_op jit(solution)/shard_map/ppermute | solution.py:34
  104.2 7.0 %all-to-all-done.1.pieces = bf16[16,80,256]{2,1,0:T(8,128)(2,1)S(1)} async-done(((bf16[16,80,256]{2,1,0:T(8,128)(2,1)}), bf16[16,80,256]{2,1,0:T(8,128)(2,1)S(1)}, u32[]{:S(2)}, u32[]{:S(2)}) %all-to-all-start.1) | async-done | bytes 655392 | tf_op jit(solution)/shard_map/all_to_all | solution.py:316
  112.9 3.1 %collective-permute-start.17 = (bf16[64,2048]{1,0:T(8,128)(2,1)S(1)}, bf16[64,2048]{1,0:T(8,128)(2,1)S(1)}, u32[]{:S(2)}, u32[]{:S(2)}) collective-permute-start(bf16[64,2048]{1,0:T(8,128)(2,1)S(1)} %shard_map.77.refs_0_), channel_id=1, source_target_pairs={{0,224},{1,225},{2,226},{3,227},{4,228},{5,229},{6,230},{7,231},{8... | collective-permute-start | bytes 786440 | tf_op jit(solution)/shard_map/ppermute | solution.py:34
  116.1 4.8 %collective-permute-done.16.refs_1_ = bf16[64,2048]{1,0:T(8,128)(2,1)S(1)} collective-permute-done((bf16[64,2048]{1,0:T(8,128)(2,1)S(1)}, bf16[64,2048]{1,0:T(8,128)(2,1)S(1)}, u32[]{:S(2)}, u32[]{:S(2)}) %collective-permute-start.16) | collective-permute-done | bytes 262176 | tf_op jit(solution)/shard_map/ppermute | solution.py:34
  121.1 9.2 %collective-permute-done.25.refs_8_.refs_6_ = bf16[256,1024]{1,0:T(8,128)(2,1)S(1)} collective-permute-done((bf16[256,1024]{1,0:T(8,128)(2,1)S(1)}, bf16[256,1024]{1,0:T(8,128)(2,1)S(1)}, u32[]{:S(2)}, u32[]{:S(2)}) %collective-permute-start.25) | collective-permute-done | bytes 524320 | tf_op jit(solution)/shard_map/ppermute | solution.py:34
  130.2 1.5 collective-permute-start.28
  131.8 3.1 %collective-permute-start.19 = (bf16[64,2048]{1,0:T(8,128)(2,1)S(1)}, bf16[64,2048]{1,0:T(8,128)(2,1)S(1)}, u32[]{:S(2)}, u32[]{:S(2)}) collective-permute-start(bf16[64,2048]{1,0:T(8,128)(2,1)S(1)} %collective-permute-done.17.refs_2_), channel_id=1, source_target_pairs={{0,224},{1,225},{2,226},{3,227},{4,228},{5,229},{6,230},{7,231},{8... | collective-permute-start | bytes 786440 | tf_op jit(solution)/shard_map/ppermute | solution.py:34
  134.9 4.4 %collective-permute-done.19.refs_4_ = bf16[64,2048]{1,0:T(8,128)(2,1)S(1)} collective-permute-done((bf16[64,2048]{1,0:T(8,128)(2,1)S(1)}, bf16[64,2048]{1,0:T(8,128)(2,1)S(1)}, u32[]{:S(2)}, u32[]{:S(2)}) %collective-permute-start.19) | collective-permute-done | bytes 262176 | tf_op jit(solution)/shard_map/ppermute | solution.py:34
  139.4 3.4 %collective-permute-start.33 = (bf16[64,2048]{1,0:T(8,128)(2,1)S(1)}, bf16[64,2048]{1,0:T(8,128)(2,1)S(1)}, u32[]{:S(2)}, u32[]{:S(2)}) collective-permute-start(bf16[64,2048]{1,0:T(8,128)(2,1)S(1)} %collective-permute-done.19.refs_4_), channel_id=1, source_target_pairs={{0,224},{1,225},{2,226},{3,227},{4,228},{5,229},{6,230},{7,231},{8... | collective-permute-start | bytes 786440 | tf_op jit(solution)/shard_map/ppermute | solution.py:34
  142.8 1.6 collective-permute-done.27.refs_9_.refs_7_
  144.4 3.7 %shard_map.78 = (f32[320,512]{1,0:T(8,128)}, bf16[320,512]{1,0:T(8,128)(2,1)S(1)}) custom-call(bf16[64,2048]{1,0:T(8,128)(2,1)S(1)} %shard_map.77.refs_0_, bf16[64,2048]{1,0:T(8,128)(2,1)S(1)} %collective-permute-done.16.refs_1_, bf16[64,2048]{1,0:T(8,128)(2,1)S(1)} %collective-permute-done.17.refs_2_, bf16[64,2048]{1,0:T(8,128)(2,1)S(1)} %collective-permute-done.18.refs_3_, ...), custom_call_target="tpu_custom_call" | custom-call | flops 1342177280 | bytes 2097152 | tf_op jit(solution)/shard_map/pallas_call | solution.py:206
  148.0 3.3 %collective-permute-start.30 = (bf16[320,512]{1,0:T(8,128)(2,1)S(1)}, bf16[320,512]{1,0:T(8,128)(2,1)S(1)}, u32[]{:S(2)}, u32[]{:S(2)}) collective-permute-start(bf16[320,512]{1,0:T(8,128)(2,1)S(1)} %get-tuple-element.22), channel_id=1, source_target_pairs={{0,8},{1,9},{2,10},{3,11},{4,12},{5,13},{6,14},{7,15},{8,0},{9,1},... | collective-permute-start | bytes 983048 | tf_op jit(solution)/shard_map/ppermute | solution.py:34
  151.4 2.3 %shard_map.79 = (f32[192,512]{1,0:T(8,128)S(1)}, bf16[192,512]{1,0:T(8,128)(2,1)S(1)}) custom-call(bf16[64,2048]{1,0:T(8,128)(2,1)S(1)} %collective-permute-done.32.refs_0_, bf16[64,2048]{1,0:T(8,128)(2,1)S(1)} %collective-permute-done.33.refs_1_, bf16[64,2048]{1,0:T(8,128)(2,1)S(1)} %collective-permute-done.34.refs_2_, ...), custom_call_target="tpu_custom_call" | custom-call | flops 805306368 | bytes 2097152 | tf_op jit(solution)/shard_map/pallas_call | solution.py:206
  153.7 1.5 collective-permute-start.35
  155.2 2.7 %collective-permute-start.31 = (bf16[320,256]{1,0:T(8,128)(2,1)S(1)}, bf16[320,256]{1,0:T(8,128)(2,1)S(1)}, u32[]{:S(2)}, u32[]{:S(2)}) collective-permute-start(bf16[320,256]{1,0:T(8,128)(2,1)S(1)} %add_convert_fusion), channel_id=1, source_target_pairs={{0,16},{1,17},{2,18},{3,19},{4,20},{5,21},{6,22},{7,23},{8,24},{9,... | collective-permute-start | bytes 491528 | tf_op jit(solution)/shard_map/ppermute | solution.py:34
  159.0 3.6 %collective-permute-done.31.refs_2_ = bf16[320,256]{1,0:T(8,128)(2,1)S(1)} collective-permute-done((bf16[320,256]{1,0:T(8,128)(2,1)S(1)}, bf16[320,256]{1,0:T(8,128)(2,1)S(1)}, u32[]{:S(2)}, u32[]{:S(2)}) %collective-permute-start.31) | collective-permute-done | bytes 163872 | tf_op jit(solution)/shard_map/ppermute | solution.py:34
  162.6 2.1 %collective-permute-done.36.refs_5_ = bf16[192,256]{1,0:T(8,128)(2,1)S(1)} collective-permute-done((bf16[192,256]{1,0:T(8,128)(2,1)S(1)}, bf16[192,256]{1,0:T(8,128)(2,1)S(1)}, u32[]{:S(2)}, u32[]{:S(2)}) %collective-permute-start.36) | collective-permute-done | bytes 98336 | tf_op jit(solution)/shard_map/ppermute | solution.py:34
  (78 shorter events, 12.7 us)
Async XLA Ops:
  6.2 48.4 %all-to-all-start = ((bf16[16,32,512]{2,1,0:T(8,128)(2,1)}), bf16[16,32,512]{2,1,0:T(8,128)(2,1)S(1)}, u32[]{:S(2)}, u32[]{:S(2)}) async-start(bf16[16,32,512]{2,1,0:T(8,128)(2,1)} %bitcast.7), calls=%async_computation | async-start | bytes 1048576 | tf_op jit(solution)/shard_map/all_to_all | solution.py:286
  15.7 18.4 %collective-permute-start.1 = (bf16[384,256]{1,0:T(8,128)(2,1)S(1)}, bf16[384,256]{1,0:T(8,128)(2,1)S(1)}, u32[]{:S(2)}, u32[]{:S(2)}) collective-permute-start(bf16[384,256]{1,0:T(8,128)(2,1)S(1)} %maximum_maximum_fusion.refs_0_), channel_id=1, source_target_pairs={{0,32},{1,33},{2,34},{3,35},{4,36},{5,37},{6,38},{7,39},{8,40},{9,... | collective-permute-start | bytes 589832 | tf_op jit(solution)/shard_map/ppermute | solution.py:34
  17.1 25.8 %collective-permute-start.7 = (bf16[384,256]{1,0:T(8,128)(2,1)S(1)}, bf16[384,256]{1,0:T(8,128)(2,1)S(1)}, u32[]{:S(2)}, u32[]{:S(2)}) collective-permute-start(bf16[384,256]{1,0:T(8,128)(2,1)S(1)} %maximum_maximum_fusion.refs_0_), channel_id=1, source_target_pairs={{0,224},{1,225},{2,226},{3,227},{4,228},{5,229},{6,230},{7,231},{8... | collective-permute-start | bytes 589832 | tf_op jit(solution)/shard_map/ppermute | solution.py:34
  34.0 12.3 %collective-permute-start.2 = (bf16[384,256]{1,0:T(8,128)(2,1)S(1)}, bf16[384,256]{1,0:T(8,128)(2,1)S(1)}, u32[]{:S(2)}, u32[]{:S(2)}) collective-permute-start(bf16[384,256]{1,0:T(8,128)(2,1)S(1)} %collective-permute-done.1.refs_2_), channel_id=1, source_target_pairs={{0,32},{1,33},{2,34},{3,35},{4,36},{5,37},{6,38},{7,39},{8,40},{9,... | collective-permute-start | bytes 589832 | tf_op jit(solution)/shard_map/ppermute | solution.py:34
  34.1 8.4 %collective-permute-start.22 = (bf16[256,256]{1,0:T(8,128)(2,1)S(1)}, bf16[256,256]{1,0:T(8,128)(2,1)S(1)}, u32[]{:S(2)}, u32[]{:S(2)}) collective-permute-start(bf16[256,256]{1,0:T(8,128)(2,1)S(1)} %get-tuple-element.27), channel_id=1, source_target_pairs={{0,24},{1,25},{2,26},{3,27},{4,28},{5,29},{6,30},{7,31},{8,16},{9,... | collective-permute-start | bytes 393224 | tf_op jit(solution)/shard_map/ppermute | solution.py:34
  38.2 7.7 %collective-permute-start.21 = (bf16[256,256]{1,0:T(8,128)(2,1)S(1)}, bf16[256,256]{1,0:T(8,128)(2,1)S(1)}, u32[]{:S(2)}, u32[]{:S(2)}) collective-permute-start(bf16[256,256]{1,0:T(8,128)(2,1)S(1)} %get-tuple-element.28), channel_id=1, source_target_pairs={{0,8},{1,9},{2,10},{3,11},{4,12},{5,13},{6,14},{7,15},{8,0},{9,1},... | collective-permute-start | bytes 393224 | tf_op jit(solution)/shard_map/ppermute | solution.py:34
  38.2 8.1 %collective-permute-start.20 = (bf16[256,256]{1,0:T(8,128)(2,1)S(1)}, bf16[256,256]{1,0:T(8,128)(2,1)S(1)}, u32[]{:S(2)}, u32[]{:S(2)}) collective-permute-start(bf16[256,256]{1,0:T(8,128)(2,1)S(1)} %get-tuple-element.26), channel_id=1, source_target_pairs={{0,16},{1,17},{2,18},{3,19},{4,20},{5,21},{6,22},{7,23},{8,24},{9,... | collective-permute-start | bytes 393224 | tf_op jit(solution)/shard_map/ppermute | solution.py:34
  46.3 8.1 %collective-permute-start.15 = (bf16[384,256]{1,0:T(8,128)(2,1)S(1)}, bf16[384,256]{1,0:T(8,128)(2,1)S(1)}, u32[]{:S(2)}, u32[]{:S(2)}) collective-permute-start(bf16[384,256]{1,0:T(8,128)(2,1)S(1)} %collective-permute-done.7.refs_4_), channel_id=1, source_target_pairs={{0,8},{1,9},{2,10},{3,11},{4,12},{5,13},{6,14},{7,15},{8,0},{9,1},... | collective-permute-start | bytes 589832 | tf_op jit(solution)/shard_map/ppermute | solution.py:34
  46.4 8.3 %collective-permute-start.3 = (bf16[384,256]{1,0:T(8,128)(2,1)S(1)}, bf16[384,256]{1,0:T(8,128)(2,1)S(1)}, u32[]{:S(2)}, u32[]{:S(2)}) collective-permute-start(bf16[384,256]{1,0:T(8,128)(2,1)S(1)} %collective-permute-done.2.refs_0_), channel_id=1, source_target_pairs={{0,32},{1,33},{2,34},{3,35},{4,36},{5,37},{6,38},{7,39},{8,40},{9,... | collective-permute-start | bytes 589832 | tf_op jit(solution)/shard_map/ppermute | solution.py:34
  46.5 55.0 %collective-permute-start.23 = (bf16[256,1024]{1,0:T(8,128)(2,1)S(1)}, bf16[256,1024]{1,0:T(8,128)(2,1)S(1)}, u32[]{:S(2)}, u32[]{:S(2)}) collective-permute-start(bf16[256,1024]{1,0:T(8,128)(2,1)S(1)} %pad_maximum_fusion.refs_5_.refs_3_), channel_id=1, source_target_pairs={{0,1},{1,0},{2,3},{3,2},{4,5},{5,4},{6,7},{7,6},{8,9},{9,8},{10,11... | collective-permute-start | bytes 1572872 | tf_op jit(solution)/shard_map/ppermute | solution.py:34
  50.0 14.9 %collective-permute-start.11 = (bf16[384,256]{1,0:T(8,128)(2,1)S(1)}, bf16[384,256]{1,0:T(8,128)(2,1)}, u32[]{:S(2)}, u32[]{:S(2)}) collective-permute-start(bf16[384,256]{1,0:T(8,128)(2,1)S(1)} %collective-permute-done.2.refs_0_), channel_id=1, source_target_pairs={{0,8},{1,9},{2,10},{3,11},{4,12},{5,13},{6,14},{7,15},{8,0},{9,1},... | collective-permute-start | bytes 589832 | tf_op jit(solution)/shard_map/ppermute | solution.py:34
  50.9 13.6 %collective-permute-start.9 = (bf16[384,256]{1,0:T(8,128)(2,1)S(1)}, bf16[384,256]{1,0:T(8,128)(2,1)}, u32[]{:S(2)}, u32[]{:S(2)}) collective-permute-start(bf16[384,256]{1,0:T(8,128)(2,1)S(1)} %collective-permute-done.8.refs_2_), channel_id=1, source_target_pairs={{0,224},{1,225},{2,226},{3,227},{4,228},{5,229},{6,230},{7,231},{8... | collective-permute-start | bytes 589832 | tf_op jit(solution)/shard_map/ppermute | solution.py:34
  54.4 11.1 %collective-permute-start.12 = (bf16[384,256]{1,0:T(8,128)(2,1)S(1)}, bf16[384,256]{1,0:T(8,128)(2,1)}, u32[]{:S(2)}, u32[]{:S(2)}) collective-permute-start(bf16[384,256]{1,0:T(8,128)(2,1)S(1)} %collective-permute-done.8.refs_2_), channel_id=1, source_target_pairs={{0,8},{1,9},{2,10},{3,11},{4,12},{5,13},{6,14},{7,15},{8,0},{9,1},... | collective-permute-start | bytes 589832 | tf_op jit(solution)/shard_map/ppermute | solution.py:34
  54.6 10.5 %collective-permute-start.4 = (bf16[384,256]{1,0:T(8,128)(2,1)S(1)}, bf16[384,256]{1,0:T(8,128)(2,1)}, u32[]{:S(2)}, u32[]{:S(2)}) collective-permute-start(bf16[384,256]{1,0:T(8,128)(2,1)S(1)} %collective-permute-done.3.refs_0_), channel_id=1, source_target_pairs={{0,32},{1,33},{2,34},{3,35},{4,36},{5,37},{6,38},{7,39},{8,40},{9,... | collective-permute-start | bytes 589832 | tf_op jit(solution)/shard_map/ppermute | solution.py:34
  64.5 10.4 %collective-permute-start.6 = (bf16[384,256]{1,0:T(8,128)(2,1)S(1)}, bf16[384,256]{1,0:T(8,128)(2,1)S(1)}, u32[]{:S(2)}, u32[]{:S(2)}) collective-permute-start(bf16[384,256]{1,0:T(8,128)(2,1)S(1)} %collective-permute-done.3.refs_0_), channel_id=1, source_target_pairs={{0,8},{1,9},{2,10},{3,11},{4,12},{5,13},{6,14},{7,15},{8,0},{9,1},... | collective-permute-start | bytes 589832 | tf_op jit(solution)/shard_map/ppermute | solution.py:34
  64.9 10.1 %collective-permute-start.10 = (bf16[384,256]{1,0:T(8,128)(2,1)}, bf16[384,256]{1,0:T(8,128)(2,1)S(1)}, u32[]{:S(2)}, u32[]{:S(2)}) collective-permute-start(bf16[384,256]{1,0:T(8,128)(2,1)} %collective-permute-done.9.refs_2_), channel_id=1, source_target_pairs={{0,8},{1,9},{2,10},{3,11},{4,12},{5,13},{6,14},{7,15},{8,0},{9,1},... | collective-permute-start | bytes 589832 | tf_op jit(solution)/shard_map/ppermute | solution.py:34
  65.2 19.3 %collective-permute-start.5 = (bf16[384,256]{1,0:T(8,128)(2,1)}, bf16[384,256]{1,0:T(8,128)(2,1)S(1)}, u32[]{:S(2)}, u32[]{:S(2)}) collective-permute-start(bf16[384,256]{1,0:T(8,128)(2,1)} %collective-permute-done.4.refs_0_), channel_id=1, source_target_pairs={{0,8},{1,9},{2,10},{3,11},{4,12},{5,13},{6,14},{7,15},{8,0},{9,1},... | collective-permute-start | bytes 589832 | tf_op jit(solution)/shard_map/ppermute | solution.py:34
  92.8 18.4 %all-to-all-start.1 = ((bf16[16,80,256]{2,1,0:T(8,128)(2,1)}), bf16[16,80,256]{2,1,0:T(8,128)(2,1)S(1)}, u32[]{:S(2)}, u32[]{:S(2)}) async-start(bf16[16,80,256]{2,1,0:T(8,128)(2,1)} %bitcast.9), calls=%async_computation.1 | async-start | bytes 1310720 | tf_op jit(solution)/shard_map/all_to_all | solution.py:316
  98.9 22.0 %collective-permute-start.24 = (bf16[256,1024]{1,0:T(8,128)(2,1)S(1)}, bf16[256,1024]{1,0:T(8,128)(2,1)S(1)}, u32[]{:S(2)}, u32[]{:S(2)}) collective-permute-start(bf16[256,1024]{1,0:T(8,128)(2,1)S(1)} %pad_maximum_fusion.refs_5_.refs_3_), channel_id=1, source_target_pairs={{0,6},{1,7},{2,0},{3,1},{4,2},{5,3},{6,4},{7,5},{8,14},{9,15},{10,... | collective-permute-start | bytes 1572872 | tf_op jit(solution)/shard_map/ppermute | solution.py:34
  101.5 19.4 %collective-permute-start.26 = (bf16[256,1024]{1,0:T(8,128)(2,1)S(1)}, bf16[256,1024]{1,0:T(8,128)(2,1)S(1)}, u32[]{:S(2)}, u32[]{:S(2)}) collective-permute-start(bf16[256,1024]{1,0:T(8,128)(2,1)S(1)} %pad_maximum_fusion.refs_5_.refs_3_), channel_id=1, source_target_pairs={{0,2},{1,3},{2,4},{3,5},{4,6},{5,7},{6,0},{7,1},{8,10},{9,11},{10,... | collective-permute-start | bytes 1572872 | tf_op jit(solution)/shard_map/ppermute | solution.py:34
  101.5 28.7 %collective-permute-start.25 = (bf16[256,1024]{1,0:T(8,128)(2,1)S(1)}, bf16[256,1024]{1,0:T(8,128)(2,1)S(1)}, u32[]{:S(2)}, u32[]{:S(2)}) collective-permute-start(bf16[256,1024]{1,0:T(8,128)(2,1)S(1)} %collective-permute-done.23.refs_6_.refs_4_), channel_id=1, source_target_pairs={{0,6},{1,7},{2,0},{3,1},{4,2},{5,3},{6,4},{7,5},{8,14},{9,15},{10,... | collective-permute-start | bytes 1572872 | tf_op jit(solution)/shard_map/ppermute | solution.py:34
  112.3 8.5 %collective-permute-start.16 = (bf16[64,2048]{1,0:T(8,128)(2,1)S(1)}, bf16[64,2048]{1,0:T(8,128)(2,1)S(1)}, u32[]{:S(2)}, u32[]{:S(2)}) collective-permute-start(bf16[64,2048]{1,0:T(8,128)(2,1)S(1)} %shard_map.77.refs_0_), channel_id=1, source_target_pairs={{0,32},{1,33},{2,34},{3,35},{4,36},{5,37},{6,38},{7,39},{8,40},{9,... | collective-permute-start | bytes 786440 | tf_op jit(solution)/shard_map/ppermute | solution.py:34
  112.9 18.8 %collective-permute-start.17 = (bf16[64,2048]{1,0:T(8,128)(2,1)S(1)}, bf16[64,2048]{1,0:T(8,128)(2,1)S(1)}, u32[]{:S(2)}, u32[]{:S(2)}) collective-permute-start(bf16[64,2048]{1,0:T(8,128)(2,1)S(1)} %shard_map.77.refs_0_), channel_id=1, source_target_pairs={{0,224},{1,225},{2,226},{3,227},{4,228},{5,229},{6,230},{7,231},{8... | collective-permute-start | bytes 786440 | tf_op jit(solution)/shard_map/ppermute | solution.py:34
  120.9 14.1 %collective-permute-start.18 = (bf16[64,2048]{1,0:T(8,128)(2,1)S(1)}, bf16[64,2048]{1,0:T(8,128)(2,1)S(1)}, u32[]{:S(2)}, u32[]{:S(2)}) collective-permute-start(bf16[64,2048]{1,0:T(8,128)(2,1)S(1)} %collective-permute-done.16.refs_1_), channel_id=1, source_target_pairs={{0,32},{1,33},{2,34},{3,35},{4,36},{5,37},{6,38},{7,39},{8,40},{9,... | collective-permute-start | bytes 786440 | tf_op jit(solution)/shard_map/ppermute | solution.py:34
  120.9 23.5 %collective-permute-start.29 = (bf16[256,1024]{1,0:T(8,128)(2,1)S(1)}, bf16[256,1024]{1,0:T(8,128)(2,1)S(1)}, u32[]{:S(2)}, u32[]{:S(2)}) collective-permute-start(bf16[256,1024]{1,0:T(8,128)(2,1)S(1)} %collective-permute-done.23.refs_6_.refs_4_), channel_id=1, source_target_pairs={{0,2},{1,3},{2,4},{3,5},{4,6},{5,7},{6,0},{7,1},{8,10},{9,11},{10,... | collective-permute-start | bytes 1572872 | tf_op jit(solution)/shard_map/ppermute | solution.py:34
  120.9 23.5 %collective-permute-start.27 = (bf16[256,1024]{1,0:T(8,128)(2,1)S(1)}, bf16[256,1024]{1,0:T(8,128)(2,1)S(1)}, u32[]{:S(2)}, u32[]{:S(2)}) collective-permute-start(bf16[256,1024]{1,0:T(8,128)(2,1)S(1)} %collective-permute-done.26.refs_11_.refs_9_), channel_id=1, source_target_pairs={{0,2},{1,3},{2,4},{3,5},{4,6},{5,7},{6,0},{7,1},{8,10},{9,11},{10,... | collective-permute-start | bytes 1572872 | tf_op jit(solution)/shard_map/ppermute | solution.py:34
  130.2 14.1 %collective-permute-start.28 = (bf16[256,1024]{1,0:T(8,128)(2,1)S(1)}, bf16[256,1024]{1,0:T(8,128)(2,1)S(1)}, u32[]{:S(2)}, u32[]{:S(2)}) collective-permute-start(bf16[256,1024]{1,0:T(8,128)(2,1)S(1)} %collective-permute-done.25.refs_8_.refs_6_), channel_id=1, source_target_pairs={{0,6},{1,7},{2,0},{3,1},{4,2},{5,3},{6,4},{7,5},{8,14},{9,15},{10,... | collective-permute-start | bytes 1572872 | tf_op jit(solution)/shard_map/ppermute | solution.py:34
  131.8 7.6 %collective-permute-start.19 = (bf16[64,2048]{1,0:T(8,128)(2,1)S(1)}, bf16[64,2048]{1,0:T(8,128)(2,1)S(1)}, u32[]{:S(2)}, u32[]{:S(2)}) collective-permute-start(bf16[64,2048]{1,0:T(8,128)(2,1)S(1)} %collective-permute-done.17.refs_2_), channel_id=1, source_target_pairs={{0,224},{1,225},{2,226},{3,227},{4,228},{5,229},{6,230},{7,231},{8... | collective-permute-start | bytes 786440 | tf_op jit(solution)/shard_map/ppermute | solution.py:34
  134.9 7.9 %collective-permute-start.32 = (bf16[64,2048]{1,0:T(8,128)(2,1)S(1)}, bf16[64,2048]{1,0:T(8,128)(2,1)S(1)}, u32[]{:S(2)}, u32[]{:S(2)}) collective-permute-start(bf16[64,2048]{1,0:T(8,128)(2,1)S(1)} %collective-permute-done.18.refs_3_), channel_id=1, source_target_pairs={{0,32},{1,33},{2,34},{3,35},{4,36},{5,37},{6,38},{7,39},{8,40},{9,... | collective-permute-start | bytes 786440 | tf_op jit(solution)/shard_map/ppermute | solution.py:34
  139.4 12.0 %collective-permute-start.33 = (bf16[64,2048]{1,0:T(8,128)(2,1)S(1)}, bf16[64,2048]{1,0:T(8,128)(2,1)S(1)}, u32[]{:S(2)}, u32[]{:S(2)}) collective-permute-start(bf16[64,2048]{1,0:T(8,128)(2,1)S(1)} %collective-permute-done.19.refs_4_), channel_id=1, source_target_pairs={{0,224},{1,225},{2,226},{3,227},{4,228},{5,229},{6,230},{7,231},{8... | collective-permute-start | bytes 786440 | tf_op jit(solution)/shard_map/ppermute | solution.py:34
  142.8 8.6 %collective-permute-start.34 = (bf16[64,2048]{1,0:T(8,128)(2,1)S(1)}, bf16[64,2048]{1,0:T(8,128)(2,1)S(1)}, u32[]{:S(2)}, u32[]{:S(2)}) collective-permute-start(bf16[64,2048]{1,0:T(8,128)(2,1)S(1)} %collective-permute-done.32.refs_0_), channel_id=1, source_target_pairs={{0,32},{1,33},{2,34},{3,35},{4,36},{5,37},{6,38},{7,39},{8,40},{9,... | collective-permute-start | bytes 786440 | tf_op jit(solution)/shard_map/ppermute | solution.py:34
  155.2 7.4 %collective-permute-start.31 = (bf16[320,256]{1,0:T(8,128)(2,1)S(1)}, bf16[320,256]{1,0:T(8,128)(2,1)S(1)}, u32[]{:S(2)}, u32[]{:S(2)}) collective-permute-start(bf16[320,256]{1,0:T(8,128)(2,1)S(1)} %add_convert_fusion), channel_id=1, source_target_pairs={{0,16},{1,17},{2,18},{3,19},{4,20},{5,21},{6,22},{7,23},{8,24},{9,... | collective-permute-start | bytes 491528 | tf_op jit(solution)/shard_map/ppermute | solution.py:34
  (14 other events, 119.3 us)
where the time goes:
time: 166 us
  starting transfers between devices  61.5 us (37%)
  waiting for transfers between devices  56.4 us (34%)
  Pallas kernels  45.7 us (28%)
  local copies, waits for them, and re-layouts  2.02 us (1%)
    ppermute x37, waiting for transfers between devices, permute(): return lax.ppermute(value, AXES, pairs)  49.4 us
    ppermute x37, starting transfers between devices, permute(): return lax.ppermute(value, AXES, pairs)  46 us
    pallas_call x4, Pallas kernels, attend(): pl.pallas_call(functools.partial(attend_kernel, tuple(shifts), first, las...  37.2 us
    all_to_all x1, starting transfers between devices, shards(): lax.all_to_all(near.reshape(NZ * NY, NC * fresh // NZ, half), ('z', 'yh')...  9.33 us
    all_to_all x1, waiting for transfers between devices, shards(): lax.all_to_all(pieces.reshape(NY * NZ, group, width), ('yh', 'x', 'yl'),...  7.01 us
    all_to_all x1, starting transfers between devices, shards(): lax.all_to_all(pieces.reshape(NY * NZ, group, width), ('yh', 'x', 'yl'),...  6.08 us
    pallas_call x2, Pallas kernels, project(): pl.pallas_call(functools.partial(project_kernel, len(blocks)), grid=(4,),...  6 us
  transfers between devices with their start and end apart: 39, of which 11 were waited for; matrix products, arithmetic and copies ran while one was open for 0% of the time, Pallas kernels for 27%

commit v1 on v0

--- a/solution.py
+++ b/solution.py
@@ -14,7 +14,7 @@
 NEG = -1e30
 VMEM = 48 * 1024 * 1024
 AXES = ("z", "yh", "core", "x", "yl")
-TILE = 256
+TILE = 512
 TAIL = 16
 F32 = jnp.float32
 BF16 = jnp.bfloat16
@@ -50,27 +50,29 @@
     count = 2 * len(shifts)
     kv_refs, refs = refs[:count], refs[count:]
     if not first:
-        acc_in, ml_in = refs[:2]
-        refs = refs[2:]
+        acc_in, top_in, sum_in = refs[:3]
+        refs = refs[3:]
     z, yh, core = meta[0], meta[1], meta[2]
     factor = math.log2(math.e) / math.sqrt(HEAD)
-    group = rows // NZ
-    strip = group // (NY * NC)
     for start in range(0, rows, TILE):
-        q = q_ref[start : start + TILE, :]
-        row = start + lax.broadcasted_iota(jnp.int32, (TILE, 1), 0)
-        place = (row // group) * (NY * NC * fresh) + ((row % group) // strip) * fresh + z * strip + row % strip
+        here = slice(start, start + TILE)
+        q = q_ref[here, :]
         parts, top = [], None
         for index in range(count):
-            zs = lax.rem(z + shifts[index // 2] + NZ, NZ)
-            block = zs * NY * NC + yh * NC + (core if index % 2 == 0 else 1 - core)
+            shift = shifts[index // 2]
+            zs = lax.rem(z + shift + NZ, NZ)
+            mine = yh * NC + (core if index % 2 == 0 else 1 - core)
             s = lax.dot_general(
                 q, kv_refs[index][:, :HEAD], (((1,), (1,)), ((), ())), preferred_element_type=F32
             )
             col = lax.broadcasted_iota(jnp.int32, (1, cache), 1)
-            stored = s[:, :cache] + jnp.where(col < lens[block], 0.0, NEG)
-            col = lax.broadcasted_iota(jnp.int32, (1, fresh), 1)
-            new = jnp.where(block * fresh + col <= place, s[:, cache:], NEG)
+            stored = s[:, :cache] + jnp.where(col < lens[zs * NY * NC + mine], 0.0, NEG)
+            if shift == 0:
+                row = start + lax.broadcasted_iota(jnp.int32, (TILE, fresh), 0)
+                col = mine * fresh + lax.broadcasted_iota(jnp.int32, (TILE, fresh), 1)
+                new = jnp.where(col <= row, s[:, cache:], NEG)
+            else:
+                new = s[:, cache:] + jnp.where(zs < z, 0.0, NEG)
             s = jnp.concatenate([stored, new], 1)
             parts.append(s)
             for at in range(0, cache + fresh, HEAD):
@@ -78,26 +80,32 @@
                 top = piece if top is None else jnp.maximum(top, piece)
         m = top.max(axis=1, keepdims=True)
         if first:
-            l, acc = 0.0, 0.0
+            l, acc = None, None
         else:
-            before = ml_in[start : start + TILE, 0:1]
+            before = top_in[here, :]
             m = jnp.maximum(m, before)
             alpha = jnp.exp2((before - m) * factor)
-            l = ml_in[start : start + TILE, 64:65] * alpha
-            acc = acc_in[start : start + TILE, :] * alpha
+            m = m[:, 0:1]
+            l = sum_in[here, :] * alpha
+            acc = acc_in[here, :] * alpha
         for index in range(count):
             p = jnp.exp2((parts[index] - m) * factor)
-            l = l + p.sum(axis=1, keepdims=True)
-            acc = acc + jnp.dot(p.astype(BF16), kv_refs[index][:, HEAD:], preferred_element_type=F32)
+            for at in range(0, cache + fresh, HEAD):
+                piece = p[:, at : at + HEAD]
+                l = piece if l is None else l + piece
+            term = jnp.dot(p.astype(BF16), kv_refs[index][:, HEAD:], preferred_element_type=F32)
+            acc = term if acc is None else acc + term
         if not last:
-            acc_out, ml_out = refs
-            acc_out[start : start + TILE, :] = acc
-            lane = lax.broadcasted_iota(jnp.int32, (TILE, HEAD), 1)
-            ml_out[start : start + TILE, :] = jnp.where(lane < 64, m, l)
+            acc_out, top_out, sum_out = refs
+            acc_out[here, :] = acc
+            top_out[here, :] = jnp.broadcast_to(m, (TILE, HEAD))
+            sum_out[here, :] = l
             continue
         out_ref = refs[0]
+        l = l.sum(axis=1, keepdims=True)
         out = (acc / l).astype(BF16)
         lse = m * factor + jnp.log2(l)
+        group = rows // (NX * NL)
         for at in range(0, TILE, group):
             out_ref[0, (start + at) // group, 0:group, :] = out[at : at + group, :]
         for at in range(0, TILE, 2 * group):
@@ -114,7 +122,7 @@
 def attend(meta, lens, q, kvs, shifts, state, last, cache, fresh):
     rows, width = q.shape
     heads = width // HEAD
-    group = rows // NZ
+    group = rows // (NX * NL)
     first = state is None
     span = cache + fresh
     whole = pl.BlockSpec((span, 2 * HEAD), lambda h, *_: (0, 0))
@@ -122,15 +130,15 @@
     in_specs = [per_head] + [whole] * len(kvs)
     args = [q] + list(kvs)
     if not first:
-        in_specs += [per_head, per_head]
+        in_specs += [per_head] * 3
         args += list(state)
     if last:
         pair = heads // NY
-        out_specs = pl.BlockSpec((1, NZ, group + TAIL, HEAD), lambda h, *_: (h // pair, 0, 0, h % pair))
-        out_shape = jax.ShapeDtypeStruct((NY, NZ, group + TAIL, pair * HEAD), BF16)
+        out_specs = pl.BlockSpec((1, NX * NL, group + TAIL, HEAD), lambda h, *_: (h // pair, 0, 0, h % pair))
+        out_shape = jax.ShapeDtypeStruct((NY, NX * NL, group + TAIL, pair * HEAD), BF16)
     else:
-        out_specs = [per_head, per_head]
-        out_shape = [jax.ShapeDtypeStruct((rows, width), F32)] * 2
+        out_specs = [per_head] * 3
+        out_shape = [jax.ShapeDtypeStruct((rows, width), F32)] * 3
     return pl.pallas_call(
         functools.partial(attend_kernel, tuple(shifts), first, last, rows, cache, fresh),
         grid_spec=pltpu.PrefetchScalarGridSpec(
@@ -224,31 +232,30 @@
     )(*blocks, *weights)
 
 
-def finish_kernel(order, strip, meta, *refs):
+def settle_kernel(order, meta, *refs):
     out = refs[-1]
-    width = out.shape[1]
-    z = meta[0]
-    parts = len(order)
+    width = out.shape[3]
+    z, yh = meta[0], meta[1]
     for part, shifts in enumerate(order):
-        kept, core, far = refs[3 * part : 3 * part + 3]
+        kept, near = refs[2 * part : 2 * part + 2]
+        group = kept.shape[0] // len(shifts)
         for at, shift in enumerate(shifts):
             zs = lax.rem(z + shift + NZ, NZ)
-            for p in range(NY * NC):
-                here = pl.ds((at * NY * NC + p) * strip, strip)
-                total = kept[here, :width] + core[here, :width].astype(F32) + far[here, :].astype(F32)
-                spot = pl.multiple_of((p * NZ + zs) * strip, strip)
-                out[pl.ds(spot, strip), :] = total.astype(BF16)
-
-
-def finish(meta, order, parts):
-    strip = 16
+            here = pl.ds(at * group, group)
+            total = (kept[here, :] + near[here, :].astype(F32)).astype(BF16)
+            for half in range(NY):
+                out[lax.rem(yh + half, NY), zs] = total[:, half * width : (half + 1) * width]
+
+
+def settle(meta, order, parts):
     rows = sum(part[0].shape[0] for part in parts)
+    width = parts[0][0].shape[1] // NY
     flat = [array for part in parts for array in part]
     return pl.pallas_call(
-        functools.partial(finish_kernel, order, strip),
+        functools.partial(settle_kernel, order),
         in_specs=[pl.BlockSpec(memory_space=pltpu.SMEM)] + [pl.BlockSpec(memory_space=pltpu.VMEM)] * len(flat),
         out_specs=pl.BlockSpec(memory_space=pltpu.VMEM),
-        out_shape=jax.ShapeDtypeStruct((rows, parts[0][2].shape[1]), BF16),
+        out_shape=jax.ShapeDtypeStruct((NY, NZ, rows // NZ, width), BF16),
         compiler_params=pltpu.CompilerParams(vmem_limit_bytes=VMEM),
     )(meta, *flat)
 
@@ -276,27 +283,18 @@
     mine = lax.dynamic_slice_in_dim(queries, core * half, half, 1)
     theirs = lax.dynamic_slice_in_dim(queries, (1 - core) * half, half, 1)
     received = swap(theirs, b=1)
-    strips = lambda value: value.reshape(NZ, 1, fresh // NZ, half)
     near = jnp.where(
         core == 0,
-        jnp.concatenate([strips(mine), strips(received)], 1),
-        jnp.concatenate([strips(received), strips(mine)], 1),
-    )
-    near = jnp.broadcast_to(near[:, None], (NZ, NY, NC, fresh // NZ, half))
-    q = lax.all_to_all(
-        near.reshape(NZ * NY, NC * fresh // NZ, half), ("z", "yh"), split_axis=0, concat_axis=0, tiled=True
-    ).reshape(NY * NC * fresh, half)
-
-    state = attend(
-        meta, cache_lengths, q, pair(kv) + pair(forth[1]) + pair(back[1]), (0, -1, 1), None, False, cache, fresh
-    )
-    state = attend(
-        meta, cache_lengths, q, pair(forth[2]) + pair(back[2]), (-2, 2), state, False, cache, fresh
-    )
-    state = attend(
-        meta, cache_lengths, q, pair(forth[3]) + pair(back[3]), (-3, 3), state, False, cache, fresh
-    )
-    pieces = attend(meta, cache_lengths, q, pair(forth[4]), (-4,), state, True, cache, fresh)
+        jnp.concatenate([mine, received], 0),
+        jnp.concatenate([received, mine], 0),
+    )
+    far = swap(near, a=1)
+    q = jnp.where(yh == 0, jnp.concatenate([near, far], 0), jnp.concatenate([far, near], 0))
+
+    near_kv = pair(kv) + pair(forth[1]) + pair(back[1]) + pair(forth[2]) + pair(back[2])
+    state = attend(meta, cache_lengths, q, near_kv, (0, -1, 1, -2, 2), None, False, cache, fresh)
+    far_kv = pair(forth[3]) + pair(back[3]) + pair(forth[4])
+    pieces = attend(meta, cache_lengths, q, far_kv, (-3, 3, -4), state, True, cache, fresh)
 
     depth = out_weight.shape[0] // 4
 
@@ -312,7 +310,8 @@
     own_2, twin_2 = shift_x(own_f, 1), shift_x(twin_b, -1)
     weights = [own, twin, own_b, twin_b, own_2, twin_2, own_f, twin_f]
 
-    group, width = pieces.shape[2] , pieces.shape[3]
+    group, width = pieces.shape[2], pieces.shape[3]
+    pieces, weights = lax.optimization_barrier((pieces, weights))
     pieces = lax.all_to_all(
         pieces.reshape(NY * NZ, group, width), ("yh", "x", "yl"), split_axis=0, concat_axis=0, tiled=True
     )
@@ -325,15 +324,17 @@
 
     def share(blocks):
         kept, sent = project(blocks, weights)
-        near = swap(sent, b=1)
-        width = kept.shape[1] // 2
-        part = (kept[:, width:] + near[:, width:].astype(F32)).astype(BF16)
-        return kept, near, swap(part, a=1)
+        return kept, swap(sent, b=1)
 
     order = ((0, -1, 1, -2, 2), (-3, 3, -4))
     first = share([a, forth[1], back[1], forth[2], back[2]])
     second = share([forth[3], back[3], forth[4]])
-    return finish(meta, order, (first, second))
+    settled = settle(meta, order, (first, second))
+    rows, width = settled.shape[2:]
+    home = lax.all_to_all(
+        settled.reshape(NY * NZ, rows, width), ("yh", "x", "yl"), split_axis=0, concat_axis=0, tiled=True
+    ).reshape(NY, NZ * rows, width)
+    return (home[0].astype(F32) + home[1].astype(F32)).astype(BF16)
 
 
 def solution(mesh):

time: 166 us -> 155 us (0.934)
  blocking collectives: 0 us -> 29 us
  waiting for transfers between devices: 56.4 us -> 30.6 us
  Pallas kernels: 45.7 us -> 33.5 us
  starting transfers between devices: 61.5 us -> 55.9 us
  other arithmetic: 0.19 us -> 2.29 us
    all_to_all x0 -> x2, blocking collectives: none -> 29 us  [the longest x1 15.2 us: shards(): lax.all_to_all(pieces.reshape(NY * NZ, group, width), ('yh', 'x', 'yl'),...]
    ppermute x37 -> x36, waiting for transfers between devices: 49.4 us -> 30.6 us  [permute(): return lax.ppermute(value, AXES, pairs)]
    all_to_all x2 -> x0, starting transfers between devices: 15.4 us -> none  [the longest x1 9.33 us: shards(): lax.all_to_all(near.reshape(NZ * NY, NC * fresh // NZ, half), ('z', 'yh')...]
    pallas_call x4 -> x2, Pallas kernels: 37.2 us -> 25.7 us  [attend(): pl.pallas_call(functools.partial(attend_kernel, tuple(shifts), first, las...]
    ppermute x37 -> x36, starting transfers between devices: 46 us -> 55.9 us  [permute(): return lax.ppermute(value, AXES, pairs)]
    all_to_all x2 -> x0, waiting for transfers between devices: 7.01 us -> none  [the longest x1 7.01 us: shards(): lax.all_to_all(pieces.reshape(NY * NZ, group, width), ('yh', 'x', 'yl'),...]
    unnamed x14 -> x28, local copies, waits for them, and re-layouts: 0.03 us -> 2.09 us
  transfers between devices with their start and end apart: 39 -> 36, of which waited for: 11 -> 10; matrix products, arithmetic and copies ran while one was open for 0% -> 1% of each run, Pallas kernels for 27% -> 20%
where the time goes in v1:
time: 155 us
  starting transfers between devices  55.9 us (36%)
  Pallas kernels  33.5 us (22%)
  waiting for transfers between devices  30.6 us (20%)
  blocking collectives  29 us (19%)
  local copies, waits for them, and re-layouts  3.36 us (2%)
  other arithmetic  2.29 us (1%)
    ppermute x36, starting transfers between devices, permute(): return lax.ppermute(value, AXES, pairs)  55.9 us
    ppermute x36, waiting for transfers between devices, permute(): return lax.ppermute(value, AXES, pairs)  30.6 us
    pallas_call x2, Pallas kernels, attend(): pl.pallas_call(functools.partial(attend_kernel, tuple(shifts), first, las...  25.7 us
    all_to_all x1, blocking collectives, shards(): lax.all_to_all(pieces.reshape(NY * NZ, group, width), ('yh', 'x', 'yl'),...  15.2 us
    all_to_all x1, blocking collectives, shards(): lax.all_to_all(settled.reshape(NY * NZ, rows, width), ('yh', 'x', 'yl'),...  13.7 us
    pallas_call x2, Pallas kernels, project(): pl.pallas_call(functools.partial(project_kernel, len(blocks)), grid=(4,),...  6.01 us
  transfers between devices with their start and end apart: 36, of which 10 were waited for; matrix products, arithmetic and copies ran while one was open for 1% of the time, Pallas kernels for 20%

profile of v1, /device:TPU:1, one launch (start us, length us, event | category | flops | bytes accessed | tf_op | source)
XLA Modules:
  0.0 154.9 jit_solution(11648446427937417107)
XLA Ops:
  1.2 4.4 %collective-permute-start.19 = (bf16[256,256]{1,0:T(8,128)(2,1)S(1)}, bf16[256,256]{1,0:T(8,128)(2,1)S(1)}, u32[]{:S(2)}, u32[]{:S(2)}) collective-permute-start(bf16[256,256]{1,0:T(8,128)(2,1)S(1)} %get-tuple-element.39), channel_id=1, source_target_pairs={{0,24},{1,25},{2,26},{3,27},{4,28},{5,29},{6,30},{7,31},{8,16},{9,... | collective-permute-start | bytes 393224 | tf_op jit(solution)/shard_map/ppermute | solution.py:34
  5.6 1.8 %collective-permute-start.17 = (bf16[256,256]{1,0:T(8,128)(2,1)S(1)}, bf16[256,256]{1,0:T(8,128)(2,1)S(1)}, u32[]{:S(2)}, u32[]{:S(2)}) collective-permute-start(bf16[256,256]{1,0:T(8,128)(2,1)S(1)} %get-tuple-element.38), channel_id=1, source_target_pairs={{0,16},{1,17},{2,18},{3,19},{4,20},{5,21},{6,22},{7,23},{8,24},{9,... | collective-permute-start | bytes 393224 | tf_op jit(solution)/shard_map/ppermute | solution.py:34
  8.9 3.1 %collective-permute-done.17 = bf16[256,256]{1,0:T(8,128)(2,1)S(1)} collective-permute-done((bf16[256,256]{1,0:T(8,128)(2,1)S(1)}, bf16[256,256]{1,0:T(8,128)(2,1)S(1)}, u32[]{:S(2)}, u32[]{:S(2)}) %collective-permute-start.17) | collective-permute-done | bytes 131104 | tf_op jit(solution)/shard_map/ppermute | solution.py:34
  12.1 1.6 %collective-permute-start.20 = (bf16[256,1024]{1,0:T(8,128)(2,1)S(1)}, bf16[256,1024]{1,0:T(8,128)(2,1)S(1)}, u32[]{:S(2)}, u32[]{:S(2)}) collective-permute-start(bf16[256,1024]{1,0:T(8,128)(2,1)S(1)} %pad_maximum_fusion.refs_5_.refs_3_), channel_id=1, source_target_pairs={{0,1},{1,0},{2,3},{3,2},{4,5},{5,4},{6,7},{7,6},{8,9},{9,8},{10,11... | collective-permute-start | bytes 1572872 | tf_op jit(solution)/shard_map/ppermute | solution.py:34
  13.7 1.7 %collective-permute-start.2 = (bf16[384,256]{1,0:T(8,128)(2,1)S(1)}, bf16[384,256]{1,0:T(8,128)(2,1)S(1)}, u32[]{:S(2)}, u32[]{:S(2)}) collective-permute-start(bf16[384,256]{1,0:T(8,128)(2,1)S(1)} %maximum_maximum_fusion.refs_0_), channel_id=1, source_target_pairs={{0,32},{1,33},{2,34},{3,35},{4,36},{5,37},{6,38},{7,39},{8,40},{9,... | collective-permute-start | bytes 589832 | tf_op jit(solution)/shard_map/ppermute | solution.py:34
  15.5 4.0 %collective-permute-start.6 = (bf16[384,256]{1,0:T(8,128)(2,1)S(1)}, bf16[384,256]{1,0:T(8,128)(2,1)S(1)}, u32[]{:S(2)}, u32[]{:S(2)}) collective-permute-start(bf16[384,256]{1,0:T(8,128)(2,1)S(1)} %maximum_maximum_fusion.refs_0_), channel_id=1, source_target_pairs={{0,224},{1,225},{2,226},{3,227},{4,228},{5,229},{6,230},{7,231},{8... | collective-permute-start | bytes 589832 | tf_op jit(solution)/shard_map/ppermute | solution.py:34
  19.6 2.9 %collective-permute-start.1 = (bf16[256,512]{1,0:T(8,128)(2,1)S(1)}, bf16[256,512]{1,0:T(8,128)(2,1)}, u32[]{:S(2)}, u32[]{:S(2)}) collective-permute-start(bf16[256,512]{1,0:T(8,128)(2,1)S(1)} %maximum_select_fusion.1), channel_id=1, source_target_pairs={{0,16},{1,17},{2,18},{3,19},{4,20},{5,21},{6,22},{7,23},{8,24},{9,... | collective-permute-start | bytes 786440 | tf_op jit(solution)/shard_map/ppermute | solution.py:34
  23.8 2.7 %collective-permute-start.7 = (bf16[384,256]{1,0:T(8,128)(2,1)S(1)}, bf16[384,256]{1,0:T(8,128)(2,1)S(1)}, u32[]{:S(2)}, u32[]{:S(2)}) collective-permute-start(bf16[384,256]{1,0:T(8,128)(2,1)S(1)} %collective-permute-done.6.refs_4_), channel_id=1, source_target_pairs={{0,224},{1,225},{2,226},{3,227},{4,228},{5,229},{6,230},{7,231},{8... | collective-permute-start | bytes 589832 | tf_op jit(solution)/shard_map/ppermute | solution.py:34
  26.4 2.1 %collective-permute-start.13 = (bf16[384,256]{1,0:T(8,128)(2,1)S(1)}, bf16[384,256]{1,0:T(8,128)(2,1)S(1)}, u32[]{:S(2)}, u32[]{:S(2)}) collective-permute-start(bf16[384,256]{1,0:T(8,128)(2,1)S(1)} %collective-permute-done.2.refs_2_), channel_id=1, source_target_pairs={{0,8},{1,9},{2,10},{3,11},{4,12},{5,13},{6,14},{7,15},{8,0},{9,1},... | collective-permute-start | bytes 589832 | tf_op jit(solution)/shard_map/ppermute | solution.py:34
  28.5 5.4 %collective-permute-done.1 = bf16[256,512]{1,0:T(8,128)(2,1)} collective-permute-done((bf16[256,512]{1,0:T(8,128)(2,1)S(1)}, bf16[256,512]{1,0:T(8,128)(2,1)}, u32[]{:S(2)}, u32[]{:S(2)}) %collective-permute-start.1) | collective-permute-done | bytes 262176 | tf_op jit(solution)/shard_map/ppermute | solution.py:34
  35.1 1.6 %collective-permute-start.4 = (bf16[384,256]{1,0:T(8,128)(2,1)S(1)}, bf16[384,256]{1,0:T(8,128)(2,1)}, u32[]{:S(2)}, u32[]{:S(2)}) collective-permute-start(bf16[384,256]{1,0:T(8,128)(2,1)S(1)} %collective-permute-done.3.refs_6_), channel_id=1, source_target_pairs={{0,32},{1,33},{2,34},{3,35},{4,36},{5,37},{6,38},{7,39},{8,40},{9,... | collective-permute-start | bytes 589832 | tf_op jit(solution)/shard_map/ppermute | solution.py:34
  38.0 1.5 collective-permute-start.22
  39.5 4.0 %collective-permute-start.8 = (bf16[384,256]{1,0:T(8,128)(2,1)S(1)}, bf16[384,256]{1,0:T(8,128)(2,1)}, u32[]{:S(2)}, u32[]{:S(2)}) collective-permute-start(bf16[384,256]{1,0:T(8,128)(2,1)S(1)} %collective-permute-done.7.refs_8_), channel_id=1, source_target_pairs={{0,224},{1,225},{2,226},{3,227},{4,228},{5,229},{6,230},{7,231},{8... | collective-permute-start | bytes 589832 | tf_op jit(solution)/shard_map/ppermute | solution.py:34
  47.2 1.4 collective-permute-start.5
  50.2 1.4 maximum_select_fusion.q_ref
  51.6 1.3 collective-permute-start.21
  53.2 5.4 %collective-permute-done.10.refs_4_ = bf16[384,256]{1,0:T(8,128)(2,1)} collective-permute-done((bf16[384,256]{1,0:T(8,128)(2,1)}, bf16[384,256]{1,0:T(8,128)(2,1)}, u32[]{:S(2)}, u32[]{:S(2)}) %collective-permute-start.10) | collective-permute-done | bytes 196640 | tf_op jit(solution)/shard_map/ppermute | solution.py:34
  59.7 1.3 collective-permute-start.25
  61.0 13.6 %shard_map.73 = (f32[512,512]{1,0:T(8,128)S(1)}, f32[512,512]{1,0:T(8,128)S(1)}, f32[512,512]{1,0:T(8,128)S(1)}) custom-call(s32[5]{0:T(128)S(1)} %stack.23.meta, s32[32]{0:T(128)S(1)} %copy-done.7, bf16[512,512]{1,0:T(8,128)(2,1)S(1)} %maximum_select_fusion.q_ref, bf16[384,256]{1,0:T(8,128)(2,1)S(1)} %maximum_maximum_fusion.refs_0_, ...), custom_call_target="tpu_custom_call" | custom-call | flops 8053063680 | bytes 1048576 | tf_op jit(solution)/shard_map/pallas_call | solution.py:142
  74.5 12.1 %shard_map.74 = bf16[2,8,80,256]{3,2,1,0:T(8,128)(2,1)S(1)} custom-call(s32[5]{0:T(128)S(1)} %stack.23.meta, s32[32]{0:T(128)S(1)} %copy-done.7, bf16[512,512]{1,0:T(8,128)(2,1)S(1)} %maximum_select_fusion.q_ref, bf16[384,256]{1,0:T(8,128)(2,1)} %collective-permute-done.4.refs_0_, bf16[384,256]{1,0:T(8,128)(2,1)} %collective-permute-done.5.refs_1_, ...), custom_call_target="tpu_custom_call" | custom-call | flops 4831838208 | bytes 1048576 | tf_op jit(solution)/shard_map/pallas_call | solution.py:142
  86.7 15.2 %all_to_all.10.pieces = bf16[16,80,256]{2,1,0:T(8,128)(2,1)S(1)} all-to-all(bf16[16,80,256]{2,1,0:T(8,128)(2,1)S(1)} %bitcast.9), channel_id=1, replica_groups=mesh['z'=8,'yh'=2,'core'=2,'x'=4,'yl'=2] {'yh','x','yl'}, dimensions={0} | all-to-all | bytes 1310720 | tf_op jit(solution)/shard_map/all_to_all | solution.py:315
  103.3 2.7 %collective-permute-start.28 = (bf16[64,2048]{1,0:T(8,128)(2,1)S(1)}, bf16[64,2048]{1,0:T(8,128)(2,1)S(1)}, u32[]{:S(2)}, u32[]{:S(2)}) collective-permute-start(bf16[64,2048]{1,0:T(8,128)(2,1)S(1)} %shard_map.75.refs_0_), channel_id=1, source_target_pairs={{0,224},{1,225},{2,226},{3,227},{4,228},{5,229},{6,230},{7,231},{8... | collective-permute-start | bytes 786440 | tf_op jit(solution)/shard_map/ppermute | solution.py:34
  105.9 5.3 %collective-permute-done.27.refs_1_ = bf16[64,2048]{1,0:T(8,128)(2,1)S(1)} collective-permute-done((bf16[64,2048]{1,0:T(8,128)(2,1)S(1)}, bf16[64,2048]{1,0:T(8,128)(2,1)S(1)}, u32[]{:S(2)}, u32[]{:S(2)}) %collective-permute-start.27) | collective-permute-done | bytes 262176 | tf_op jit(solution)/shard_map/ppermute | solution.py:34
  111.2 2.7 %collective-permute-start.30 = (bf16[64,2048]{1,0:T(8,128)(2,1)S(1)}, bf16[64,2048]{1,0:T(8,128)(2,1)S(1)}, u32[]{:S(2)}, u32[]{:S(2)}) collective-permute-start(bf16[64,2048]{1,0:T(8,128)(2,1)S(1)} %collective-permute-done.28.refs_2_), channel_id=1, source_target_pairs={{0,224},{1,225},{2,226},{3,227},{4,228},{5,229},{6,230},{7,231},{8... | collective-permute-start | bytes 786440 | tf_op jit(solution)/shard_map/ppermute | solution.py:34
  113.9 4.4 %collective-permute-done.29.refs_3_ = bf16[64,2048]{1,0:T(8,128)(2,1)S(1)} collective-permute-done((bf16[64,2048]{1,0:T(8,128)(2,1)S(1)}, bf16[64,2048]{1,0:T(8,128)(2,1)S(1)}, u32[]{:S(2)}, u32[]{:S(2)}) %collective-permute-start.29) | collective-permute-done | bytes 262176 | tf_op jit(solution)/shard_map/ppermute | solution.py:34
  118.2 2.7 %collective-permute-start.33 = (bf16[64,2048]{1,0:T(8,128)(2,1)S(1)}, bf16[64,2048]{1,0:T(8,128)(2,1)S(1)}, u32[]{:S(2)}, u32[]{:S(2)}) collective-permute-start(bf16[64,2048]{1,0:T(8,128)(2,1)S(1)} %collective-permute-done.30.refs_4_), channel_id=1, source_target_pairs={{0,224},{1,225},{2,226},{3,227},{4,228},{5,229},{6,230},{7,231},{8... | collective-permute-start | bytes 786440 | tf_op jit(solution)/shard_map/ppermute | solution.py:34
  120.9 3.8 %collective-permute-done.32.refs_0_ = bf16[64,2048]{1,0:T(8,128)(2,1)S(1)} collective-permute-done((bf16[64,2048]{1,0:T(8,128)(2,1)S(1)}, bf16[64,2048]{1,0:T(8,128)(2,1)S(1)}, u32[]{:S(2)}, u32[]{:S(2)}) %collective-permute-start.32) | collective-permute-done | bytes 262176 | tf_op jit(solution)/shard_map/ppermute | solution.py:34
  124.7 3.7 %shard_map.76 = (f32[320,512]{1,0:T(8,128)}, bf16[320,512]{1,0:T(8,128)(2,1)S(1)}) custom-call(bf16[64,2048]{1,0:T(8,128)(2,1)S(1)} %shard_map.75.refs_0_, bf16[64,2048]{1,0:T(8,128)(2,1)S(1)} %collective-permute-done.27.refs_1_, bf16[64,2048]{1,0:T(8,128)(2,1)S(1)} %collective-permute-done.28.refs_2_, bf16[64,2048]{1,0:T(8,128)(2,1)S(1)} %collective-permute-done.29.refs_3_, ...), custom_call_target="tpu_custom_call" | custom-call | flops 1342177280 | bytes 2097152 | tf_op jit(solution)/shard_map/pallas_call | solution.py:214
  128.3 4.0 %collective-permute-start.31 = (bf16[320,512]{1,0:T(8,128)(2,1)S(1)}, bf16[320,512]{1,0:T(8,128)(2,1)S(1)}, u32[]{:S(2)}, u32[]{:S(2)}) collective-permute-start(bf16[320,512]{1,0:T(8,128)(2,1)S(1)} %get-tuple-element.34), channel_id=1, source_target_pairs={{0,8},{1,9},{2,10},{3,11},{4,12},{5,13},{6,14},{7,15},{8,0},{9,1},... | collective-permute-start | bytes 983048 | tf_op jit(solution)/shard_map/ppermute | solution.py:34
  132.4 2.4 %shard_map.77 = (f32[192,512]{1,0:T(8,128)S(1)}, bf16[192,512]{1,0:T(8,128)(2,1)S(1)}) custom-call(bf16[64,2048]{1,0:T(8,128)(2,1)S(1)} %collective-permute-done.32.refs_0_, bf16[64,2048]{1,0:T(8,128)(2,1)S(1)} %collective-permute-done.33.refs_1_, bf16[64,2048]{1,0:T(8,128)(2,1)S(1)} %collective-permute-done.34.refs_2_, ...), custom_call_target="tpu_custom_call" | custom-call | flops 805306368 | bytes 2097152 | tf_op jit(solution)/shard_map/pallas_call | solution.py:214
  134.7 4.0 %collective-permute-start.35 = (bf16[192,512]{1,0:T(8,128)(2,1)S(1)}, bf16[192,512]{1,0:T(8,128)(2,1)S(1)}, u32[]{:S(2)}, u32[]{:S(2)}) collective-permute-start(bf16[192,512]{1,0:T(8,128)(2,1)S(1)} %get-tuple-element.36), channel_id=1, source_target_pairs={{0,8},{1,9},{2,10},{3,11},{4,12},{5,13},{6,14},{7,15},{8,0},{9,1},... | collective-permute-start | bytes 589832 | tf_op jit(solution)/shard_map/ppermute | solution.py:34
  140.4 13.7 %all_to_all.11 = bf16[16,64,256]{2,1,0:T(8,128)(2,1)S(1)} all-to-all(bf16[16,64,256]{2,1,0:T(8,128)(2,1)S(1)} %bitcast.8), channel_id=1, replica_groups=mesh['z'=8,'yh'=2,'core'=2,'x'=4,'yl'=2] {'yh','x','yl'}, dimensions={0} | all-to-all | bytes 1048576 | tf_op jit(solution)/shard_map/all_to_all | solution.py:334
  (84 shorter events, 16.9 us)
Async XLA Ops:
  1.2 7.7 %collective-permute-start.19 = (bf16[256,256]{1,0:T(8,128)(2,1)S(1)}, bf16[256,256]{1,0:T(8,128)(2,1)S(1)}, u32[]{:S(2)}, u32[]{:S(2)}) collective-permute-start(bf16[256,256]{1,0:T(8,128)(2,1)S(1)} %get-tuple-element.39), channel_id=1, source_target_pairs={{0,24},{1,25},{2,26},{3,27},{4,28},{5,29},{6,30},{7,31},{8,16},{9,... | collective-permute-start | bytes 393224 | tf_op jit(solution)/shard_map/ppermute | solution.py:34
  5.6 6.4 %collective-permute-start.17 = (bf16[256,256]{1,0:T(8,128)(2,1)S(1)}, bf16[256,256]{1,0:T(8,128)(2,1)S(1)}, u32[]{:S(2)}, u32[]{:S(2)}) collective-permute-start(bf16[256,256]{1,0:T(8,128)(2,1)S(1)} %get-tuple-element.38), channel_id=1, source_target_pairs={{0,16},{1,17},{2,18},{3,19},{4,20},{5,21},{6,22},{7,23},{8,24},{9,... | collective-permute-start | bytes 393224 | tf_op jit(solution)/shard_map/ppermute | solution.py:34
  7.4 12.1 %collective-permute-start = (bf16[128,512]{1,0:T(8,128)(2,1)S(1)}, bf16[128,512]{1,0:T(8,128)(2,1)S(1)}, u32[]{:S(2)}, u32[]{:S(2)}) collective-permute-start(bf16[128,512]{1,0:T(8,128)(2,1)S(1)} %get-tuple-element.42), channel_id=1, source_target_pairs={{0,8},{1,9},{2,10},{3,11},{4,12},{5,13},{6,14},{7,15},{8,0},{9,1},... | collective-permute-start | bytes 393224 | tf_op jit(solution)/shard_map/ppermute | solution.py:34
  12.1 25.9 %collective-permute-start.20 = (bf16[256,1024]{1,0:T(8,128)(2,1)S(1)}, bf16[256,1024]{1,0:T(8,128)(2,1)S(1)}, u32[]{:S(2)}, u32[]{:S(2)}) collective-permute-start(bf16[256,1024]{1,0:T(8,128)(2,1)S(1)} %pad_maximum_fusion.refs_5_.refs_3_), channel_id=1, source_target_pairs={{0,1},{1,0},{2,3},{3,2},{4,5},{5,4},{6,7},{7,6},{8,9},{9,8},{10,11... | collective-permute-start | bytes 1572872 | tf_op jit(solution)/shard_map/ppermute | solution.py:34
  13.7 10.0 %collective-permute-start.2 = (bf16[384,256]{1,0:T(8,128)(2,1)S(1)}, bf16[384,256]{1,0:T(8,128)(2,1)S(1)}, u32[]{:S(2)}, u32[]{:S(2)}) collective-permute-start(bf16[384,256]{1,0:T(8,128)(2,1)S(1)} %maximum_maximum_fusion.refs_0_), channel_id=1, source_target_pairs={{0,32},{1,33},{2,34},{3,35},{4,36},{5,37},{6,38},{7,39},{8,40},{9,... | collective-permute-start | bytes 589832 | tf_op jit(solution)/shard_map/ppermute | solution.py:34
  15.5 8.3 %collective-permute-start.6 = (bf16[384,256]{1,0:T(8,128)(2,1)S(1)}, bf16[384,256]{1,0:T(8,128)(2,1)S(1)}, u32[]{:S(2)}, u32[]{:S(2)}) collective-permute-start(bf16[384,256]{1,0:T(8,128)(2,1)S(1)} %maximum_maximum_fusion.refs_0_), channel_id=1, source_target_pairs={{0,224},{1,225},{2,226},{3,227},{4,228},{5,229},{6,230},{7,231},{8... | collective-permute-start | bytes 589832 | tf_op jit(solution)/shard_map/ppermute | solution.py:34
  19.6 14.3 %collective-permute-start.1 = (bf16[256,512]{1,0:T(8,128)(2,1)S(1)}, bf16[256,512]{1,0:T(8,128)(2,1)}, u32[]{:S(2)}, u32[]{:S(2)}) collective-permute-start(bf16[256,512]{1,0:T(8,128)(2,1)S(1)} %maximum_select_fusion.1), channel_id=1, source_target_pairs={{0,16},{1,17},{2,18},{3,19},{4,20},{5,21},{6,22},{7,23},{8,24},{9,... | collective-permute-start | bytes 786440 | tf_op jit(solution)/shard_map/ppermute | solution.py:34
  23.8 11.4 %collective-permute-start.3 = (bf16[384,256]{1,0:T(8,128)(2,1)S(1)}, bf16[384,256]{1,0:T(8,128)(2,1)S(1)}, u32[]{:S(2)}, u32[]{:S(2)}) collective-permute-start(bf16[384,256]{1,0:T(8,128)(2,1)S(1)} %collective-permute-done.2.refs_2_), channel_id=1, source_target_pairs={{0,32},{1,33},{2,34},{3,35},{4,36},{5,37},{6,38},{7,39},{8,40},{9,... | collective-permute-start | bytes 589832 | tf_op jit(solution)/shard_map/ppermute | solution.py:34
  23.8 13.0 %collective-permute-start.7 = (bf16[384,256]{1,0:T(8,128)(2,1)S(1)}, bf16[384,256]{1,0:T(8,128)(2,1)S(1)}, u32[]{:S(2)}, u32[]{:S(2)}) collective-permute-start(bf16[384,256]{1,0:T(8,128)(2,1)S(1)} %collective-permute-done.6.refs_4_), channel_id=1, source_target_pairs={{0,224},{1,225},{2,226},{3,227},{4,228},{5,229},{6,230},{7,231},{8... | collective-permute-start | bytes 589832 | tf_op jit(solution)/shard_map/ppermute | solution.py:34
  26.4 13.0 %collective-permute-start.13 = (bf16[384,256]{1,0:T(8,128)(2,1)S(1)}, bf16[384,256]{1,0:T(8,128)(2,1)S(1)}, u32[]{:S(2)}, u32[]{:S(2)}) collective-permute-start(bf16[384,256]{1,0:T(8,128)(2,1)S(1)} %collective-permute-done.2.refs_2_), channel_id=1, source_target_pairs={{0,8},{1,9},{2,10},{3,11},{4,12},{5,13},{6,14},{7,15},{8,0},{9,1},... | collective-permute-start | bytes 589832 | tf_op jit(solution)/shard_map/ppermute | solution.py:34
  33.9 9.6 %collective-permute-start.14 = (bf16[384,256]{1,0:T(8,128)(2,1)S(1)}, bf16[384,256]{1,0:T(8,128)(2,1)S(1)}, u32[]{:S(2)}, u32[]{:S(2)}) collective-permute-start(bf16[384,256]{1,0:T(8,128)(2,1)S(1)} %collective-permute-done.6.refs_4_), channel_id=1, source_target_pairs={{0,8},{1,9},{2,10},{3,11},{4,12},{5,13},{6,14},{7,15},{8,0},{9,1},... | collective-permute-start | bytes 589832 | tf_op jit(solution)/shard_map/ppermute | solution.py:34
  35.1 11.0 %collective-permute-start.4 = (bf16[384,256]{1,0:T(8,128)(2,1)S(1)}, bf16[384,256]{1,0:T(8,128)(2,1)}, u32[]{:S(2)}, u32[]{:S(2)}) collective-permute-start(bf16[384,256]{1,0:T(8,128)(2,1)S(1)} %collective-permute-done.3.refs_6_), channel_id=1, source_target_pairs={{0,32},{1,33},{2,34},{3,35},{4,36},{5,37},{6,38},{7,39},{8,40},{9,... | collective-permute-start | bytes 589832 | tf_op jit(solution)/shard_map/ppermute | solution.py:34
  36.8 14.8 %collective-permute-start.23 = (bf16[256,1024]{1,0:T(8,128)(2,1)S(1)}, bf16[256,1024]{1,0:T(8,128)(2,1)S(1)}, u32[]{:S(2)}, u32[]{:S(2)}) collective-permute-start(bf16[256,1024]{1,0:T(8,128)(2,1)S(1)} %pad_maximum_fusion.refs_5_.refs_3_), channel_id=1, source_target_pairs={{0,2},{1,3},{2,4},{3,5},{4,6},{5,7},{6,0},{7,1},{8,10},{9,11},{10,... | collective-permute-start | bytes 1572872 | tf_op jit(solution)/shard_map/ppermute | solution.py:34
  38.0 21.7 %collective-permute-start.22 = (bf16[256,1024]{1,0:T(8,128)(2,1)S(1)}, bf16[256,1024]{1,0:T(8,128)(2,1)S(1)}, u32[]{:S(2)}, u32[]{:S(2)}) collective-permute-start(bf16[256,1024]{1,0:T(8,128)(2,1)S(1)} %collective-permute-done.20.refs_6_.refs_4_), channel_id=1, source_target_pairs={{0,6},{1,7},{2,0},{3,1},{4,2},{5,3},{6,4},{7,5},{8,14},{9,15},{10,... | collective-permute-start | bytes 1572872 | tf_op jit(solution)/shard_map/ppermute | solution.py:34
  39.5 7.7 %collective-permute-start.8 = (bf16[384,256]{1,0:T(8,128)(2,1)S(1)}, bf16[384,256]{1,0:T(8,128)(2,1)}, u32[]{:S(2)}, u32[]{:S(2)}) collective-permute-start(bf16[384,256]{1,0:T(8,128)(2,1)S(1)} %collective-permute-done.7.refs_8_), channel_id=1, source_target_pairs={{0,224},{1,225},{2,226},{3,227},{4,228},{5,229},{6,230},{7,231},{8... | collective-permute-start | bytes 589832 | tf_op jit(solution)/shard_map/ppermute | solution.py:34
  44.2 4.4 %collective-permute-start.15 = (bf16[384,256]{1,0:T(8,128)(2,1)S(1)}, bf16[384,256]{1,0:T(8,128)(2,1)S(1)}, u32[]{:S(2)}, u32[]{:S(2)}) collective-permute-start(bf16[384,256]{1,0:T(8,128)(2,1)S(1)} %collective-permute-done.3.refs_6_), channel_id=1, source_target_pairs={{0,8},{1,9},{2,10},{3,11},{4,12},{5,13},{6,14},{7,15},{8,0},{9,1},... | collective-permute-start | bytes 589832 | tf_op jit(solution)/shard_map/ppermute | solution.py:34
  47.2 5.8 %collective-permute-start.5 = (bf16[384,256]{1,0:T(8,128)(2,1)}, bf16[384,256]{1,0:T(8,128)(2,1)}, u32[]{:S(2)}, u32[]{:S(2)}) collective-permute-start(bf16[384,256]{1,0:T(8,128)(2,1)} %collective-permute-done.4.refs_0_), channel_id=1, source_target_pairs={{0,8},{1,9},{2,10},{3,11},{4,12},{5,13},{6,14},{7,15},{8,0},{9,1},... | collective-permute-start | bytes 589832 | tf_op jit(solution)/shard_map/ppermute | solution.py:34
  50.0 8.6 %collective-permute-start.10 = (bf16[384,256]{1,0:T(8,128)(2,1)}, bf16[384,256]{1,0:T(8,128)(2,1)}, u32[]{:S(2)}, u32[]{:S(2)}) collective-permute-start(bf16[384,256]{1,0:T(8,128)(2,1)} %collective-permute-done.4.refs_0_), channel_id=1, source_target_pairs={{0,32},{1,33},{2,34},{3,35},{4,36},{5,37},{6,38},{7,39},{8,40},{9,... | collective-permute-start | bytes 589832 | tf_op jit(solution)/shard_map/ppermute | solution.py:34
  51.6 35.1 %collective-permute-start.21 = (bf16[256,1024]{1,0:T(8,128)(2,1)S(1)}, bf16[256,1024]{1,0:T(8,128)(2,1)S(1)}, u32[]{:S(2)}, u32[]{:S(2)}) collective-permute-start(bf16[256,1024]{1,0:T(8,128)(2,1)S(1)} %pad_maximum_fusion.refs_5_.refs_3_), channel_id=1, source_target_pairs={{0,6},{1,7},{2,0},{3,1},{4,2},{5,3},{6,4},{7,5},{8,14},{9,15},{10,... | collective-permute-start | bytes 1572872 | tf_op jit(solution)/shard_map/ppermute | solution.py:34
  52.9 33.8 %collective-permute-start.26 = (bf16[256,1024]{1,0:T(8,128)(2,1)S(1)}, bf16[256,1024]{1,0:T(8,128)(2,1)S(1)}, u32[]{:S(2)}, u32[]{:S(2)}) collective-permute-start(bf16[256,1024]{1,0:T(8,128)(2,1)S(1)} %collective-permute-done.20.refs_6_.refs_4_), channel_id=1, source_target_pairs={{0,2},{1,3},{2,4},{3,5},{4,6},{5,7},{6,0},{7,1},{8,10},{9,11},{10,... | collective-permute-start | bytes 1572872 | tf_op jit(solution)/shard_map/ppermute | solution.py:34
  53.1 33.6 %collective-permute-start.24 = (bf16[256,1024]{1,0:T(8,128)(2,1)S(1)}, bf16[256,1024]{1,0:T(8,128)(2,1)S(1)}, u32[]{:S(2)}, u32[]{:S(2)}) collective-permute-start(bf16[256,1024]{1,0:T(8,128)(2,1)S(1)} %collective-permute-done.23.refs_11_.refs_9_), channel_id=1, source_target_pairs={{0,2},{1,3},{2,4},{3,5},{4,6},{5,7},{6,0},{7,1},{8,10},{9,11},{10,... | collective-permute-start | bytes 1572872 | tf_op jit(solution)/shard_map/ppermute | solution.py:34
  58.6 15.9 %collective-permute-start.11 = (bf16[384,256]{1,0:T(8,128)(2,1)}, bf16[384,256]{1,0:T(8,128)(2,1)S(1)}, u32[]{:S(2)}, u32[]{:S(2)}) collective-permute-start(bf16[384,256]{1,0:T(8,128)(2,1)} %collective-permute-done.10.refs_4_), channel_id=1, source_target_pairs={{0,8},{1,9},{2,10},{3,11},{4,12},{5,13},{6,14},{7,15},{8,0},{9,1},... | collective-permute-start | bytes 589832 | tf_op jit(solution)/shard_map/ppermute | solution.py:34
  59.7 27.1 %collective-permute-start.25 = (bf16[256,1024]{1,0:T(8,128)(2,1)S(1)}, bf16[256,1024]{1,0:T(8,128)(2,1)S(1)}, u32[]{:S(2)}, u32[]{:S(2)}) collective-permute-start(bf16[256,1024]{1,0:T(8,128)(2,1)S(1)} %collective-permute-done.22.refs_8_.refs_6_), channel_id=1, source_target_pairs={{0,6},{1,7},{2,0},{3,1},{4,2},{5,3},{6,4},{7,5},{8,14},{9,15},{10,... | collective-permute-start | bytes 1572872 | tf_op jit(solution)/shard_map/ppermute | solution.py:34
  103.2 8.0 %collective-permute-start.27 = (bf16[64,2048]{1,0:T(8,128)(2,1)S(1)}, bf16[64,2048]{1,0:T(8,128)(2,1)S(1)}, u32[]{:S(2)}, u32[]{:S(2)}) collective-permute-start(bf16[64,2048]{1,0:T(8,128)(2,1)S(1)} %shard_map.75.refs_0_), channel_id=1, source_target_pairs={{0,32},{1,33},{2,34},{3,35},{4,36},{5,37},{6,38},{7,39},{8,40},{9,... | collective-permute-start | bytes 786440 | tf_op jit(solution)/shard_map/ppermute | solution.py:34
  103.3 7.9 %collective-permute-start.28 = (bf16[64,2048]{1,0:T(8,128)(2,1)S(1)}, bf16[64,2048]{1,0:T(8,128)(2,1)S(1)}, u32[]{:S(2)}, u32[]{:S(2)}) collective-permute-start(bf16[64,2048]{1,0:T(8,128)(2,1)S(1)} %shard_map.75.refs_0_), channel_id=1, source_target_pairs={{0,224},{1,225},{2,226},{3,227},{4,228},{5,229},{6,230},{7,231},{8... | collective-permute-start | bytes 786440 | tf_op jit(solution)/shard_map/ppermute | solution.py:34
  111.2 7.0 %collective-permute-start.29 = (bf16[64,2048]{1,0:T(8,128)(2,1)S(1)}, bf16[64,2048]{1,0:T(8,128)(2,1)S(1)}, u32[]{:S(2)}, u32[]{:S(2)}) collective-permute-start(bf16[64,2048]{1,0:T(8,128)(2,1)S(1)} %collective-permute-done.27.refs_1_), channel_id=1, source_target_pairs={{0,32},{1,33},{2,34},{3,35},{4,36},{5,37},{6,38},{7,39},{8,40},{9,... | collective-permute-start | bytes 786440 | tf_op jit(solution)/shard_map/ppermute | solution.py:34
  111.2 7.0 %collective-permute-start.30 = (bf16[64,2048]{1,0:T(8,128)(2,1)S(1)}, bf16[64,2048]{1,0:T(8,128)(2,1)S(1)}, u32[]{:S(2)}, u32[]{:S(2)}) collective-permute-start(bf16[64,2048]{1,0:T(8,128)(2,1)S(1)} %collective-permute-done.28.refs_2_), channel_id=1, source_target_pairs={{0,224},{1,225},{2,226},{3,227},{4,228},{5,229},{6,230},{7,231},{8... | collective-permute-start | bytes 786440 | tf_op jit(solution)/shard_map/ppermute | solution.py:34
  118.2 6.4 %collective-permute-start.32 = (bf16[64,2048]{1,0:T(8,128)(2,1)S(1)}, bf16[64,2048]{1,0:T(8,128)(2,1)S(1)}, u32[]{:S(2)}, u32[]{:S(2)}) collective-permute-start(bf16[64,2048]{1,0:T(8,128)(2,1)S(1)} %collective-permute-done.29.refs_3_), channel_id=1, source_target_pairs={{0,32},{1,33},{2,34},{3,35},{4,36},{5,37},{6,38},{7,39},{8,40},{9,... | collective-permute-start | bytes 786440 | tf_op jit(solution)/shard_map/ppermute | solution.py:34
  118.2 14.1 %collective-permute-start.33 = (bf16[64,2048]{1,0:T(8,128)(2,1)S(1)}, bf16[64,2048]{1,0:T(8,128)(2,1)S(1)}, u32[]{:S(2)}, u32[]{:S(2)}) collective-permute-start(bf16[64,2048]{1,0:T(8,128)(2,1)S(1)} %collective-permute-done.30.refs_4_), channel_id=1, source_target_pairs={{0,224},{1,225},{2,226},{3,227},{4,228},{5,229},{6,230},{7,231},{8... | collective-permute-start | bytes 786440 | tf_op jit(solution)/shard_map/ppermute | solution.py:34
  124.7 7.7 %collective-permute-start.34 = (bf16[64,2048]{1,0:T(8,128)(2,1)S(1)}, bf16[64,2048]{1,0:T(8,128)(2,1)S(1)}, u32[]{:S(2)}, u32[]{:S(2)}) collective-permute-start(bf16[64,2048]{1,0:T(8,128)(2,1)S(1)} %collective-permute-done.32.refs_0_), channel_id=1, source_target_pairs={{0,32},{1,33},{2,34},{3,35},{4,36},{5,37},{6,38},{7,39},{8,40},{9,... | collective-permute-start | bytes 786440 | tf_op jit(solution)/shard_map/ppermute | solution.py:34
  128.3 10.4 %collective-permute-start.31 = (bf16[320,512]{1,0:T(8,128)(2,1)S(1)}, bf16[320,512]{1,0:T(8,128)(2,1)S(1)}, u32[]{:S(2)}, u32[]{:S(2)}) collective-permute-start(bf16[320,512]{1,0:T(8,128)(2,1)S(1)} %get-tuple-element.34), channel_id=1, source_target_pairs={{0,8},{1,9},{2,10},{3,11},{4,12},{5,13},{6,14},{7,15},{8,0},{9,1},... | collective-permute-start | bytes 983048 | tf_op jit(solution)/shard_map/ppermute | solution.py:34
  134.7 5.0 %collective-permute-start.35 = (bf16[192,512]{1,0:T(8,128)(2,1)S(1)}, bf16[192,512]{1,0:T(8,128)(2,1)S(1)}, u32[]{:S(2)}, u32[]{:S(2)}) collective-permute-start(bf16[192,512]{1,0:T(8,128)(2,1)S(1)} %get-tuple-element.36), channel_id=1, source_target_pairs={{0,8},{1,9},{2,10},{3,11},{4,12},{5,13},{6,14},{7,15},{8,0},{9,1},... | collective-permute-start | bytes 589832 | tf_op jit(solution)/shard_map/ppermute | solution.py:34
  (18 other events, 114.8 us)

commit v2 on v1

--- a/solution.py
+++ b/solution.py
@@ -46,8 +46,8 @@
     return permute(value, lambda z, yh, c, x, yl: (z, yh ^ a, c ^ b, x, yl ^ d))
 
 
-def attend_kernel(shifts, first, last, rows, cache, fresh, meta, lens, q_ref, *refs):
-    count = 2 * len(shifts)
+def attend_kernel(sources, first, last, rows, cache, fresh, meta, lens, q_ref, *refs):
+    count = len(sources)
     kv_refs, refs = refs[:count], refs[count:]
     if not first:
         acc_in, top_in, sum_in = refs[:3]
@@ -59,9 +59,9 @@
         q = q_ref[here, :]
         parts, top = [], None
         for index in range(count):
-            shift = shifts[index // 2]
+            shift, other = sources[index]
             zs = lax.rem(z + shift + NZ, NZ)
-            mine = yh * NC + (core if index % 2 == 0 else 1 - core)
+            mine = yh * NC + (1 - core if other else core)
             s = lax.dot_general(
                 q, kv_refs[index][:, :HEAD], (((1,), (1,)), ((), ())), preferred_element_type=F32
             )
@@ -119,16 +119,18 @@
                 out_ref[0, (start + at) // group + half, group : group + TAIL, :] = tail
 
 
-def attend(meta, lens, q, kvs, shifts, state, last, cache, fresh):
+def attend(meta, lens, q, kvs, state, last, cache, fresh):
     rows, width = q.shape
     heads = width // HEAD
     group = rows // (NX * NL)
     first = state is None
     span = cache + fresh
-    whole = pl.BlockSpec((span, 2 * HEAD), lambda h, *_: (0, 0))
+    whole = [
+        pl.BlockSpec((span, 2 * HEAD), functools.partial(lambda at, h, *_: (at, 0), at)) for _, at, _, _ in kvs
+    ]
     per_head = pl.BlockSpec((rows, HEAD), lambda h, *_: (0, h))
-    in_specs = [per_head] + [whole] * len(kvs)
-    args = [q] + list(kvs)
+    in_specs = [per_head] + whole
+    args = [q] + [entry[0] for entry in kvs]
     if not first:
         in_specs += [per_head] * 3
         args += list(state)
@@ -140,7 +142,7 @@
         out_specs = [per_head] * 3
         out_shape = [jax.ShapeDtypeStruct((rows, width), F32)] * 3
     return pl.pallas_call(
-        functools.partial(attend_kernel, tuple(shifts), first, last, rows, cache, fresh),
+        functools.partial(attend_kernel, tuple(entry[2:] for entry in kvs), first, last, rows, cache, fresh),
         grid_spec=pltpu.PrefetchScalarGridSpec(
             num_scalar_prefetch=2, grid=(heads,), in_specs=in_specs, out_specs=out_specs
         ),
@@ -155,10 +157,10 @@
 
 
 def combine_kernel(group, meta, pieces, out):
-    x, yl = meta[3], meta[4]
+    yl = meta[4]
 
     def one(t, _):
-        spot = lax.rem(t // NL - x + NX, NX) * NL + lax.rem(t + yl, NL)
+        spot = t // NL * NL + lax.rem(t + yl, NL)
         for at in range(0, pieces.shape[2], HEAD):
             values, weights = [], []
             for half in range(NY):
@@ -187,14 +189,11 @@
     )(meta, pieces)
 
 
-def project_kernel(count, *refs):
-    blocks, weights, (keep, send) = refs[:count], refs[count:-2], refs[-2:]
-    depth = weights[0].shape[0]
-    total = None
-    for at, weight in enumerate(weights):
-        a = jnp.concatenate([block[:, at * depth : (at + 1) * depth] for block in blocks], 0)
-        term = jnp.dot(a, weight[...], preferred_element_type=F32)
-        total = term if total is None else total + term
+def project_kernel(*refs):
+    blocks, weight, (keep, send) = refs[:-3], refs[-3], refs[-2:]
+    total = jnp.dot(
+        jnp.concatenate([block[...] for block in blocks], 0), weight[...], preferred_element_type=F32
+    )
 
     @pl.when(pl.program_id(0) < 2)
     def _():
@@ -205,16 +204,16 @@
         send[...] = total.astype(BF16)
 
 
-def project(blocks, weights):
+def project(blocks, weight):
     rows = blocks[0].shape[0] * len(blocks)
-    depth, width = weights[0].shape
+    depth, width = weight.shape
     tile = width // 4
+    place = lambda j: 2 * (j % 2) + j // 2
     whole = pl.BlockSpec(blocks[0].shape, lambda j: (0, 0))
-    column = pl.BlockSpec((depth, tile), lambda j: (0, j))
     return pl.pallas_call(
-        functools.partial(project_kernel, len(blocks)),
+        project_kernel,
         grid=(4,),
-        in_specs=[whole] * len(blocks) + [column] * len(weights),
+        in_specs=[whole] * len(blocks) + [pl.BlockSpec((depth, tile), lambda j: (0, place(j)))],
         out_specs=[
             pl.BlockSpec((rows, tile), lambda j: (0, jnp.minimum(j, 1))),
             pl.BlockSpec((rows, tile), lambda j: (0, jnp.maximum(j - 2, 0))),
@@ -225,11 +224,9 @@
         ],
         compiler_params=pltpu.CompilerParams(vmem_limit_bytes=VMEM),
         cost_estimate=pl.CostEstimate(
-            flops=2 * rows * depth * width * len(weights),
-            bytes_accessed=8 * depth * width,
-            transcendentals=0,
+            flops=2 * rows * depth * width, bytes_accessed=2 * depth * width, transcendentals=0
         ),
-    )(*blocks, *weights)
+    )(*blocks, weight)
 
 
 def settle_kernel(order, meta, *refs):
@@ -272,12 +269,8 @@
         ],
         0,
     )
-    forth, back = [kv], [kv]
-    for _ in range(3):
-        forth.append(shift_z(forth[-1], 1))
-        back.append(shift_z(back[-1], -1))
-    forth.append(shift_z(forth[-1], 1))
-    pair = lambda value: [value, swap(value, b=1)]
+    forth, back = shift_z(kv, 1), shift_z(kv, -1)
+    twin_kv = swap(kv, b=1)
 
     half = queries.shape[1] // 2
     mine = lax.dynamic_slice_in_dim(queries, core * half, half, 1)
@@ -291,27 +284,41 @@
     far = swap(near, a=1)
     q = jnp.where(yh == 0, jnp.concatenate([near, far], 0), jnp.concatenate([far, near], 0))
 
-    near_kv = pair(kv) + pair(forth[1]) + pair(back[1]) + pair(forth[2]) + pair(back[2])
-    state = attend(meta, cache_lengths, q, near_kv, (0, -1, 1, -2, 2), None, False, cache, fresh)
-    far_kv = pair(forth[3]) + pair(back[3]) + pair(forth[4])
-    pieces = attend(meta, cache_lengths, q, far_kv, (-3, 3, -4), state, True, cache, fresh)
+    blocks = [(kv, 0, 0, 0), (twin_kv, 0, 0, 1)]
+    state = None
+    for step in range(1, 5):
+        last = step == 4
+        if step > 1:
+            forth, back, state = lax.optimization_barrier((forth, back, state))
+        theirs = swap(forth if last else jnp.concatenate([forth, back], 0), b=1)
+        blocks += [(forth, 0, -step, 0)] + ([] if last else [(back, 0, step, 0)])
+        later = [(theirs, 0, -step, 1)] + ([] if last else [(theirs, 1, step, 1)])
+        if last:
+            blocks += later
+        else:
+            ahead, behind = shift_z(forth, 1), shift_z(back, -1) if step < 3 else None
+        state = attend(meta, cache_lengths, q, blocks, state, last, cache, fresh)
+        if not last:
+            forth, back, blocks = ahead, behind, later
+    pieces = state
 
     depth = out_weight.shape[0] // 4
-
-    def rows_of(a, b):
-        return lax.dynamic_slice_in_dim(out_weight, ((core ^ b) * 2 + (yh ^ a)) * depth, depth, 0)
-
-    own = jnp.concatenate(
-        [rows_of(0, 0), swap(rows_of(1, 0), a=1), swap(rows_of(0, 1), b=1), swap(rows_of(1, 1), a=1, b=1)], 1
-    )
-    twin = swap(own, d=1)
-    own_f, twin_f = shift_x(own, 1), shift_x(twin, 1)
-    own_b, twin_b = shift_x(own, -1), shift_x(twin, -1)
-    own_2, twin_2 = shift_x(own_f, 1), shift_x(twin_b, -1)
-    weights = [own, twin, own_b, twin_b, own_2, twin_2, own_f, twin_f]
+    weight, _ = lax.optimization_barrier((out_weight, received))
+    block = lambda value, at, rows: lax.dynamic_slice_in_dim(value, at * rows, rows, 0)
+    wide = jnp.concatenate(
+        [block(weight, core, 2 * depth), swap(block(weight, 1 - core, 2 * depth), b=1)], 1
+    )
+    keep, give = block(wide, yh, depth), block(wide, 1 - yh, depth)
+    wide = jnp.concatenate(
+        [
+            jnp.concatenate([keep, swap(give, a=1)], 1),
+            jnp.concatenate([swap(keep, d=1), swap(give, a=1, d=1)], 1),
+        ],
+        0,
+    )
+    weight = lax.all_gather(wide, "x", axis=0, tiled=True)
 
     group, width = pieces.shape[2], pieces.shape[3]
-    pieces, weights = lax.optimization_barrier((pieces, weights))
     pieces = lax.all_to_all(
         pieces.reshape(NY * NZ, group, width), ("yh", "x", "yl"), split_axis=0, concat_axis=0, tiled=True
     )
@@ -323,7 +330,7 @@
     forth.append(shift_z(forth[-1], 1))
 
     def share(blocks):
-        kept, sent = project(blocks, weights)
+        kept, sent = project(blocks, weight)
         return kept, swap(sent, b=1)
 
     order = ((0, -1, 1, -2, 2), (-3, 3, -4))

time: 155 us -> 166 us (1.071)
  starting transfers between devices: 55.9 us -> 41.5 us
  between operations: 0.21 us -> 13.6 us
  Pallas kernels: 33.5 us -> 40 us
  blocking collectives: 29 us -> 32.4 us
  local copies, waits for them, and re-layouts: 3.36 us -> 6.01 us
    ppermute x36 -> x27, starting transfers between devices: 55.9 us -> 41.5 us  [permute(): return lax.ppermute(value, AXES, pairs)]
    pallas_call x4 -> x6, Pallas kernels: 31.7 us -> 38.1 us  [the longest x4 31.3 us: attend(): pl.pallas_call(functools.partial(attend_kernel, tuple((entry[2:] for entr...]
    all_to_all x1, blocking collectives: 15.2 us -> 18.5 us  [shards(): lax.all_to_all(pieces.reshape(NY * NZ, group, width), ('yh', 'x', 'yl'),...]
    unnamed x28 -> x20, local copies, waits for them, and re-layouts: 2.09 us -> 3.87 us
    ppermute x36 -> x27, waiting for transfers between devices: 30.6 us -> 29.6 us  [permute(): return lax.ppermute(value, AXES, pairs)]
  transfers between devices with their start and end apart: 36 -> 28, of which waited for: 10 -> 11; matrix products, arithmetic and copies ran while one was open for 1% -> 0% of each run, Pallas kernels for 20% -> 24%
where the time goes in v2:
time: 166 us; the launch traced here: 165 us
  starting transfers between devices  41.5 us (25%)
  Pallas kernels  40 us (24%)
  blocking collectives  32.4 us (20%)
  waiting for transfers between devices  29.6 us (18%)
  between operations  13.6 us (8%)
  local copies, waits for them, and re-layouts  6.01 us (4%)
  other arithmetic  2.32 us (1%)
    ppermute x27, starting transfers between devices, permute(): return lax.ppermute(value, AXES, pairs)  41.5 us
    pallas_call x4, Pallas kernels, attend(): pl.pallas_call(functools.partial(attend_kernel, tuple((entry[2:] for entr...  31.3 us
    ppermute x27, waiting for transfers between devices, permute(): return lax.ppermute(value, AXES, pairs)  29.6 us
    all_to_all x1, blocking collectives, shards(): lax.all_to_all(pieces.reshape(NY * NZ, group, width), ('yh', 'x', 'yl'),...  18.5 us
    all_to_all x1, blocking collectives, shards(): lax.all_to_all(settled.reshape(NY * NZ, rows, width), ('yh', 'x', 'yl'),...  13.9 us
    pallas_call x2, Pallas kernels, project(): pl.pallas_call(project_kernel, grid=(4,), in_specs=[whole] * len(blocks)...  6.82 us
    unnamed x20, local copies, waits for them, and re-layouts  3.87 us
  transfers between devices with their start and end apart: 28, of which 11 were waited for; matrix products, arithmetic and copies ran while one was open for 0% of the time, Pallas kernels for 24%

profile of v2, /device:TPU:1, one launch (start us, length us, event | category | flops | bytes accessed | tf_op | source)
XLA Modules:
  0.0 165.4 jit_solution(9980713626496621599)
XLA Ops:
  7.5 3.3 %collective-permute-start = (bf16[128,512]{1,0:T(8,128)(2,1)S(1)}, bf16[128,512]{1,0:T(8,128)(2,1)S(1)}, u32[]{:S(2)}, u32[]{:S(2)}) collective-permute-start(bf16[128,512]{1,0:T(8,128)(2,1)S(1)} %get-tuple-element.66), channel_id=1, source_target_pairs={{0,8},{1,9},{2,10},{3,11},{4,12},{5,13},{6,14},{7,15},{8,0},{9,1},... | collective-permute-start | bytes 393224 | tf_op jit(solution)/shard_map/ppermute | solution.py:34
  13.4 1.2 collective-permute-done.18
  14.6 1.3 collective-permute-start.19
  16.3 1.7 %collective-permute-start.21 = (bf16[256,512]{1,0:T(8,128)(2,1)S(1)}, bf16[256,512]{1,0:T(8,128)(2,1)S(1)}, u32[]{:S(2)}, u32[]{:S(2)}) collective-permute-start(bf16[256,512]{1,0:T(8,128)(2,1)S(1)} %get-tuple-element.62), channel_id=1, source_target_pairs={{0,17},{1,16},{2,19},{3,18},{4,21},{5,20},{6,23},{7,22},{8,25},{9,... | collective-permute-start | bytes 786440 | tf_op jit(solution)/shard_map/ppermute | solution.py:34
  17.9 5.8 %collective-permute-done.19 = bf16[256,512]{1,0:T(8,128)(2,1)S(1)} collective-permute-done((bf16[256,512]{1,0:T(8,128)(2,1)S(1)}, bf16[256,512]{1,0:T(8,128)(2,1)S(1)}, u32[]{:S(2)}, u32[]{:S(2)}) %collective-permute-start.19) | collective-permute-done | bytes 262176 | tf_op jit(solution)/shard_map/ppermute | solution.py:34
  23.8 4.2 %collective-permute-done.20 = bf16[256,512]{1,0:T(8,128)(2,1)S(1)} collective-permute-done((bf16[256,512]{1,0:T(8,128)(2,1)S(1)}, bf16[256,512]{1,0:T(8,128)(2,1)S(1)}, u32[]{:S(2)}, u32[]{:S(2)}) %collective-permute-start.20) | collective-permute-done | bytes 262176 | tf_op jit(solution)/shard_map/ppermute | solution.py:34
  28.0 2.0 %collective-permute-done.21 = bf16[256,512]{1,0:T(8,128)(2,1)S(1)} collective-permute-done((bf16[256,512]{1,0:T(8,128)(2,1)S(1)}, bf16[256,512]{1,0:T(8,128)(2,1)S(1)}, u32[]{:S(2)}, u32[]{:S(2)}) %collective-permute-start.21) | collective-permute-done | bytes 262176 | tf_op jit(solution)/shard_map/ppermute | solution.py:34
  30.0 1.1 maximum_maximum_fusion
  31.4 3.9 %collective-permute-start.4 = (bf16[384,256]{1,0:T(8,128)(2,1)S(1)}, bf16[384,256]{1,0:T(8,128)(2,1)S(1)}, u32[]{:S(2)}, u32[]{:S(2)}) collective-permute-start(bf16[384,256]{1,0:T(8,128)(2,1)S(1)} %maximum_maximum_fusion.1.refs_0_), channel_id=1, source_target_pairs={{0,224},{1,225},{2,226},{3,227},{4,228},{5,229},{6,230},{7,231},{8... | collective-permute-start | bytes 589832 | tf_op jit(solution)/shard_map/ppermute | solution.py:34
  35.3 3.0 %collective-permute-start.1 = (bf16[256,512]{1,0:T(8,128)(2,1)S(1)}, bf16[256,512]{1,0:T(8,128)(2,1)S(1)}, u32[]{:S(2)}, u32[]{:S(2)}) collective-permute-start(bf16[256,512]{1,0:T(8,128)(2,1)S(1)} %maximum_select_fusion.1), channel_id=1, source_target_pairs={{0,16},{1,17},{2,18},{3,19},{4,20},{5,21},{6,22},{7,23},{8,24},{9,... | collective-permute-start | bytes 786440 | tf_op jit(solution)/shard_map/ppermute | solution.py:34
  39.6 1.6 collective-permute-start.9
  41.2 2.8 %collective-permute-start.5 = (bf16[384,256]{1,0:T(8,128)(2,1)S(1)}, bf16[384,256]{1,0:T(8,128)(2,1)S(1)}, u32[]{:S(2)}, u32[]{:S(2)}) collective-permute-start(bf16[384,256]{1,0:T(8,128)(2,1)S(1)} %collective-permute-done.4.refs_3_), channel_id=1, source_target_pairs={{0,224},{1,225},{2,226},{3,227},{4,228},{5,229},{6,230},{7,231},{8... | collective-permute-start | bytes 589832 | tf_op jit(solution)/shard_map/ppermute | solution.py:34
  44.2 6.5 %shard_map.73 = (f32[512,512]{1,0:T(8,128)S(1)}, f32[512,512]{1,0:T(8,128)S(1)}, f32[512,512]{1,0:T(8,128)S(1)}) custom-call(s32[5]{0:T(128)S(1)} %stack.23.meta, s32[32]{0:T(128)S(1)} %copy-done.1, bf16[512,512]{1,0:T(8,128)(2,1)S(1)} %maximum_select_fusion.q_ref, bf16[384,256]{1,0:T(8,128)(2,1)S(1)} %maximum_maximum_fusion.1.refs_0_, ...), custom_call_target="tpu_custom_call" | custom-call | flops 3221225472 | bytes 1048576 | tf_op jit(solution)/shard_map/pallas_call | solution.py:144
  52.6 2.7 %collective-permute-start.8 = (bf16[384,256]{1,0:T(8,128)(2,1)S(1)}, bf16[384,256]{1,0:T(8,128)(2,1)S(1)}, u32[]{:S(2)}, u32[]{:S(2)}) collective-permute-start(bf16[384,256]{1,0:T(8,128)(2,1)S(1)} %collective-permute-done.5.refs_3_), channel_id=1, source_target_pairs={{0,224},{1,225},{2,226},{3,227},{4,228},{5,229},{6,230},{7,231},{8... | collective-permute-start | bytes 589832 | tf_op jit(solution)/shard_map/ppermute | solution.py:34
  55.3 2.5 %collective-permute-start.12 = (bf16[768,256]{1,0:T(8,128)(2,1)S(1)}, bf16[768,256]{1,0:T(8,128)(2,1)S(1)}, u32[]{:S(2)}, u32[]{:S(2)}) collective-permute-start(bf16[768,256]{1,0:T(8,128)(2,1)S(1)} %pad_maximum_fusion.2), channel_id=1, source_target_pairs={{0,8},{1,9},{2,10},{3,11},{4,12},{5,13},{6,14},{7,15},{8,0},{9,1},... | collective-permute-start | bytes 1179656 | tf_op jit(solution)/shard_map/ppermute | solution.py:34
  57.9 8.3 %shard_map.74 = (f32[512,512]{1,0:T(8,128)S(1)}, f32[512,512]{1,0:T(8,128)S(1)}, f32[512,512]{1,0:T(8,128)S(1)}) custom-call(s32[5]{0:T(128)S(1)} %stack.23.meta, s32[32]{0:T(128)S(1)} %copy-done.1, bf16[512,512]{1,0:T(8,128)(2,1)S(1)} %maximum_select_fusion.q_ref, bf16[768,256]{1,0:T(8,128)(2,1)S(1)} %collective-permute-done.9.refs_0_.refs_1_, ...), custom_call_target="tpu_custom_call" | custom-call | flops 3221225472 | bytes 1048576 | tf_op jit(solution)/shard_map/pallas_call | solution.py:144
  68.3 8.3 %shard_map.75 = (f32[512,512]{1,0:T(8,128)S(1)}, f32[512,512]{1,0:T(8,128)S(1)}, f32[512,512]{1,0:T(8,128)S(1)}) custom-call(s32[5]{0:T(128)S(1)} %stack.23.meta, s32[32]{0:T(128)S(1)} %copy-done.1, bf16[512,512]{1,0:T(8,128)(2,1)S(1)} %maximum_select_fusion.q_ref, bf16[768,256]{1,0:T(8,128)(2,1)S(1)} %collective-permute-done.12.refs_0_.refs_1_, ...), custom_call_target="tpu_custom_call" | custom-call | flops 3221225472 | bytes 1048576 | tf_op jit(solution)/shard_map/pallas_call | solution.py:144
  78.2 8.2 %shard_map.76 = bf16[2,8,80,256]{3,2,1,0:T(8,128)(2,1)S(1)} custom-call(s32[5]{0:T(128)S(1)} %stack.23.meta, s32[32]{0:T(128)S(1)} %copy-done.1, bf16[512,512]{1,0:T(8,128)(2,1)S(1)} %maximum_select_fusion.q_ref, bf16[768,256]{1,0:T(8,128)(2,1)S(1)} %collective-permute-done.10.refs_0_.refs_1_, bf16[768,256]{1,0:T(8,128)(2,1)S(1)} %collective-permute-done.10.refs_0_.refs_1_, ...), custom_call_target="tpu_custom_call" | custom-call | flops 3221225472 | bytes 1048576 | tf_op jit(solution)/shard_map/pallas_call | solution.py:144
  86.5 18.5 %all_to_all.10.pieces = bf16[16,80,256]{2,1,0:T(8,128)(2,1)S(1)} all-to-all(bf16[16,80,256]{2,1,0:T(8,128)(2,1)S(1)} %bitcast.9), channel_id=1, replica_groups=mesh['z'=8,'yh'=2,'core'=2,'x'=4,'yl'=2] {'yh','x','yl'}, dimensions={0} | all-to-all | bytes 1310720 | tf_op jit(solution)/shard_map/all_to_all | solution.py:322
  104.9 1.2 shard_map.77.refs_0_
  106.3 3.3 %collective-permute-start.15 = (bf16[64,2048]{1,0:T(8,128)(2,1)S(1)}, bf16[64,2048]{1,0:T(8,128)(2,1)S(1)}, u32[]{:S(2)}, u32[]{:S(2)}) collective-permute-start(bf16[64,2048]{1,0:T(8,128)(2,1)S(1)} %shard_map.77.refs_0_), channel_id=1, source_target_pairs={{0,224},{1,225},{2,226},{3,227},{4,228},{5,229},{6,230},{7,231},{8... | collective-permute-start | bytes 786440 | tf_op jit(solution)/shard_map/ppermute | solution.py:34
  109.5 5.1 %collective-permute-done.14.refs_1_ = bf16[64,2048]{1,0:T(8,128)(2,1)S(1)} collective-permute-done((bf16[64,2048]{1,0:T(8,128)(2,1)S(1)}, bf16[64,2048]{1,0:T(8,128)(2,1)S(1)}, u32[]{:S(2)}, u32[]{:S(2)}) %collective-permute-start.14) | collective-permute-done | bytes 262176 | tf_op jit(solution)/shard_map/ppermute | solution.py:34
  114.6 2.7 %collective-permute-start.17 = (bf16[64,2048]{1,0:T(8,128)(2,1)S(1)}, bf16[64,2048]{1,0:T(8,128)(2,1)S(1)}, u32[]{:S(2)}, u32[]{:S(2)}) collective-permute-start(bf16[64,2048]{1,0:T(8,128)(2,1)S(1)} %collective-permute-done.15.refs_2_), channel_id=1, source_target_pairs={{0,224},{1,225},{2,226},{3,227},{4,228},{5,229},{6,230},{7,231},{8... | collective-permute-start | bytes 786440 | tf_op jit(solution)/shard_map/ppermute | solution.py:34
  117.3 4.2 %collective-permute-done.16.refs_3_ = bf16[64,2048]{1,0:T(8,128)(2,1)S(1)} collective-permute-done((bf16[64,2048]{1,0:T(8,128)(2,1)S(1)}, bf16[64,2048]{1,0:T(8,128)(2,1)S(1)}, u32[]{:S(2)}, u32[]{:S(2)}) %collective-permute-start.16) | collective-permute-done | bytes 262176 | tf_op jit(solution)/shard_map/ppermute | solution.py:34
  121.5 2.7 %collective-permute-start.24 = (bf16[64,2048]{1,0:T(8,128)(2,1)S(1)}, bf16[64,2048]{1,0:T(8,128)(2,1)S(1)}, u32[]{:S(2)}, u32[]{:S(2)}) collective-permute-start(bf16[64,2048]{1,0:T(8,128)(2,1)S(1)} %collective-permute-done.17.refs_4_), channel_id=1, source_target_pairs={{0,224},{1,225},{2,226},{3,227},{4,228},{5,229},{6,230},{7,231},{8... | collective-permute-start | bytes 786440 | tf_op jit(solution)/shard_map/ppermute | solution.py:34
  124.2 3.8 %collective-permute-done.23.refs_0_ = bf16[64,2048]{1,0:T(8,128)(2,1)S(1)} collective-permute-done((bf16[64,2048]{1,0:T(8,128)(2,1)S(1)}, bf16[64,2048]{1,0:T(8,128)(2,1)S(1)}, u32[]{:S(2)}, u32[]{:S(2)}) %collective-permute-start.23) | collective-permute-done | bytes 262176 | tf_op jit(solution)/shard_map/ppermute | solution.py:34
  127.9 4.4 %shard_map.78 = (f32[320,512]{1,0:T(8,128)S(1)}, bf16[320,512]{1,0:T(8,128)(2,1)S(1)}) custom-call(bf16[64,2048]{1,0:T(8,128)(2,1)S(1)} %shard_map.77.refs_0_, bf16[64,2048]{1,0:T(8,128)(2,1)S(1)} %collective-permute-done.14.refs_1_, bf16[64,2048]{1,0:T(8,128)(2,1)S(1)} %collective-permute-done.15.refs_2_, ...), custom_call_target="tpu_custom_call" | custom-call | flops 1342177280 | bytes 4194304 | tf_op jit(solution)/shard_map/pallas_call | solution.py:213
  132.4 4.3 %collective-permute-start.22 = (bf16[320,512]{1,0:T(8,128)(2,1)S(1)}, bf16[320,512]{1,0:T(8,128)(2,1)S(1)}, u32[]{:S(2)}, u32[]{:S(2)}) collective-permute-start(bf16[320,512]{1,0:T(8,128)(2,1)S(1)} %get-tuple-element.58), channel_id=1, source_target_pairs={{0,8},{1,9},{2,10},{3,11},{4,12},{5,13},{6,14},{7,15},{8,0},{9,1},... | collective-permute-start | bytes 983048 | tf_op jit(solution)/shard_map/ppermute | solution.py:34
  136.7 2.4 %shard_map.79 = (f32[192,512]{1,0:T(8,128)S(1)}, bf16[192,512]{1,0:T(8,128)(2,1)S(1)}) custom-call(bf16[64,2048]{1,0:T(8,128)(2,1)S(1)} %collective-permute-done.23.refs_0_, bf16[64,2048]{1,0:T(8,128)(2,1)S(1)} %collective-permute-done.24.refs_1_, bf16[64,2048]{1,0:T(8,128)(2,1)S(1)} %collective-permute-done.25.refs_2_, bf16[2048,1024]{1,0:T(8,128)(2,1)S(1)} %copy-done), custom_call_target="tpu_custom_call" | custom-call | flops 805306368 | bytes 4194304 | tf_op jit(solution)/shard_map/pallas_call | solution.py:213
  139.1 3.1 %collective-permute-start.26 = (bf16[192,512]{1,0:T(8,128)(2,1)S(1)}, bf16[192,512]{1,0:T(8,128)(2,1)S(1)}, u32[]{:S(2)}, u32[]{:S(2)}) collective-permute-start(bf16[192,512]{1,0:T(8,128)(2,1)S(1)} %get-tuple-element.60), channel_id=1, source_target_pairs={{0,8},{1,9},{2,10},{3,11},{4,12},{5,13},{6,14},{7,15},{8,0},{9,1},... | collective-permute-start | bytes 589832 | tf_op jit(solution)/shard_map/ppermute | solution.py:34
  142.1 1.1 collective-permute-done.26.refs_3_
  143.9 13.9 %all_to_all.11 = bf16[16,64,256]{2,1,0:T(8,128)(2,1)S(1)} all-to-all(bf16[16,64,256]{2,1,0:T(8,128)(2,1)S(1)} %bitcast.8), channel_id=1, replica_groups=mesh['z'=8,'yh'=2,'core'=2,'x'=4,'yl'=2] {'yh','x','yl'}, dimensions={0} | all-to-all | bytes 1048576 | tf_op jit(solution)/shard_map/all_to_all | solution.py:341
  (67 shorter events, 12.9 us)
Async XLA Ops:
  6.5 121.4 %all-gather.2.cloned.1.call-start = ((), (), s32[]{:S(2)}) async-start(), calls=%async_computation.2 | async-start | bytes 5242880 | tf_op jit(solution)/shard_map/all_gather | solution.py:319
  7.5 4.3 %collective-permute-start = (bf16[128,512]{1,0:T(8,128)(2,1)S(1)}, bf16[128,512]{1,0:T(8,128)(2,1)S(1)}, u32[]{:S(2)}, u32[]{:S(2)}) collective-permute-start(bf16[128,512]{1,0:T(8,128)(2,1)S(1)} %get-tuple-element.66), channel_id=1, source_target_pairs={{0,8},{1,9},{2,10},{3,11},{4,12},{5,13},{6,14},{7,15},{8,0},{9,1},... | collective-permute-start | bytes 393224 | tf_op jit(solution)/shard_map/ppermute | solution.py:34
  12.9 1.6 collective-permute-start.18
  14.5 16.7 %copy-start.6 = (bf16[256,128]{1,0:T(8,128)(2,1)S(1)}, bf16[256,128]{1,0:T(8,128)(2,1)}, u32[]{:S(2)}) copy-start(bf16[256,128]{1,0:T(8,128)(2,1)} %param.9) | copy-start | bytes 196612
  14.5 16.7 %copy-start.7 = (bf16[256,128]{1,0:T(8,128)(2,1)S(1)}, bf16[256,128]{1,0:T(8,128)(2,1)}, u32[]{:S(2)}) copy-start(bf16[256,128]{1,0:T(8,128)(2,1)} %param.8) | copy-start | bytes 196612
  14.5 16.7 %copy-start.8 = (bf16[128,128]{1,0:T(8,128)(2,1)S(1)}, bf16[128,128]{1,0:T(8,128)(2,1)}, u32[]{:S(2)}) copy-start(bf16[128,128]{1,0:T(8,128)(2,1)} %param.11) | copy-start | bytes 98308
  14.5 16.7 %copy-start.9 = (bf16[128,128]{1,0:T(8,128)(2,1)S(1)}, bf16[128,128]{1,0:T(8,128)(2,1)}, u32[]{:S(2)}) copy-start(bf16[128,128]{1,0:T(8,128)(2,1)} %param.10) | copy-start | bytes 98308
  14.6 9.2 %collective-permute-start.19 = (bf16[256,512]{1,0:T(8,128)(2,1)S(1)}, bf16[256,512]{1,0:T(8,128)(2,1)S(1)}, u32[]{:S(2)}, u32[]{:S(2)}) collective-permute-start(bf16[256,512]{1,0:T(8,128)(2,1)S(1)} %get-tuple-element.62), channel_id=1, source_target_pairs={{0,16},{1,17},{2,18},{3,19},{4,20},{5,21},{6,22},{7,23},{8,24},{9,... | collective-permute-start | bytes 786440 | tf_op jit(solution)/shard_map/ppermute | solution.py:34
  15.9 12.1 %collective-permute-start.20 = (bf16[256,512]{1,0:T(8,128)(2,1)S(1)}, bf16[256,512]{1,0:T(8,128)(2,1)S(1)}, u32[]{:S(2)}, u32[]{:S(2)}) collective-permute-start(bf16[256,512]{1,0:T(8,128)(2,1)S(1)} %get-tuple-element.61), channel_id=1, source_target_pairs={{0,1},{1,0},{2,3},{3,2},{4,5},{5,4},{6,7},{7,6},{8,9},{9,8},{10,11... | collective-permute-start | bytes 786440 | tf_op jit(solution)/shard_map/ppermute | solution.py:34
  16.3 13.8 %collective-permute-start.21 = (bf16[256,512]{1,0:T(8,128)(2,1)S(1)}, bf16[256,512]{1,0:T(8,128)(2,1)S(1)}, u32[]{:S(2)}, u32[]{:S(2)}) collective-permute-start(bf16[256,512]{1,0:T(8,128)(2,1)S(1)} %get-tuple-element.62), channel_id=1, source_target_pairs={{0,17},{1,16},{2,19},{3,18},{4,21},{5,20},{6,23},{7,22},{8,25},{9,... | collective-permute-start | bytes 786440 | tf_op jit(solution)/shard_map/ppermute | solution.py:34
  31.3 8.3 %collective-permute-start.2 = (bf16[384,256]{1,0:T(8,128)(2,1)S(1)}, bf16[384,256]{1,0:T(8,128)(2,1)S(1)}, u32[]{:S(2)}, u32[]{:S(2)}) collective-permute-start(bf16[384,256]{1,0:T(8,128)(2,1)S(1)} %maximum_maximum_fusion.1.refs_0_), channel_id=1, source_target_pairs={{0,32},{1,33},{2,34},{3,35},{4,36},{5,37},{6,38},{7,39},{8,40},{9,... | collective-permute-start | bytes 589832 | tf_op jit(solution)/shard_map/ppermute | solution.py:34
  31.4 8.2 %collective-permute-start.4 = (bf16[384,256]{1,0:T(8,128)(2,1)S(1)}, bf16[384,256]{1,0:T(8,128)(2,1)S(1)}, u32[]{:S(2)}, u32[]{:S(2)}) collective-permute-start(bf16[384,256]{1,0:T(8,128)(2,1)S(1)} %maximum_maximum_fusion.1.refs_0_), channel_id=1, source_target_pairs={{0,224},{1,225},{2,226},{3,227},{4,228},{5,229},{6,230},{7,231},{8... | collective-permute-start | bytes 589832 | tf_op jit(solution)/shard_map/ppermute | solution.py:34
  35.3 8.6 %collective-permute-start.1 = (bf16[256,512]{1,0:T(8,128)(2,1)S(1)}, bf16[256,512]{1,0:T(8,128)(2,1)S(1)}, u32[]{:S(2)}, u32[]{:S(2)}) collective-permute-start(bf16[256,512]{1,0:T(8,128)(2,1)S(1)} %maximum_select_fusion.1), channel_id=1, source_target_pairs={{0,16},{1,17},{2,18},{3,19},{4,20},{5,21},{6,22},{7,23},{8,24},{9,... | collective-permute-start | bytes 786440 | tf_op jit(solution)/shard_map/ppermute | solution.py:34
  38.3 5.8 %collective-permute-start.6 = (bf16[384,256]{1,0:T(8,128)(2,1)S(1)}, bf16[384,256]{1,0:T(8,128)(2,1)S(1)}, u32[]{:S(2)}, u32[]{:S(2)}) collective-permute-start(bf16[384,256]{1,0:T(8,128)(2,1)S(1)} %maximum_maximum_fusion.1.refs_0_), channel_id=1, source_target_pairs={{0,8},{1,9},{2,10},{3,11},{4,12},{5,13},{6,14},{7,15},{8,0},{9,1},... | collective-permute-start | bytes 589832 | tf_op jit(solution)/shard_map/ppermute | solution.py:34
  39.6 18.3 %collective-permute-start.9 = (bf16[768,256]{1,0:T(8,128)(2,1)S(1)}, bf16[768,256]{1,0:T(8,128)(2,1)S(1)}, u32[]{:S(2)}, u32[]{:S(2)}) collective-permute-start(bf16[768,256]{1,0:T(8,128)(2,1)S(1)} %pad_maximum_fusion), channel_id=1, source_target_pairs={{0,8},{1,9},{2,10},{3,11},{4,12},{5,13},{6,14},{7,15},{8,0},{9,1},... | collective-permute-start | bytes 1179656 | tf_op jit(solution)/shard_map/ppermute | solution.py:34
  41.2 11.5 %collective-permute-start.3 = (bf16[384,256]{1,0:T(8,128)(2,1)S(1)}, bf16[384,256]{1,0:T(8,128)(2,1)S(1)}, u32[]{:S(2)}, u32[]{:S(2)}) collective-permute-start(bf16[384,256]{1,0:T(8,128)(2,1)S(1)} %collective-permute-done.2.refs_2_), channel_id=1, source_target_pairs={{0,32},{1,33},{2,34},{3,35},{4,36},{5,37},{6,38},{7,39},{8,40},{9,... | collective-permute-start | bytes 589832 | tf_op jit(solution)/shard_map/ppermute | solution.py:34
  41.2 11.5 %collective-permute-start.5 = (bf16[384,256]{1,0:T(8,128)(2,1)S(1)}, bf16[384,256]{1,0:T(8,128)(2,1)S(1)}, u32[]{:S(2)}, u32[]{:S(2)}) collective-permute-start(bf16[384,256]{1,0:T(8,128)(2,1)S(1)} %collective-permute-done.4.refs_3_), channel_id=1, source_target_pairs={{0,224},{1,225},{2,226},{3,227},{4,228},{5,229},{6,230},{7,231},{8... | collective-permute-start | bytes 589832 | tf_op jit(solution)/shard_map/ppermute | solution.py:34
  52.6 15.5 %collective-permute-start.7 = (bf16[384,256]{1,0:T(8,128)(2,1)S(1)}, bf16[384,256]{1,0:T(8,128)(2,1)S(1)}, u32[]{:S(2)}, u32[]{:S(2)}) collective-permute-start(bf16[384,256]{1,0:T(8,128)(2,1)S(1)} %collective-permute-done.3.refs_2_), channel_id=1, source_target_pairs={{0,32},{1,33},{2,34},{3,35},{4,36},{5,37},{6,38},{7,39},{8,40},{9,... | collective-permute-start | bytes 589832 | tf_op jit(solution)/shard_map/ppermute | solution.py:34
  52.6 15.5 %collective-permute-start.8 = (bf16[384,256]{1,0:T(8,128)(2,1)S(1)}, bf16[384,256]{1,0:T(8,128)(2,1)S(1)}, u32[]{:S(2)}, u32[]{:S(2)}) collective-permute-start(bf16[384,256]{1,0:T(8,128)(2,1)S(1)} %collective-permute-done.5.refs_3_), channel_id=1, source_target_pairs={{0,224},{1,225},{2,226},{3,227},{4,228},{5,229},{6,230},{7,231},{8... | collective-permute-start | bytes 589832 | tf_op jit(solution)/shard_map/ppermute | solution.py:34
  55.3 12.9 %collective-permute-start.12 = (bf16[768,256]{1,0:T(8,128)(2,1)S(1)}, bf16[768,256]{1,0:T(8,128)(2,1)S(1)}, u32[]{:S(2)}, u32[]{:S(2)}) collective-permute-start(bf16[768,256]{1,0:T(8,128)(2,1)S(1)} %pad_maximum_fusion.2), channel_id=1, source_target_pairs={{0,8},{1,9},{2,10},{3,11},{4,12},{5,13},{6,14},{7,15},{8,0},{9,1},... | collective-permute-start | bytes 1179656 | tf_op jit(solution)/shard_map/ppermute | solution.py:34
  68.1 8.4 %collective-permute-start.11 = (bf16[384,256]{1,0:T(8,128)(2,1)S(1)}, bf16[384,256]{1,0:T(8,128)(2,1)S(1)}, u32[]{:S(2)}, u32[]{:S(2)}) collective-permute-start(bf16[384,256]{1,0:T(8,128)(2,1)S(1)} %collective-permute-done.7.refs_2_), channel_id=1, source_target_pairs={{0,32},{1,33},{2,34},{3,35},{4,36},{5,37},{6,38},{7,39},{8,40},{9,... | collective-permute-start | bytes 589832 | tf_op jit(solution)/shard_map/ppermute | solution.py:34
  68.2 10.0 %collective-permute-start.10 = (bf16[768,256]{1,0:T(8,128)(2,1)S(1)}, bf16[768,256]{1,0:T(8,128)(2,1)S(1)}, u32[]{:S(2)}, u32[]{:S(2)}) collective-permute-start(bf16[768,256]{1,0:T(8,128)(2,1)S(1)} %pad_maximum_fusion.1), channel_id=1, source_target_pairs={{0,8},{1,9},{2,10},{3,11},{4,12},{5,13},{6,14},{7,15},{8,0},{9,1},... | collective-permute-start | bytes 1179656 | tf_op jit(solution)/shard_map/ppermute | solution.py:34
  76.6 1.6 collective-permute-start.13
  106.1 8.5 %collective-permute-start.14 = (bf16[64,2048]{1,0:T(8,128)(2,1)S(1)}, bf16[64,2048]{1,0:T(8,128)(2,1)S(1)}, u32[]{:S(2)}, u32[]{:S(2)}) collective-permute-start(bf16[64,2048]{1,0:T(8,128)(2,1)S(1)} %shard_map.77.refs_0_), channel_id=1, source_target_pairs={{0,32},{1,33},{2,34},{3,35},{4,36},{5,37},{6,38},{7,39},{8,40},{9,... | collective-permute-start | bytes 786440 | tf_op jit(solution)/shard_map/ppermute | solution.py:34
  106.3 8.3 %collective-permute-start.15 = (bf16[64,2048]{1,0:T(8,128)(2,1)S(1)}, bf16[64,2048]{1,0:T(8,128)(2,1)S(1)}, u32[]{:S(2)}, u32[]{:S(2)}) collective-permute-start(bf16[64,2048]{1,0:T(8,128)(2,1)S(1)} %shard_map.77.refs_0_), channel_id=1, source_target_pairs={{0,224},{1,225},{2,226},{3,227},{4,228},{5,229},{6,230},{7,231},{8... | collective-permute-start | bytes 786440 | tf_op jit(solution)/shard_map/ppermute | solution.py:34
  114.6 6.9 %collective-permute-start.16 = (bf16[64,2048]{1,0:T(8,128)(2,1)S(1)}, bf16[64,2048]{1,0:T(8,128)(2,1)S(1)}, u32[]{:S(2)}, u32[]{:S(2)}) collective-permute-start(bf16[64,2048]{1,0:T(8,128)(2,1)S(1)} %collective-permute-done.14.refs_1_), channel_id=1, source_target_pairs={{0,32},{1,33},{2,34},{3,35},{4,36},{5,37},{6,38},{7,39},{8,40},{9,... | collective-permute-start | bytes 786440 | tf_op jit(solution)/shard_map/ppermute | solution.py:34
  114.6 6.9 %collective-permute-start.17 = (bf16[64,2048]{1,0:T(8,128)(2,1)S(1)}, bf16[64,2048]{1,0:T(8,128)(2,1)S(1)}, u32[]{:S(2)}, u32[]{:S(2)}) collective-permute-start(bf16[64,2048]{1,0:T(8,128)(2,1)S(1)} %collective-permute-done.15.refs_2_), channel_id=1, source_target_pairs={{0,224},{1,225},{2,226},{3,227},{4,228},{5,229},{6,230},{7,231},{8... | collective-permute-start | bytes 786440 | tf_op jit(solution)/shard_map/ppermute | solution.py:34
  121.5 6.4 %collective-permute-start.23 = (bf16[64,2048]{1,0:T(8,128)(2,1)S(1)}, bf16[64,2048]{1,0:T(8,128)(2,1)S(1)}, u32[]{:S(2)}, u32[]{:S(2)}) collective-permute-start(bf16[64,2048]{1,0:T(8,128)(2,1)S(1)} %collective-permute-done.16.refs_3_), channel_id=1, source_target_pairs={{0,32},{1,33},{2,34},{3,35},{4,36},{5,37},{6,38},{7,39},{8,40},{9,... | collective-permute-start | bytes 786440 | tf_op jit(solution)/shard_map/ppermute | solution.py:34
  121.5 15.2 %collective-permute-start.24 = (bf16[64,2048]{1,0:T(8,128)(2,1)S(1)}, bf16[64,2048]{1,0:T(8,128)(2,1)S(1)}, u32[]{:S(2)}, u32[]{:S(2)}) collective-permute-start(bf16[64,2048]{1,0:T(8,128)(2,1)S(1)} %collective-permute-done.17.refs_4_), channel_id=1, source_target_pairs={{0,224},{1,225},{2,226},{3,227},{4,228},{5,229},{6,230},{7,231},{8... | collective-permute-start | bytes 786440 | tf_op jit(solution)/shard_map/ppermute | solution.py:34
  127.9 8.7 %collective-permute-start.25 = (bf16[64,2048]{1,0:T(8,128)(2,1)S(1)}, bf16[64,2048]{1,0:T(8,128)(2,1)S(1)}, u32[]{:S(2)}, u32[]{:S(2)}) collective-permute-start(bf16[64,2048]{1,0:T(8,128)(2,1)S(1)} %collective-permute-done.23.refs_0_), channel_id=1, source_target_pairs={{0,32},{1,33},{2,34},{3,35},{4,36},{5,37},{6,38},{7,39},{8,40},{9,... | collective-permute-start | bytes 786440 | tf_op jit(solution)/shard_map/ppermute | solution.py:34
  132.4 10.8 %collective-permute-start.22 = (bf16[320,512]{1,0:T(8,128)(2,1)S(1)}, bf16[320,512]{1,0:T(8,128)(2,1)S(1)}, u32[]{:S(2)}, u32[]{:S(2)}) collective-permute-start(bf16[320,512]{1,0:T(8,128)(2,1)S(1)} %get-tuple-element.58), channel_id=1, source_target_pairs={{0,8},{1,9},{2,10},{3,11},{4,12},{5,13},{6,14},{7,15},{8,0},{9,1},... | collective-permute-start | bytes 983048 | tf_op jit(solution)/shard_map/ppermute | solution.py:34
  139.1 4.2 %collective-permute-start.26 = (bf16[192,512]{1,0:T(8,128)(2,1)S(1)}, bf16[192,512]{1,0:T(8,128)(2,1)S(1)}, u32[]{:S(2)}, u32[]{:S(2)}) collective-permute-start(bf16[192,512]{1,0:T(8,128)(2,1)S(1)} %get-tuple-element.60), channel_id=1, source_target_pairs={{0,8},{1,9},{2,10},{3,11},{4,12},{5,13},{6,14},{7,15},{8,0},{9,1},... | collective-permute-start | bytes 589832 | tf_op jit(solution)/shard_map/ppermute | solution.py:34
  (6 other events, 25.6 us)
Sparse Core Ops, SparseCore 0:
  31.3 51.9 all-gather.1

commit v3 on v2

v3 whole, which is shorter than its diff:
```python
import functools
import math

import jax
import jax.numpy as jnp
from jax import lax
from jax.experimental import pallas as pl
from jax.experimental.pallas import tpu as pltpu
from jax.sharding import Mesh
from jax.sharding import PartitionSpec as P

HEAD = 128
NZ, NY, NC, NX, NL = 8, 2, 2, 4, 2
NEG = -1e30
VMEM = 16 * 1024 * 1024
AXES = ("z", "yh", "core", "x", "yl")
TILE = 256
TAIL = 16
F32 = jnp.float32
BF16 = jnp.bfloat16


def permute(value, move):
    pairs = []
    for z in range(NZ):
        for yh in range(NY):
            for c in range(NC):
                for x in range(NX):
                    for yl in range(NL):
                        z2, yh2, c2, x2, yl2 = move(z, yh, c, x, yl)
                        source = ((z * NY + yh) * NC + c) * NX * NL + x * NL + yl
                        target = (((z2 % NZ) * NY + yh2) * NC + c2) * NX * NL + (x2 % NX) * NL + yl2
                        pairs.append((source, target))
    return lax.ppermute(value, AXES, pairs)


def meet_up(value):
    return permute(value, lambda z, yh, c, x, yl: (z + 1 - 2 * (z % 2), yh, c, x, yl))


def meet_down(value):
    return permute(value, lambda z, yh, c, x, yl: (z - 1 + 2 * (z % 2), yh, c, x, yl))


def shifted(z, shift):
    return lax.rem(z + shift * (1 - 2 * lax.rem(z, 2)) + NZ, NZ)


def swap(value, a=0, b=0, d=0):
    return permute(value, lambda z, yh, c, x, yl: (z, yh ^ a, c ^ b, x, yl ^ d))


def attend_kernel(sources, heads, which, last, cache, fresh, meta, lens, q_ref, *refs):
    count = len(sources)
    kv_refs, refs = refs[:count], refs[count:]
    rows = q_ref.shape[0]
    group = rows // (NX * NL)
    z, yh, core = meta[0], meta[1], meta[2]
    factor = math.log2(math.e) / math.sqrt(HEAD)

    def head(h, base, before):
        first = before is None
        lanes = pl.ds(pl.multiple_of(h * HEAD, HEAD), HEAD)
        q_lanes = pl.ds(pl.multiple_of((base + h) * HEAD, HEAD), HEAD)

        def score(start):
            q = q_ref[start : start + TILE, q_lanes]
            parts, top = [], None
            for kv, (at, shift, other) in zip(kv_refs, sources):
                span = slice(at * (cache + fresh), (at + 1) * (cache + fresh))
                zs = shifted(z, shift)
                mine = yh * NC + (1 - core if other else core)
                s = lax.dot_general(
                    q, kv[span, :HEAD], (((1,), (1,)), ((), ())), preferred_element_type=F32
                )
                col = lax.broadcasted_iota(jnp.int32, (1, cache), 1)
                stored = s[:, :cache] + jnp.where(col < lens[zs * NY * NC + mine], 0.0, NEG)
                if shift == 0:
                    row = start + lax.broadcasted_iota(jnp.int32, (TILE, fresh), 0)
                    col = mine * fresh + lax.broadcasted_iota(jnp.int32, (TILE, fresh), 1)
                    new = jnp.where(col <= row, s[:, cache:], NEG)
                else:
                    new = s[:, cache:] + jnp.where(zs < z, 0.0, NEG)
                s = jnp.concatenate([stored, new], 1)
                parts.append(s)
                for lane in range(0, cache + fresh, HEAD):
                    piece = s[:, lane : lane + HEAD]
                    top = piece if top is None else jnp.maximum(top, piece)
            return parts, top

        def absorb(start, parts, top):
            here = slice(start, start + TILE)
            m = top.max(axis=1, keepdims=True)
            if first:
                l, acc = None, None
            else:
                acc_in, top_in, sum_in = before
                old = top_in[here, lanes]
                m = jnp.maximum(m, old)
                alpha = jnp.exp2((old - m) * factor)
                m = m[:, 0:1]
                l = sum_in[here, lanes] * alpha
                acc = acc_in[here, lanes] * alpha
            for kv, (at, _, _), s in zip(kv_refs, sources, parts):
                span = slice(at * (cache + fresh), (at + 1) * (cache + fresh))
                p = jnp.exp2((s - m) * factor)
                for lane in range(0, cache + fresh, HEAD):
                    piece = p[:, lane : lane + HEAD]
                    l = piece if l is None else l + piece
                term = jnp.dot(p.astype(BF16), kv[span, HEAD:], preferred_element_type=F32)
                acc = term if acc is None else acc + term
            if not last:
                acc_out, top_out, sum_out = refs[:3]
                acc_out[here, lanes] = acc
                top_out[here, lanes] = jnp.broadcast_to(m, (TILE, HEAD))
                sum_out[here, lanes] = l
                return
            out_ref = refs[-1]
            half = base // heads
            l = l.sum(axis=1, keepdims=True)
            out = (acc / l).astype(BF16)
            lse = m * factor + jnp.log2(l)
            for at in range(0, TILE, group):
                out_ref[half, (start + at) // group, 0:group, lanes] = out[at : at + group, :]
            for at in range(0, TILE, 2 * group):
                line = jnp.broadcast_to(lse[at : at + 2 * group, :], (2 * group, HEAD)).T[0:1, :]
                high = line.astype(BF16).astype(F32)
                middle = (line - high).astype(BF16).astype(F32)
                low = line - high - middle
                kind = lax.broadcasted_iota(jnp.int32, (TAIL, HEAD), 0)
                tail = jnp.where(kind == 0, high, jnp.where(kind == 1, middle, low)).astype(BF16)
                for odd in range(2):
                    out_ref[half, (start + at) // group + odd, group : group + TAIL, lanes] = tail

        starts = list(range(0, rows, TILE))
        now = score(starts[0])
        for at, start in enumerate(starts):
            later = score(starts[at + 1]) if at + 1 < len(starts) else None
            absorb(start, *now)
            now = later
        return 0

    if last:
        for half in range(NY):
            lax.fori_loop(0, heads, lambda h, _: head(h, half * heads, refs[3 * half : 3 * half + 3]), 0)
    else:
        lax.fori_loop(0, heads, lambda h, _: head(h, which * heads, None), 0)


def attend(meta, lens, q, kvs, which, state, cache, fresh):
    rows, width = q.shape
    last = state is not None
    heads = width // HEAD // NY
    span = cache + fresh
    args = [meta, lens, q] + [entry[0] for entry in kvs]
    if last:
        args += [array for half in state for array in half]
        group = rows // (NX * NL)
        out_shape = jax.ShapeDtypeStruct((NY, NX * NL, group + TAIL, heads * HEAD), BF16)
    else:
        out_shape = [jax.ShapeDtypeStruct((rows, heads * HEAD), F32)] * 3
    whole = pl.BlockSpec(memory_space=pltpu.VMEM)
    scalar = pl.BlockSpec(memory_space=pltpu.SMEM)
    out = pl.pallas_call(
        functools.partial(
            attend_kernel, tuple(entry[1:] for entry in kvs), heads, which, last, cache, fresh
        ),
        in_specs=[scalar, scalar] + [whole] * (len(args) - 2),
        out_specs=whole if last else [whole] * 3,
        out_shape=out_shape,
        compiler_params=pltpu.CompilerParams(vmem_limit_bytes=VMEM),
        cost_estimate=pl.CostEstimate(
            flops=4 * rows * heads * HEAD * span * len(kvs) * (2 if last else 1),
            bytes_accessed=4 * rows * width,
            transcendentals=rows * heads * span * len(kvs),
        ),
    )(*args)
    return out if last else tuple(out)


def combine_kernel(group, meta, pieces, out):
    yl = meta[4]

    def one(t, _):
        spot = t // NL * NL + lax.rem(t + yl, NL)
        for at in range(0, pieces.shape[2], HEAD):
            values, weights = [], []
            for half in range(NY):
                tail = pieces[half * NX * NL + t, group:, at : at + HEAD].astype(F32)
                line = tail[0:1, :] + tail[1:2, :] + tail[2:3, :]
                wide = jnp.broadcast_to(line, (HEAD, HEAD)).T
                weights.append(jnp.where(yl == 0, wide[:group, :], wide[group : 2 * group, :]))
                values.append(pieces[half * NX * NL + t, 0:group, at : at + HEAD].astype(F32))
            top = jnp.maximum(weights[0], weights[1])
            a, b = jnp.exp2(weights[0] - top), jnp.exp2(weights[1] - top)
            joined = (values[0] * a + values[1] * b) / (a + b)
            out[:, pl.ds(pl.multiple_of(spot * pieces.shape[2] + at, HEAD), HEAD)] = joined.astype(BF16)
        return 0

    lax.fori_loop(0, NX * NL, one, 0, unroll=True)


def combine(meta, pieces):
    group, width = pieces.shape[1] - TAIL, pieces.shape[2]
    return pl.pallas_call(
        functools.partial(combine_kernel, group),
        in_specs=[pl.BlockSpec(memory_space=pltpu.SMEM), pl.BlockSpec(memory_space=pltpu.VMEM)],
        out_specs=pl.BlockSpec(memory_space=pltpu.VMEM),
        out_shape=jax.ShapeDtypeStruct((group, NX * NL * width), BF16),
        compiler_params=pltpu.CompilerParams(vmem_limit_bytes=VMEM),
    )(meta, pieces)


def project_kernel(*refs):
    blocks, weight, (keep, send) = refs[:-3], refs[-3], refs[-2:]
    total = jnp.dot(
        jnp.concatenate([block[...] for block in blocks], 0), weight[...], preferred_element_type=F32
    )

    @pl.when(pl.program_id(0) < 2)
    def _():
        keep[...] = total

    @pl.when(pl.program_id(0) >= 2)
    def _():
        send[...] = total.astype(BF16)


def project(blocks, weight):
    rows = blocks[0].shape[0] * len(blocks)
    depth, width = weight.shape
    tile = width // 4
    place = lambda j: 2 * (j % 2) + j // 2
    whole = pl.BlockSpec(blocks[0].shape, lambda j: (0, 0))
    return pl.pallas_call(
        project_kernel,
        grid=(4,),
        in_specs=[whole] * len(blocks) + [pl.BlockSpec((depth, tile), lambda j: (0, place(j)))],
        out_specs=[
            pl.BlockSpec((rows, tile), lambda j: (0, jnp.minimum(j, 1))),
            pl.BlockSpec((rows, tile), lambda j: (0, jnp.maximum(j - 2, 0))),
        ],
        out_shape=[
            jax.ShapeDtypeStruct((rows, width // 2), F32),
            jax.ShapeDtypeStruct((rows, width // 2), BF16),
        ],
        compiler_params=pltpu.CompilerParams(vmem_limit_bytes=VMEM),
        cost_estimate=pl.CostEstimate(
            flops=2 * rows * depth * width, bytes_accessed=2 * depth * width, transcendentals=0
        ),
    )(*blocks, weight)


def settle_kernel(order, meta, *refs):
    out = refs[-1]
    width = out.shape[3]
    z, yh = meta[0], meta[1]
    for part, shifts in enumerate(order):
        kept, near = refs[2 * part : 2 * part + 2]
        group = kept.shape[0] // len(shifts)
        for at, shift in enumerate(shifts):
            zs = shifted(z, shift)
            here = pl.ds(at * group, group)
            total = (kept[here, :] + near[here, :].astype(F32)).astype(BF16)
            for half in range(NY):
                out[lax.rem(yh + half, NY), zs] = total[:, half * width : (half + 1) * width]


def settle(meta, order, parts):
    rows = sum(part[0].shape[0] for part in parts)
    width = parts[0][0].shape[1] // NY
    flat = [array for part in parts for array in part]
    return pl.pallas_call(
        functools.partial(settle_kernel, order),
        in_specs=[pl.BlockSpec(memory_space=pltpu.SMEM)] + [pl.BlockSpec(memory_space=pltpu.VMEM)] * len(flat),
        out_specs=pl.BlockSpec(memory_space=pltpu.VMEM),
        out_shape=jax.ShapeDtypeStruct((NY, NZ, rows // NZ, width), BF16),
        compiler_params=pltpu.CompilerParams(vmem_limit_bytes=VMEM),
    )(meta, *flat)


def shards(queries, stored_keys, stored_values, fresh_keys, fresh_values, cache_lengths, out_weight):
    cache, fresh = stored_keys.shape[0], fresh_keys.shape[0]
    z, yh, core, x, yl = [lax.axis_index(name) for name in AXES]
    meta = jnp.stack([z, yh, core, x, yl]).astype(jnp.int32)

    kv = jnp.concatenate(
        [
            jnp.concatenate([stored_keys, stored_values], 1),
            jnp.concatenate([fresh_keys, fresh_values], 1),
        ],
        0,
    )
    ahead, behind = meet_up(kv), meet_down(kv)
    twin_kv = swap(kv, b=1)

    depth = out_weight.shape[0] // 4
    block = lambda value, at, rows: lax.dynamic_slice_in_dim(value, at * rows, rows, 0)
    wide = jnp.concatenate(
        [block(out_weight, core, 2 * depth), swap(block(out_weight, 1 - core, 2 * depth), b=1)], 1
    )
    keep, give = block(wide, yh, depth), block(wide, 1 - yh, depth)
    wide = jnp.concatenate(
        [
            jnp.concatenate([keep, swap(give, a=1)], 1),
            jnp.concatenate([swap(keep, d=1), swap(give, a=1, d=1)], 1),
        ],
        0,
    )

    half = queries.shape[1] // 2
    mine = lax.dynamic_slice_in_dim(queries, core * half, half, 1)
    theirs = swap(lax.dynamic_slice_in_dim(queries, (1 - core) * half, half, 1), b=1)
    near = jnp.concatenate([jnp.where(core == 0, mine, theirs), jnp.where(core == 0, theirs, mine)], 0)
    wide, near, ahead, behind = lax.optimization_barrier((wide, near, ahead, behind))
    weight = lax.all_gather(wide, "x", axis=0, tiled=True)
    far = swap(near, a=1)
    q = jnp.concatenate([jnp.where(yh == 0, near, far), jnp.where(yh == 0, far, near)], 0)

    def both(ahead, behind, step):
        near = [(ahead, 0, step, 0), (behind, 0, -step, 0)]
        return near + [(swap(array, b=1), at, shift, 1) for array, at, shift, _ in near]

    blocks = [(kv, 0, 0, 0), (twin_kv, 0, 0, 1)] + both(ahead, behind, 1)
    ahead, behind = meet_up(behind), meet_down(ahead)
    blocks += both(ahead, behind, 2)
    ahead, behind = meet_up(behind), meet_down(ahead)
    low = attend(meta, cache_lengths, q, blocks, 0, None, cache, fresh)
    ahead, behind, low = lax.optimization_barrier((ahead, behind, low))
    last_blocks = both(ahead, behind, 3)
    ahead = meet_up(behind)
    high = attend(meta, cache_lengths, q, blocks, 1, None, cache, fresh)
    ahead, high = lax.optimization_barrier((ahead, high))
    last_blocks += [(ahead, 0, 4, 0), (swap(ahead, b=1), 0, 4, 1)]
    pieces = attend(meta, cache_lengths, q, last_blocks, None, (low, high), cache, fresh)

    group, width = pieces.shape[2], pieces.shape[3]
    pieces = lax.all_to_all(
        pieces.reshape(NY * NZ, group, width), ("yh", "x", "yl"), split_axis=0, concat_axis=0, tiled=True
    )
    a = combine(meta, pieces)
    ahead, behind = [a], [a]
    for _ in range(3):
        up, down = meet_up(behind[-1]), meet_down(ahead[-1])
        ahead.append(up)
        behind.append(down)
    ahead.append(meet_up(behind[-1]))

    def share(blocks):
        kept, sent = project(blocks, weight)
        return kept, swap(sent, b=1)

    order = ((0, 1, -1, 2, -2), (3, -3, 4))
    first = share([a, ahead[1], behind[1], ahead[2], behind[2]])
    second = share([ahead[3], behind[3], ahead[4]])
    settled = settle(meta, order, (first, second))
    rows, width = settled.shape[2:]
    home = lax.all_to_all(
        settled.reshape(NY * NZ, rows, width), ("yh", "x", "yl"), split_axis=0, concat_axis=0, tiled=True
    ).reshape(NY, NZ * rows, width)
    return (home[0].astype(F32) + home[1].astype(F32)).astype(BF16)


def solution(mesh):
    split = Mesh(mesh.devices.reshape(NZ, NY, NC, NX, NL), AXES)
    ctx, tp = ("z", "yh", "core"), ("x", "yl")
    spec = P(ctx, tp)
    return jax.shard_map(
        shards,
        mesh=split,
        in_specs=(spec, spec, spec, spec, spec, P(), P(tp, ctx)),
        out_specs=P(tp, ctx),
        check_vma=False,
    )
```

time: 166 us -> 151 us (0.910)
  Pallas kernels: 40 us -> 29.4 us
  starting transfers between devices: 41.5 us -> 37.9 us
  local copies, waits for them, and re-layouts: 6.01 us -> 4.3 us
    pallas_call x4 -> x3, Pallas kernels: 31.3 us -> 22.4 us  [attend(): pl.pallas_call(functools.partial(attend_kernel, tuple((entry[1:] for entr...]
    ppermute x27 -> x30, starting transfers between devices: 41.5 us -> 37.9 us  [permute(): return lax.ppermute(value, AXES, pairs)]
    unnamed x20 -> x8, local copies, waits for them, and re-layouts: 3.87 us -> 2.2 us
    ppermute x27 -> x30, waiting for transfers between devices: 29.6 us -> 30.2 us  [permute(): return lax.ppermute(value, AXES, pairs)]
  transfers between devices with their start and end apart: 28 -> 31, of which waited for: 11 -> 10; matrix products, arithmetic and copies ran while one was open for 0% -> 2% of each run, Pallas kernels for 24% -> 19%
where the time goes in v3:
time: 151 us
  starting transfers between devices  37.9 us (25%)
  blocking collectives  32.1 us (21%)
  waiting for transfers between devices  30.3 us (20%)
  Pallas kernels  29.4 us (19%)
  between operations  13.6 us (9%)
  local copies, waits for them, and re-layouts  4.3 us (3%)
  other arithmetic  3.03 us (2%)
    ppermute x30, starting transfers between devices, permute(): return lax.ppermute(value, AXES, pairs)  37.9 us
    ppermute x30, waiting for transfers between devices, permute(): return lax.ppermute(value, AXES, pairs)  30.2 us
    pallas_call x3, Pallas kernels, attend(): pl.pallas_call(functools.partial(attend_kernel, tuple((entry[1:] for entr...  22.4 us
    all_to_all x1, blocking collectives, shards(): lax.all_to_all(pieces.reshape(NY * NZ, group, width), ('yh', 'x', 'yl'),...  17.7 us
    all_to_all x1, blocking collectives, shards(): lax.all_to_all(settled.reshape(NY * NZ, rows, width), ('yh', 'x', 'yl'),...  14.3 us
    pallas_call x2, Pallas kernels, project(): pl.pallas_call(project_kernel, grid=(4,), in_specs=[whole] * len(blocks)...  5.28 us
  transfers between devices with their start and end apart: 31, of which 10 were waited for; matrix products, arithmetic and copies ran while one was open for 2% of the time, Pallas kernels for 19%

profile of v3, /device:TPU:1, one launch (start us, length us, event | category | flops | bytes accessed | tf_op | source)
XLA Modules:
  0.0 150.6 jit_solution(3956538928561479154)
XLA Ops:
  6.5 1.1 constant_dynamic-slice_fusion.1
  7.6 3.3 %collective-permute-start = (bf16[512,256]{1,0:T(8,128)(2,1)S(1)}, bf16[512,256]{1,0:T(8,128)(2,1)S(1)}, u32[]{:S(2)}, u32[]{:S(2)}) collective-permute-start(bf16[512,256]{1,0:T(8,128)(2,1)S(1)} %get-tuple-element.55), channel_id=1, source_target_pairs={{0,8},{1,9},{2,10},{3,11},{4,12},{5,13},{6,14},{7,15},{8,0},{9,1},... | collective-permute-start | bytes 786440 | tf_op jit(solution)/shard_map/ppermute | solution.py:34
  13.0 4.6 %collective-permute-start.6 = (bf16[384,256]{1,0:T(8,128)(2,1)S(1)}, bf16[384,256]{1,0:T(8,128)(2,1)S(1)}, u32[]{:S(2)}, u32[]{:S(2)}) collective-permute-start(bf16[384,256]{1,0:T(8,128)(2,1)S(1)} %maximum_maximum_fusion.1.refs_0_), channel_id=1, source_target_pairs={{0,224},{1,225},{2,226},{3,227},{4,228},{5,229},{6,230},{7,231},{8... | collective-permute-start | bytes 589832 | tf_op jit(solution)/shard_map/ppermute | solution.py:34
  17.6 3.0 %collective-permute-start.1 = (bf16[256,512]{1,0:T(8,128)(2,1)S(1)}, bf16[256,512]{1,0:T(8,128)(2,1)S(1)}, u32[]{:S(2)}, u32[]{:S(2)}) collective-permute-start(bf16[256,512]{1,0:T(8,128)(2,1)S(1)} %get-tuple-element.54), channel_id=1, source_target_pairs={{0,16},{1,17},{2,18},{3,19},{4,20},{5,21},{6,22},{7,23},{8,24},{9,... | collective-permute-start | bytes 786440 | tf_op jit(solution)/shard_map/ppermute | solution.py:34
  21.5 4.5 %collective-permute-done.1 = bf16[256,512]{1,0:T(8,128)(2,1)S(1)} collective-permute-done((bf16[256,512]{1,0:T(8,128)(2,1)S(1)}, bf16[256,512]{1,0:T(8,128)(2,1)S(1)}, u32[]{:S(2)}, u32[]{:S(2)}) %collective-permute-start.1) | collective-permute-done | bytes 262176 | tf_op jit(solution)/shard_map/ppermute | solution.py:34
  26.0 6.0 %collective-permute-done.2 = bf16[256,512]{1,0:T(8,128)(2,1)S(1)} collective-permute-done((bf16[256,512]{1,0:T(8,128)(2,1)S(1)}, bf16[256,512]{1,0:T(8,128)(2,1)S(1)}, u32[]{:S(2)}, u32[]{:S(2)}) %collective-permute-start.2) | collective-permute-done | bytes 262176 | tf_op jit(solution)/shard_map/ppermute | solution.py:34
  33.0 1.1 maximum_maximum_fusion
  34.2 1.5 collective-permute-start.7
  35.6 1.5 collective-permute-start.8
  37.1 2.2 %collective-permute-start.12 = (bf16[384,256]{1,0:T(8,128)(2,1)S(1)}, bf16[384,256]{1,0:T(8,128)(2,1)S(1)}, u32[]{:S(2)}, u32[]{:S(2)}) collective-permute-start(bf16[384,256]{1,0:T(8,128)(2,1)S(1)} %maximum_maximum_fusion.1.refs_0_), channel_id=1, source_target_pairs={{0,8},{1,9},{2,10},{3,11},{4,12},{5,13},{6,14},{7,15},{8,0},{9,1},... | collective-permute-start | bytes 589832 | tf_op jit(solution)/shard_map/ppermute | solution.py:34
  40.4 2.5 %collective-permute-start.14 = (bf16[384,256]{1,0:T(8,128)(2,1)S(1)}, bf16[384,256]{1,0:T(8,128)(2,1)S(1)}, u32[]{:S(2)}, u32[]{:S(2)}) collective-permute-start(bf16[384,256]{1,0:T(8,128)(2,1)S(1)} %collective-permute-done.6.refs_3_), channel_id=1, source_target_pairs={{0,8},{1,9},{2,10},{3,11},{4,12},{5,13},{6,14},{7,15},{8,0},{9,1},... | collective-permute-start | bytes 589832 | tf_op jit(solution)/shard_map/ppermute | solution.py:34
  42.9 1.2 collective-permute-start.15
  44.5 1.5 collective-permute-start.11
  46.1 6.4 %shard_map.73 = (f32[512,256]{1,0:T(8,128)S(1)}, f32[512,256]{1,0:T(8,128)S(1)}, f32[512,256]{1,0:T(8,128)S(1)}) custom-call(s32[5]{0:T(128)S(1)} %stack.23.meta, s32[32]{0:T(128)S(1)} %copy-done.2, bf16[512,512]{1,0:T(8,128)(2,1)S(1)} %pad_maximum_fusion.q_ref, bf16[384,256]{1,0:T(8,128)(2,1)S(1)} %maximum_maximum_fusion.1.refs_0_, ...), custom_call_target="tpu_custom_call" | custom-call | flops 2013265920 | bytes 1048576 | tf_op jit(solution)/shard_map/pallas_call | solution.py:164
  52.6 1.6 %collective-permute-start.19 = (bf16[384,256]{1,0:T(8,128)(2,1)S(1)}, bf16[384,256]{1,0:T(8,128)(2,1)S(1)}, u32[]{:S(2)}, u32[]{:S(2)}) collective-permute-start(bf16[384,256]{1,0:T(8,128)(2,1)S(1)} %collective-permute-done.11.refs_1_), channel_id=1, source_target_pairs={{0,32},{1,33},{2,34},{3,35},{4,36},{5,37},{6,38},{7,39},{8,40},{9,... | collective-permute-start | bytes 589832 | tf_op jit(solution)/shard_map/ppermute | solution.py:34
  54.1 1.3 collective-permute-start.18
  55.5 6.5 %shard_map.74 = (f32[512,256]{1,0:T(8,128)S(1)}, f32[512,256]{1,0:T(8,128)S(1)}, f32[512,256]{1,0:T(8,128)S(1)}) custom-call(s32[5]{0:T(128)S(1)} %stack.23.meta, s32[32]{0:T(128)S(1)} %copy-done.2, bf16[512,512]{1,0:T(8,128)(2,1)S(1)} %pad_maximum_fusion.q_ref, bf16[384,256]{1,0:T(8,128)(2,1)S(1)} %maximum_maximum_fusion.1.refs_0_, ...), custom_call_target="tpu_custom_call" | custom-call | flops 2013265920 | bytes 1048576 | tf_op jit(solution)/shard_map/pallas_call | solution.py:164
  63.7 9.4 %shard_map.75 = bf16[2,8,80,256]{3,2,1,0:T(8,128)(2,1)S(1)} custom-call(s32[5]{0:T(128)S(1)} %stack.23.meta, s32[32]{0:T(128)S(1)} %copy-done.2, bf16[512,512]{1,0:T(8,128)(2,1)S(1)} %pad_maximum_fusion.q_ref, bf16[384,256]{1,0:T(8,128)(2,1)S(1)} %collective-permute-done.9.refs_0_, bf16[384,256]{1,0:T(8,128)(2,1)S(1)} %collective-permute-done.11.refs_1_, ...), custom_call_target="tpu_custom_call" | custom-call | flops 2415919104 | bytes 1048576 | tf_op jit(solution)/shard_map/pallas_call | solution.py:164
  73.1 17.7 %all_to_all.10.pieces = bf16[16,80,256]{2,1,0:T(8,128)(2,1)S(1)} all-to-all(bf16[16,80,256]{2,1,0:T(8,128)(2,1)S(1)} %bitcast.9), channel_id=1, replica_groups=mesh['z'=8,'yh'=2,'core'=2,'x'=4,'yl'=2] {'yh','x','yl'}, dimensions={0} | all-to-all | bytes 1310720 | tf_op jit(solution)/shard_map/all_to_all | solution.py:338
  90.8 1.2 shard_map.76.refs_0_
  92.0 3.6 %collective-permute-start.22 = (bf16[64,2048]{1,0:T(8,128)(2,1)S(1)}, bf16[64,2048]{1,0:T(8,128)(2,1)S(1)}, u32[]{:S(2)}, u32[]{:S(2)}) collective-permute-start(bf16[64,2048]{1,0:T(8,128)(2,1)S(1)} %shard_map.76.refs_0_), channel_id=1, source_target_pairs={{0,224},{1,225},{2,226},{3,227},{4,228},{5,229},{6,230},{7,231},{8... | collective-permute-start | bytes 786440 | tf_op jit(solution)/shard_map/ppermute | solution.py:34
  95.6 5.4 %collective-permute-done.22.refs_2_ = bf16[64,2048]{1,0:T(8,128)(2,1)S(1)} collective-permute-done((bf16[64,2048]{1,0:T(8,128)(2,1)S(1)}, bf16[64,2048]{1,0:T(8,128)(2,1)S(1)}, u32[]{:S(2)}, u32[]{:S(2)}) %collective-permute-start.22) | collective-permute-done | bytes 262176 | tf_op jit(solution)/shard_map/ppermute | solution.py:34
  102.0 1.5 collective-permute-start.24
  103.5 3.9 %collective-permute-done.23.refs_3_ = bf16[64,2048]{1,0:T(8,128)(2,1)S(1)} collective-permute-done((bf16[64,2048]{1,0:T(8,128)(2,1)S(1)}, bf16[64,2048]{1,0:T(8,128)(2,1)S(1)}, u32[]{:S(2)}, u32[]{:S(2)}) %collective-permute-start.23) | collective-permute-done | bytes 262176 | tf_op jit(solution)/shard_map/ppermute | solution.py:34
  107.4 1.9 %collective-permute-start.27 = (bf16[64,2048]{1,0:T(8,128)(2,1)S(1)}, bf16[64,2048]{1,0:T(8,128)(2,1)S(1)}, u32[]{:S(2)}, u32[]{:S(2)}) collective-permute-start(bf16[64,2048]{1,0:T(8,128)(2,1)S(1)} %collective-permute-done.23.refs_3_), channel_id=1, source_target_pairs={{0,224},{1,225},{2,226},{3,227},{4,228},{5,229},{6,230},{7,231},{8... | collective-permute-start | bytes 786440 | tf_op jit(solution)/shard_map/ppermute | solution.py:34
  109.2 5.3 %collective-permute-done.27.refs_1_ = bf16[64,2048]{1,0:T(8,128)(2,1)S(1)} collective-permute-done((bf16[64,2048]{1,0:T(8,128)(2,1)S(1)}, bf16[64,2048]{1,0:T(8,128)(2,1)S(1)}, u32[]{:S(2)}, u32[]{:S(2)}) %collective-permute-start.27) | collective-permute-done | bytes 262176 | tf_op jit(solution)/shard_map/ppermute | solution.py:34
  114.7 2.2 %copy-done = bf16[2048,1024]{1,0:T(8,128)(2,1)S(1)} copy-done((bf16[2048,1024]{1,0:T(8,128)(2,1)S(1)}, bf16[2048,1024]{1,0:T(8,128)(2,1)}, u32[]{:S(2)}) %copy-start) | copy-done | bytes 4194328
  116.9 2.9 %shard_map.77 = (f32[320,512]{1,0:T(8,128)S(1)}, bf16[320,512]{1,0:T(8,128)(2,1)S(1)}) custom-call(bf16[64,2048]{1,0:T(8,128)(2,1)S(1)} %shard_map.76.refs_0_, bf16[64,2048]{1,0:T(8,128)(2,1)S(1)} %collective-permute-done.21.refs_1_, bf16[64,2048]{1,0:T(8,128)(2,1)S(1)} %collective-permute-done.22.refs_2_, ...), custom_call_target="tpu_custom_call" | custom-call | flops 1342177280 | bytes 4194304 | tf_op jit(solution)/shard_map/pallas_call | solution.py:235
  119.8 3.0 %collective-permute-start.25 = (bf16[320,512]{1,0:T(8,128)(2,1)S(1)}, bf16[320,512]{1,0:T(8,128)(2,1)S(1)}, u32[]{:S(2)}, u32[]{:S(2)}) collective-permute-start(bf16[320,512]{1,0:T(8,128)(2,1)S(1)} %get-tuple-element.48), channel_id=1, source_target_pairs={{0,8},{1,9},{2,10},{3,11},{4,12},{5,13},{6,14},{7,15},{8,0},{9,1},... | collective-permute-start | bytes 983048 | tf_op jit(solution)/shard_map/ppermute | solution.py:34
  122.9 2.4 %shard_map.78 = (f32[192,512]{1,0:T(8,128)S(1)}, bf16[192,512]{1,0:T(8,128)(2,1)S(1)}) custom-call(bf16[64,2048]{1,0:T(8,128)(2,1)S(1)} %collective-permute-done.26.refs_0_, bf16[64,2048]{1,0:T(8,128)(2,1)S(1)} %collective-permute-done.27.refs_1_, bf16[64,2048]{1,0:T(8,128)(2,1)S(1)} %collective-permute-done.28.refs_2_, bf16[2048,1024]{1,0:T(8,128)(2,1)S(1)} %copy-done.1), custom_call_target="tpu_custom_call" | custom-call | flops 805306368 | bytes 4194304 | tf_op jit(solution)/shard_map/pallas_call | solution.py:235
  125.3 1.7 %collective-permute-start.29 = (bf16[192,512]{1,0:T(8,128)(2,1)S(1)}, bf16[192,512]{1,0:T(8,128)(2,1)S(1)}, u32[]{:S(2)}, u32[]{:S(2)}) collective-permute-start(bf16[192,512]{1,0:T(8,128)(2,1)S(1)} %get-tuple-element.50), channel_id=1, source_target_pairs={{0,8},{1,9},{2,10},{3,11},{4,12},{5,13},{6,14},{7,15},{8,0},{9,1},... | collective-permute-start | bytes 589832 | tf_op jit(solution)/shard_map/ppermute | solution.py:34
  128.6 14.3 %all_to_all.11 = bf16[16,64,256]{2,1,0:T(8,128)(2,1)S(1)} all-to-all(bf16[16,64,256]{2,1,0:T(8,128)(2,1)S(1)} %bitcast.8), channel_id=1, replica_groups=mesh['z'=8,'yh'=2,'core'=2,'x'=4,'yl'=2] {'yh','x','yl'}, dimensions={0} | all-to-all | bytes 1048576 | tf_op jit(solution)/shard_map/all_to_all | solution.py:358
  (59 shorter events, 10.9 us)
Async XLA Ops:
  6.5 14.9 %copy-start.3 = (bf16[128,1024]{1,0:T(8,128)(2,1)S(1)}, bf16[128,1024]{1,0:T(8,128)(2,1)}, u32[]{:S(2)}) copy-start(bf16[128,1024]{1,0:T(8,128)(2,1)} %param.7) | copy-start | bytes 786436
  6.5 108.2 %all-gather.2.cloned.1.call-start = ((), (), s32[]{:S(2)}) async-start(), calls=%async_computation.2 | async-start | bytes 5242880 | tf_op jit(solution)/shard_map/all_gather | solution.py:316
  7.6 9.9 %collective-permute-start = (bf16[512,256]{1,0:T(8,128)(2,1)S(1)}, bf16[512,256]{1,0:T(8,128)(2,1)S(1)}, u32[]{:S(2)}, u32[]{:S(2)}) collective-permute-start(bf16[512,256]{1,0:T(8,128)(2,1)S(1)} %get-tuple-element.55), channel_id=1, source_target_pairs={{0,8},{1,9},{2,10},{3,11},{4,12},{5,13},{6,14},{7,15},{8,0},{9,1},... | collective-permute-start | bytes 786440 | tf_op jit(solution)/shard_map/ppermute | solution.py:34
  11.9 9.5 %collective-permute-start.4 = (bf16[128,512]{1,0:T(8,128)(2,1)S(1)}, bf16[128,512]{1,0:T(8,128)(2,1)S(1)}, u32[]{:S(2)}, u32[]{:S(2)}) collective-permute-start(bf16[128,512]{1,0:T(8,128)(2,1)S(1)} %constant_dynamic-slice_fusion), channel_id=1, source_target_pairs={{0,8},{1,9},{2,10},{3,11},{4,12},{5,13},{6,14},{7,15},{8,0},{9,1},... | collective-permute-start | bytes 393224 | tf_op jit(solution)/shard_map/ppermute | solution.py:34
  12.9 21.2 %collective-permute-start.5 = (bf16[384,256]{1,0:T(8,128)(2,1)S(1)}, bf16[384,256]{1,0:T(8,128)(2,1)S(1)}, u32[]{:S(2)}, u32[]{:S(2)}) collective-permute-start(bf16[384,256]{1,0:T(8,128)(2,1)S(1)} %maximum_maximum_fusion.1.refs_0_), channel_id=1, source_target_pairs={{0,32},{1,33},{2,34},{3,35},{4,36},{5,37},{6,38},{7,39},{8,40},{9,... | collective-permute-start | bytes 589832 | tf_op jit(solution)/shard_map/ppermute | solution.py:34
  13.0 21.1 %collective-permute-start.6 = (bf16[384,256]{1,0:T(8,128)(2,1)S(1)}, bf16[384,256]{1,0:T(8,128)(2,1)S(1)}, u32[]{:S(2)}, u32[]{:S(2)}) collective-permute-start(bf16[384,256]{1,0:T(8,128)(2,1)S(1)} %maximum_maximum_fusion.1.refs_0_), channel_id=1, source_target_pairs={{0,224},{1,225},{2,226},{3,227},{4,228},{5,229},{6,230},{7,231},{8... | collective-permute-start | bytes 589832 | tf_op jit(solution)/shard_map/ppermute | solution.py:34
  17.6 8.3 %collective-permute-start.1 = (bf16[256,512]{1,0:T(8,128)(2,1)S(1)}, bf16[256,512]{1,0:T(8,128)(2,1)S(1)}, u32[]{:S(2)}, u32[]{:S(2)}) collective-permute-start(bf16[256,512]{1,0:T(8,128)(2,1)S(1)} %get-tuple-element.54), channel_id=1, source_target_pairs={{0,16},{1,17},{2,18},{3,19},{4,20},{5,21},{6,22},{7,23},{8,24},{9,... | collective-permute-start | bytes 786440 | tf_op jit(solution)/shard_map/ppermute | solution.py:34
  20.6 12.3 %collective-permute-start.3 = (bf16[256,512]{1,0:T(8,128)(2,1)S(1)}, bf16[256,512]{1,0:T(8,128)(2,1)S(1)}, u32[]{:S(2)}, u32[]{:S(2)}) collective-permute-start(bf16[256,512]{1,0:T(8,128)(2,1)S(1)} %get-tuple-element.54), channel_id=1, source_target_pairs={{0,17},{1,16},{2,19},{3,18},{4,21},{5,20},{6,23},{7,22},{8,25},{9,... | collective-permute-start | bytes 786440 | tf_op jit(solution)/shard_map/ppermute | solution.py:34
  21.4 10.6 %collective-permute-start.2 = (bf16[256,512]{1,0:T(8,128)(2,1)S(1)}, bf16[256,512]{1,0:T(8,128)(2,1)S(1)}, u32[]{:S(2)}, u32[]{:S(2)}) collective-permute-start(bf16[256,512]{1,0:T(8,128)(2,1)S(1)} %get-tuple-element.53), channel_id=1, source_target_pairs={{0,1},{1,0},{2,3},{3,2},{4,5},{5,4},{6,7},{7,6},{8,9},{9,8},{10,11... | collective-permute-start | bytes 786440 | tf_op jit(solution)/shard_map/ppermute | solution.py:34
  34.2 10.0 %collective-permute-start.7 = (bf16[256,512]{1,0:T(8,128)(2,1)S(1)}, bf16[256,512]{1,0:T(8,128)(2,1)S(1)}, u32[]{:S(2)}, u32[]{:S(2)}) collective-permute-start(bf16[256,512]{1,0:T(8,128)(2,1)S(1)} %pad_maximum_fusion.1), channel_id=1, source_target_pairs={{0,16},{1,17},{2,18},{3,19},{4,20},{5,21},{6,22},{7,23},{8,24},{9,... | collective-permute-start | bytes 786440 | tf_op jit(solution)/shard_map/ppermute | solution.py:34
  35.6 4.8 %collective-permute-start.10 = (bf16[384,256]{1,0:T(8,128)(2,1)S(1)}, bf16[384,256]{1,0:T(8,128)(2,1)S(1)}, u32[]{:S(2)}, u32[]{:S(2)}) collective-permute-start(bf16[384,256]{1,0:T(8,128)(2,1)S(1)} %collective-permute-done.6.refs_3_), channel_id=1, source_target_pairs={{0,32},{1,33},{2,34},{3,35},{4,36},{5,37},{6,38},{7,39},{8,40},{9,... | collective-permute-start | bytes 589832 | tf_op jit(solution)/shard_map/ppermute | solution.py:34
  35.6 7.3 %collective-permute-start.8 = (bf16[384,256]{1,0:T(8,128)(2,1)S(1)}, bf16[384,256]{1,0:T(8,128)(2,1)S(1)}, u32[]{:S(2)}, u32[]{:S(2)}) collective-permute-start(bf16[384,256]{1,0:T(8,128)(2,1)S(1)} %collective-permute-done.5.refs_2_), channel_id=1, source_target_pairs={{0,224},{1,225},{2,226},{3,227},{4,228},{5,229},{6,230},{7,231},{8... | collective-permute-start | bytes 589832 | tf_op jit(solution)/shard_map/ppermute | solution.py:34
  37.1 7.4 %collective-permute-start.12 = (bf16[384,256]{1,0:T(8,128)(2,1)S(1)}, bf16[384,256]{1,0:T(8,128)(2,1)S(1)}, u32[]{:S(2)}, u32[]{:S(2)}) collective-permute-start(bf16[384,256]{1,0:T(8,128)(2,1)S(1)} %maximum_maximum_fusion.1.refs_0_), channel_id=1, source_target_pairs={{0,8},{1,9},{2,10},{3,11},{4,12},{5,13},{6,14},{7,15},{8,0},{9,1},... | collective-permute-start | bytes 589832 | tf_op jit(solution)/shard_map/ppermute | solution.py:34
  39.3 6.7 %collective-permute-start.13 = (bf16[384,256]{1,0:T(8,128)(2,1)S(1)}, bf16[384,256]{1,0:T(8,128)(2,1)S(1)}, u32[]{:S(2)}, u32[]{:S(2)}) collective-permute-start(bf16[384,256]{1,0:T(8,128)(2,1)S(1)} %collective-permute-done.5.refs_2_), channel_id=1, source_target_pairs={{0,8},{1,9},{2,10},{3,11},{4,12},{5,13},{6,14},{7,15},{8,0},{9,1},... | collective-permute-start | bytes 589832 | tf_op jit(solution)/shard_map/ppermute | solution.py:34
  40.4 5.6 %collective-permute-start.14 = (bf16[384,256]{1,0:T(8,128)(2,1)S(1)}, bf16[384,256]{1,0:T(8,128)(2,1)S(1)}, u32[]{:S(2)}, u32[]{:S(2)}) collective-permute-start(bf16[384,256]{1,0:T(8,128)(2,1)S(1)} %collective-permute-done.6.refs_3_), channel_id=1, source_target_pairs={{0,8},{1,9},{2,10},{3,11},{4,12},{5,13},{6,14},{7,15},{8,0},{9,1},... | collective-permute-start | bytes 589832 | tf_op jit(solution)/shard_map/ppermute | solution.py:34
  42.9 3.1 %collective-permute-start.15 = (bf16[384,256]{1,0:T(8,128)(2,1)S(1)}, bf16[384,256]{1,0:T(8,128)(2,1)S(1)}, u32[]{:S(2)}, u32[]{:S(2)}) collective-permute-start(bf16[384,256]{1,0:T(8,128)(2,1)S(1)} %collective-permute-done.10.refs_6_), channel_id=1, source_target_pairs={{0,8},{1,9},{2,10},{3,11},{4,12},{5,13},{6,14},{7,15},{8,0},{9,1},... | collective-permute-start | bytes 589832 | tf_op jit(solution)/shard_map/ppermute | solution.py:34
  44.2 1.9 %collective-permute-start.16 = (bf16[384,256]{1,0:T(8,128)(2,1)S(1)}, bf16[384,256]{1,0:T(8,128)(2,1)S(1)}, u32[]{:S(2)}, u32[]{:S(2)}) collective-permute-start(bf16[384,256]{1,0:T(8,128)(2,1)S(1)} %collective-permute-done.8.refs_7_), channel_id=1, source_target_pairs={{0,8},{1,9},{2,10},{3,11},{4,12},{5,13},{6,14},{7,15},{8,0},{9,1},... | collective-permute-start | bytes 589832 | tf_op jit(solution)/shard_map/ppermute | solution.py:34
  44.5 8.0 %collective-permute-start.11 = (bf16[384,256]{1,0:T(8,128)(2,1)S(1)}, bf16[384,256]{1,0:T(8,128)(2,1)S(1)}, u32[]{:S(2)}, u32[]{:S(2)}) collective-permute-start(bf16[384,256]{1,0:T(8,128)(2,1)S(1)} %collective-permute-done.10.refs_6_), channel_id=1, source_target_pairs={{0,224},{1,225},{2,226},{3,227},{4,228},{5,229},{6,230},{7,231},{8... | collective-permute-start | bytes 589832 | tf_op jit(solution)/shard_map/ppermute | solution.py:34
  46.0 6.6 %collective-permute-start.9 = (bf16[384,256]{1,0:T(8,128)(2,1)S(1)}, bf16[384,256]{1,0:T(8,128)(2,1)S(1)}, u32[]{:S(2)}, u32[]{:S(2)}) collective-permute-start(bf16[384,256]{1,0:T(8,128)(2,1)S(1)} %collective-permute-done.8.refs_7_), channel_id=1, source_target_pairs={{0,32},{1,33},{2,34},{3,35},{4,36},{5,37},{6,38},{7,39},{8,40},{9,... | collective-permute-start | bytes 589832 | tf_op jit(solution)/shard_map/ppermute | solution.py:34
  52.6 9.4 %collective-permute-start.19 = (bf16[384,256]{1,0:T(8,128)(2,1)S(1)}, bf16[384,256]{1,0:T(8,128)(2,1)S(1)}, u32[]{:S(2)}, u32[]{:S(2)}) collective-permute-start(bf16[384,256]{1,0:T(8,128)(2,1)S(1)} %collective-permute-done.11.refs_1_), channel_id=1, source_target_pairs={{0,32},{1,33},{2,34},{3,35},{4,36},{5,37},{6,38},{7,39},{8,40},{9,... | collective-permute-start | bytes 589832 | tf_op jit(solution)/shard_map/ppermute | solution.py:34
  54.1 8.5 %collective-permute-start.18 = (bf16[384,256]{1,0:T(8,128)(2,1)S(1)}, bf16[384,256]{1,0:T(8,128)(2,1)S(1)}, u32[]{:S(2)}, u32[]{:S(2)}) collective-permute-start(bf16[384,256]{1,0:T(8,128)(2,1)S(1)} %collective-permute-done.11.refs_1_), channel_id=1, source_target_pairs={{0,8},{1,9},{2,10},{3,11},{4,12},{5,13},{6,14},{7,15},{8,0},{9,1},... | collective-permute-start | bytes 589832 | tf_op jit(solution)/shard_map/ppermute | solution.py:34
  55.5 7.1 %collective-permute-start.17 = (bf16[384,256]{1,0:T(8,128)(2,1)S(1)}, bf16[384,256]{1,0:T(8,128)(2,1)S(1)}, u32[]{:S(2)}, u32[]{:S(2)}) collective-permute-start(bf16[384,256]{1,0:T(8,128)(2,1)S(1)} %collective-permute-done.9.refs_0_), channel_id=1, source_target_pairs={{0,8},{1,9},{2,10},{3,11},{4,12},{5,13},{6,14},{7,15},{8,0},{9,1},... | collective-permute-start | bytes 589832 | tf_op jit(solution)/shard_map/ppermute | solution.py:34
  62.0 1.7 %collective-permute-start.20 = (bf16[384,256]{1,0:T(8,128)(2,1)S(1)}, bf16[384,256]{1,0:T(8,128)(2,1)S(1)}, u32[]{:S(2)}, u32[]{:S(2)}) collective-permute-start(bf16[384,256]{1,0:T(8,128)(2,1)S(1)} %collective-permute-done.19.refs_4_), channel_id=1, source_target_pairs={{0,8},{1,9},{2,10},{3,11},{4,12},{5,13},{6,14},{7,15},{8,0},{9,1},... | collective-permute-start | bytes 589832 | tf_op jit(solution)/shard_map/ppermute | solution.py:34
  92.0 9.1 %collective-permute-start.22 = (bf16[64,2048]{1,0:T(8,128)(2,1)S(1)}, bf16[64,2048]{1,0:T(8,128)(2,1)S(1)}, u32[]{:S(2)}, u32[]{:S(2)}) collective-permute-start(bf16[64,2048]{1,0:T(8,128)(2,1)S(1)} %shard_map.76.refs_0_), channel_id=1, source_target_pairs={{0,224},{1,225},{2,226},{3,227},{4,228},{5,229},{6,230},{7,231},{8... | collective-permute-start | bytes 786440 | tf_op jit(solution)/shard_map/ppermute | solution.py:34
  95.6 6.4 %collective-permute-start.21 = (bf16[64,2048]{1,0:T(8,128)(2,1)S(1)}, bf16[64,2048]{1,0:T(8,128)(2,1)S(1)}, u32[]{:S(2)}, u32[]{:S(2)}) collective-permute-start(bf16[64,2048]{1,0:T(8,128)(2,1)S(1)} %shard_map.76.refs_0_), channel_id=1, source_target_pairs={{0,32},{1,33},{2,34},{3,35},{4,36},{5,37},{6,38},{7,39},{8,40},{9,... | collective-permute-start | bytes 786440 | tf_op jit(solution)/shard_map/ppermute | solution.py:34
  101.0 6.4 %collective-permute-start.23 = (bf16[64,2048]{1,0:T(8,128)(2,1)S(1)}, bf16[64,2048]{1,0:T(8,128)(2,1)S(1)}, u32[]{:S(2)}, u32[]{:S(2)}) collective-permute-start(bf16[64,2048]{1,0:T(8,128)(2,1)S(1)} %collective-permute-done.22.refs_2_), channel_id=1, source_target_pairs={{0,32},{1,33},{2,34},{3,35},{4,36},{5,37},{6,38},{7,39},{8,40},{9,... | collective-permute-start | bytes 786440 | tf_op jit(solution)/shard_map/ppermute | solution.py:34
  102.0 7.2 %collective-permute-start.24 = (bf16[64,2048]{1,0:T(8,128)(2,1)S(1)}, bf16[64,2048]{1,0:T(8,128)(2,1)S(1)}, u32[]{:S(2)}, u32[]{:S(2)}) collective-permute-start(bf16[64,2048]{1,0:T(8,128)(2,1)S(1)} %collective-permute-done.21.refs_1_), channel_id=1, source_target_pairs={{0,224},{1,225},{2,226},{3,227},{4,228},{5,229},{6,230},{7,231},{8... | collective-permute-start | bytes 786440 | tf_op jit(solution)/shard_map/ppermute | solution.py:34
  107.4 7.1 %collective-permute-start.27 = (bf16[64,2048]{1,0:T(8,128)(2,1)S(1)}, bf16[64,2048]{1,0:T(8,128)(2,1)S(1)}, u32[]{:S(2)}, u32[]{:S(2)}) collective-permute-start(bf16[64,2048]{1,0:T(8,128)(2,1)S(1)} %collective-permute-done.23.refs_3_), channel_id=1, source_target_pairs={{0,224},{1,225},{2,226},{3,227},{4,228},{5,229},{6,230},{7,231},{8... | collective-permute-start | bytes 786440 | tf_op jit(solution)/shard_map/ppermute | solution.py:34
  109.2 13.6 %collective-permute-start.26 = (bf16[64,2048]{1,0:T(8,128)(2,1)S(1)}, bf16[64,2048]{1,0:T(8,128)(2,1)S(1)}, u32[]{:S(2)}, u32[]{:S(2)}) collective-permute-start(bf16[64,2048]{1,0:T(8,128)(2,1)S(1)} %collective-permute-done.24.refs_4_), channel_id=1, source_target_pairs={{0,32},{1,33},{2,34},{3,35},{4,36},{5,37},{6,38},{7,39},{8,40},{9,... | collective-permute-start | bytes 786440 | tf_op jit(solution)/shard_map/ppermute | solution.py:34
  114.5 8.3 %collective-permute-start.28 = (bf16[64,2048]{1,0:T(8,128)(2,1)S(1)}, bf16[64,2048]{1,0:T(8,128)(2,1)S(1)}, u32[]{:S(2)}, u32[]{:S(2)}) collective-permute-start(bf16[64,2048]{1,0:T(8,128)(2,1)S(1)} %collective-permute-done.27.refs_1_), channel_id=1, source_target_pairs={{0,32},{1,33},{2,34},{3,35},{4,36},{5,37},{6,38},{7,39},{8,40},{9,... | collective-permute-start | bytes 786440 | tf_op jit(solution)/shard_map/ppermute | solution.py:34
  119.8 8.2 %collective-permute-start.25 = (bf16[320,512]{1,0:T(8,128)(2,1)S(1)}, bf16[320,512]{1,0:T(8,128)(2,1)S(1)}, u32[]{:S(2)}, u32[]{:S(2)}) collective-permute-start(bf16[320,512]{1,0:T(8,128)(2,1)S(1)} %get-tuple-element.48), channel_id=1, source_target_pairs={{0,8},{1,9},{2,10},{3,11},{4,12},{5,13},{6,14},{7,15},{8,0},{9,1},... | collective-permute-start | bytes 983048 | tf_op jit(solution)/shard_map/ppermute | solution.py:34
  125.3 2.7 %collective-permute-start.29 = (bf16[192,512]{1,0:T(8,128)(2,1)S(1)}, bf16[192,512]{1,0:T(8,128)(2,1)S(1)}, u32[]{:S(2)}, u32[]{:S(2)}) collective-permute-start(bf16[192,512]{1,0:T(8,128)(2,1)S(1)} %get-tuple-element.50), channel_id=1, source_target_pairs={{0,8},{1,9},{2,10},{3,11},{4,12},{5,13},{6,14},{7,15},{8,0},{9,1},... | collective-permute-start | bytes 589832 | tf_op jit(solution)/shard_map/ppermute | solution.py:34
  (3 other events, 20.1 us)
Sparse Core Ops, SparseCore 0:
  34.3 48.2 all-gather.1

commit v4 on v3

--- a/solution.py
+++ b/solution.py
@@ -40,6 +40,10 @@
 
 def meet_down(value):
     return permute(value, lambda z, yh, c, x, yl: (z - 1 + 2 * (z % 2), yh, c, x, yl))
+
+
+def shift_x(value, step):
+    return permute(value, lambda z, yh, c, x, yl: (z, yh, c, x + step, yl))
 
 
 def shifted(z, shift):
@@ -179,10 +183,10 @@
 
 
 def combine_kernel(group, meta, pieces, out):
-    yl = meta[4]
+    x, yl = meta[3], meta[4]
 
     def one(t, _):
-        spot = t // NL * NL + lax.rem(t + yl, NL)
+        spot = lax.rem(t // NL - x + NX, NX) * NL + lax.rem(t + yl, NL)
         for at in range(0, pieces.shape[2], HEAD):
             values, weights = [], []
             for half in range(NY):
@@ -211,44 +215,51 @@
     )(meta, pieces)
 
 
-def project_kernel(*refs):
-    blocks, weight, (keep, send) = refs[:-3], refs[-3], refs[-2:]
-    total = jnp.dot(
-        jnp.concatenate([block[...] for block in blocks], 0), weight[...], preferred_element_type=F32
-    )
-
-    @pl.when(pl.program_id(0) < 2)
+def project_kernel(count, *refs):
+    blocks, weights, (keep, send) = refs[:count], refs[count:-2], refs[-2:]
+    total, at = None, 0
+    for weight in weights:
+        depth = weight.shape[0]
+        a = jnp.concatenate([block[:, at : at + depth] for block in blocks], 0)
+        term = jnp.dot(a, weight[...], preferred_element_type=F32)
+        total = term if total is None else total + term
+        at += depth
+
+    @pl.when(pl.program_id(0) < NY)
     def _():
         keep[...] = total
 
-    @pl.when(pl.program_id(0) >= 2)
+    @pl.when(pl.program_id(0) >= NY)
     def _():
         send[...] = total.astype(BF16)
 
 
-def project(blocks, weight):
+def project(blocks, weights):
     rows = blocks[0].shape[0] * len(blocks)
-    depth, width = weight.shape
-    tile = width // 4
-    place = lambda j: 2 * (j % 2) + j // 2
+    width = weights[0].shape[1]
+    tile = width // (NY * NC)
+    place = lambda j: j % NY * NC + j // NY
     whole = pl.BlockSpec(blocks[0].shape, lambda j: (0, 0))
     return pl.pallas_call(
-        project_kernel,
-        grid=(4,),
-        in_specs=[whole] * len(blocks) + [pl.BlockSpec((depth, tile), lambda j: (0, place(j)))],
+        functools.partial(project_kernel, len(blocks)),
+        grid=(NC * NY,),
+        in_specs=[whole] * len(blocks)
+        + [pl.BlockSpec((weight.shape[0], tile), lambda j: (0, place(j))) for weight in weights],
         out_specs=[
-            pl.BlockSpec((rows, tile), lambda j: (0, jnp.minimum(j, 1))),
-            pl.BlockSpec((rows, tile), lambda j: (0, jnp.maximum(j - 2, 0))),
+            pl.BlockSpec((rows, tile), lambda j: (0, jnp.minimum(j, NY - 1))),
+            pl.BlockSpec((rows, tile), lambda j: (0, jnp.maximum(j - NY, 0))),
         ],
         out_shape=[
-            jax.ShapeDtypeStruct((rows, width // 2), F32),
-            jax.ShapeDtypeStruct((rows, width // 2), BF16),
+            jax.ShapeDtypeStruct((rows, NY * tile), F32),
+            jax.ShapeDtypeStruct((rows, NY * tile), BF16),
         ],
         compiler_params=pltpu.CompilerParams(vmem_limit_bytes=VMEM),
         cost_estimate=pl.CostEstimate(
-            flops=2 * rows * depth * width, bytes_accessed=2 * depth * width, transcendentals=0
+            flops=2 * rows * blocks[0].shape[1] * width,
+            bytes_accessed=2 * blocks[0].shape[1] * width,
+            transcendentals=0,
         ),
-    )(*blocks, weight)
+    )(*blocks, *weights)
 
 
 def settle_kernel(order, meta, *refs):
@@ -294,28 +305,21 @@
     ahead, behind = meet_up(kv), meet_down(kv)
     twin_kv = swap(kv, b=1)
 
+    half = queries.shape[1] // 2
+    mine = lax.dynamic_slice_in_dim(queries, core * half, half, 1)
+    theirs = swap(lax.dynamic_slice_in_dim(queries, (1 - core) * half, half, 1), b=1)
+    near = jnp.concatenate([jnp.where(core == 0, mine, theirs), jnp.where(core == 0, theirs, mine)], 0)
+    far = swap(near, a=1)
+    q = jnp.concatenate([jnp.where(yh == 0, near, far), jnp.where(yh == 0, far, near)], 0)
+
+    ahead, behind, out_weight = lax.optimization_barrier((ahead, behind, out_weight))
     depth = out_weight.shape[0] // 4
     block = lambda value, at, rows: lax.dynamic_slice_in_dim(value, at * rows, rows, 0)
     wide = jnp.concatenate(
         [block(out_weight, core, 2 * depth), swap(block(out_weight, 1 - core, 2 * depth), b=1)], 1
     )
     keep, give = block(wide, yh, depth), block(wide, 1 - yh, depth)
-    wide = jnp.concatenate(
-        [
-            jnp.concatenate([keep, swap(give, a=1)], 1),
-            jnp.concatenate([swap(keep, d=1), swap(give, a=1, d=1)], 1),
-        ],
-        0,
-    )
-
-    half = queries.shape[1] // 2
-    mine = lax.dynamic_slice_in_dim(queries, core * half, half, 1)
-    theirs = swap(lax.dynamic_slice_in_dim(queries, (1 - core) * half, half, 1), b=1)
-    near = jnp.concatenate([jnp.where(core == 0, mine, theirs), jnp.where(core == 0, theirs, mine)], 0)
-    wide, near, ahead, behind = lax.optimization_barrier((wide, near, ahead, behind))
-    weight = lax.all_gather(wide, "x", axis=0, tiled=True)
-    far = swap(near, a=1)
-    q = jnp.concatenate([jnp.where(yh == 0, near, far), jnp.where(yh == 0, far, near)], 0)
+    quarters = [keep, swap(give, a=1), swap(keep, d=1), swap(give, a=1, d=1)]
 
     def both(ahead, behind, step):
         near = [(ahead, 0, step, 0), (behind, 0, -step, 0)]
@@ -326,7 +330,11 @@
     blocks += both(ahead, behind, 2)
     ahead, behind = meet_up(behind), meet_down(ahead)
     low = attend(meta, cache_lengths, q, blocks, 0, None, cache, fresh)
-    ahead, behind, low = lax.optimization_barrier((ahead, behind, low))
+    ahead, behind, low, quarters = lax.optimization_barrier((ahead, behind, low, quarters))
+    wide = jnp.concatenate(
+        [jnp.concatenate(quarters[:2], 1), jnp.concatenate(quarters[2:], 1)], 0
+    )
+    wide_f, wide_b = shift_x(wide, 1), shift_x(wide, -1)
     last_blocks = both(ahead, behind, 3)
     ahead = meet_up(behind)
     high = attend(meta, cache_lengths, q, blocks, 1, None, cache, fresh)
@@ -339,6 +347,8 @@
         pieces.reshape(NY * NZ, group, width), ("yh", "x", "yl"), split_axis=0, concat_axis=0, tiled=True
     )
     a = combine(meta, pieces)
+    a, wide_f, wide_b = lax.optimization_barrier((a, wide_f, wide_b))
+    weights = [wide, wide_b, shift_x(wide_f[:depth], 1), shift_x(wide_b[depth:], -1), wide_f]
     ahead, behind = [a], [a]
     for _ in range(3):
         up, down = meet_up(behind[-1]), meet_down(ahead[-1])
@@ -347,7 +357,7 @@
     ahead.append(meet_up(behind[-1]))
 
     def share(blocks):
-        kept, sent = project(blocks, weight)
+        kept, sent = project(blocks, weights)
         return kept, swap(sent, b=1)
 
     order = ((0, 1, -1, 2, -2), (3, -3, 4))

time: 151 us -> 138 us (0.914)
  between operations: 13.6 us -> 0.23 us
  starting transfers between devices: 37.9 us -> 41.5 us
  local copies, waits for them, and re-layouts: 4.3 us -> 1.17 us
    ppermute x30 -> x34, starting transfers between devices: 37.9 us -> 41.5 us  [permute(): return lax.ppermute(value, AXES, pairs)]
    unnamed x8 -> x4, local copies, waits for them, and re-layouts: 2.2 us -> 0.01 us
    ppermute x30 -> x34, waiting for transfers between devices: 30.2 us -> 29 us  [permute(): return lax.ppermute(value, AXES, pairs)]
  transfers between devices with their start and end apart: 31 -> 34, of which waited for: 10 -> 12; matrix products, arithmetic and copies ran while one was open for 2% -> 2% of each run, Pallas kernels for 19% -> 21%
where the time goes in v4:
time: 138 us
  starting transfers between devices  41.5 us (30%)
  blocking collectives  33.3 us (24%)
  Pallas kernels  29.6 us (21%)
  waiting for transfers between devices  29 us (21%)
  other arithmetic  2.98 us (2%)
    ppermute x34, starting transfers between devices, permute(): return lax.ppermute(value, AXES, pairs)  41.5 us
    ppermute x34, waiting for transfers between devices, permute(): return lax.ppermute(value, AXES, pairs)  29 us
    pallas_call x3, Pallas kernels, attend(): pl.pallas_call(functools.partial(attend_kernel, tuple((entry[1:] for entr...  22.5 us
    all_to_all x1, blocking collectives, shards(): lax.all_to_all(pieces.reshape(NY * NZ, group, width), ('yh', 'x', 'yl'),...  18.1 us
    all_to_all x1, blocking collectives, shards(): lax.all_to_all(settled.reshape(NY * NZ, rows, width), ('yh', 'x', 'yl'),...  15.2 us
    pallas_call x2, Pallas kernels, project(): pl.pallas_call(functools.partial(project_kernel, len(blocks)), grid=(NC *...  5.32 us
  transfers between devices with their start and end apart: 34, of which 12 were waited for; matrix products, arithmetic and copies ran while one was open for 2% of the time, Pallas kernels for 21%

profile of v4, /device:TPU:1, one launch (start us, length us, event | category | flops | bytes accessed | tf_op | source)
XLA Modules:
  0.0 137.8 jit_solution(17032137281190233464)
XLA Ops:
  1.0 3.3 %collective-permute-start = (bf16[128,512]{1,0:T(8,128)(2,1)S(1)}, bf16[128,512]{1,0:T(8,128)(2,1)S(1)}, u32[]{:S(2)}, u32[]{:S(2)}) collective-permute-start(bf16[128,512]{1,0:T(8,128)(2,1)S(1)} %constant_dynamic-slice_fusion.2), channel_id=1, source_target_pairs={{0,8},{1,9},{2,10},{3,11},{4,12},{5,13},{6,14},{7,15},{8,0},{9,1},... | collective-permute-start | bytes 393224 | tf_op jit(solution)/shard_map/ppermute | solution.py:34
  5.2 3.9 %collective-permute-start.3 = (bf16[384,256]{1,0:T(8,128)(2,1)S(1)}, bf16[384,256]{1,0:T(8,128)(2,1)S(1)}, u32[]{:S(2)}, u32[]{:S(2)}) collective-permute-start(bf16[384,256]{1,0:T(8,128)(2,1)S(1)} %maximum_maximum_fusion.1.refs_0_), channel_id=1, source_target_pairs={{0,224},{1,225},{2,226},{3,227},{4,228},{5,229},{6,230},{7,231},{8... | collective-permute-start | bytes 589832 | tf_op jit(solution)/shard_map/ppermute | solution.py:34
  10.2 3.0 %collective-permute-start.1 = (bf16[256,512]{1,0:T(8,128)(2,1)S(1)}, bf16[256,512]{1,0:T(8,128)(2,1)S(1)}, u32[]{:S(2)}, u32[]{:S(2)}) collective-permute-start(bf16[256,512]{1,0:T(8,128)(2,1)S(1)} %pad_maximum_fusion.1), channel_id=1, source_target_pairs={{0,16},{1,17},{2,18},{3,19},{4,20},{5,21},{6,22},{7,23},{8,24},{9,... | collective-permute-start | bytes 786440 | tf_op jit(solution)/shard_map/ppermute | solution.py:34
  13.2 1.3 collective-permute-done.3.refs_3_
  15.4 1.2 collective-permute-start.13
  16.6 1.2 collective-permute-start.4
  19.4 1.1 collective-permute-start.9
  20.5 3.8 %collective-permute-done.4.refs_7_ = bf16[384,256]{1,0:T(8,128)(2,1)S(1)} collective-permute-done((bf16[384,256]{1,0:T(8,128)(2,1)S(1)}, bf16[384,256]{1,0:T(8,128)(2,1)S(1)}, u32[]{:S(2)}, u32[]{:S(2)}) %collective-permute-start.4) | collective-permute-done | bytes 196640 | tf_op jit(solution)/shard_map/ppermute | solution.py:34
  26.0 1.3 collective-permute-start.7
  27.3 2.9 %collective-permute-start.14 = (bf16[256,512]{1,0:T(8,128)(2,1)S(1)}, bf16[256,512]{1,0:T(8,128)(2,1)S(1)}, u32[]{:S(2)}, u32[]{:S(2)}) collective-permute-start(bf16[256,512]{1,0:T(8,128)(2,1)S(1)} %get-tuple-element.63), channel_id=1, source_target_pairs={{0,16},{1,17},{2,18},{3,19},{4,20},{5,21},{6,22},{7,23},{8,24},{9,... | collective-permute-start | bytes 786440 | tf_op jit(solution)/shard_map/ppermute | solution.py:34
  31.0 6.5 %shard_map.73 = (f32[512,256]{1,0:T(8,128)S(1)}, f32[512,256]{1,0:T(8,128)S(1)}, f32[512,256]{1,0:T(8,128)S(1)}) custom-call(s32[5]{0:T(128)S(1)} %stack.23.meta, s32[32]{0:T(128)S(1)} %copy-done, bf16[512,512]{1,0:T(8,128)(2,1)S(1)} %pad_maximum_fusion.q_ref, bf16[384,256]{1,0:T(8,128)(2,1)S(1)} %maximum_maximum_fusion.1.refs_0_, ...), custom_call_target="tpu_custom_call" | custom-call | flops 2013265920 | bytes 1048576 | tf_op jit(solution)/shard_map/pallas_call | solution.py:168
  37.6 5.0 %collective-permute-done.16 = bf16[256,512]{1,0:T(8,128)(2,1)S(1)} collective-permute-done((bf16[256,512]{1,0:T(8,128)(2,1)S(1)}, bf16[256,512]{1,0:T(8,128)(2,1)S(1)}, u32[]{:S(2)}, u32[]{:S(2)}) %collective-permute-start.16) | collective-permute-done | bytes 262176 | tf_op jit(solution)/shard_map/ppermute | solution.py:34
  43.6 2.6 %collective-permute-start.22 = (bf16[512,1024]{1,0:T(8,128)(2,1)S(1)}, bf16[512,1024]{1,0:T(8,128)(2,1)S(1)}, u32[]{:S(2)}, u32[]{:S(2)}) collective-permute-start(bf16[512,1024]{1,0:T(8,128)(2,1)S(1)} %maximum_maximum_fusion.refs_5_.refs_3_), channel_id=1, source_target_pairs={{0,6},{1,7},{2,0},{3,1},{4,2},{5,3},{6,4},{7,5},{8,14},{9,15},{10,... | collective-permute-start | bytes 3145736 | tf_op jit(solution)/shard_map/ppermute | solution.py:34
  46.2 6.7 %shard_map.74 = (f32[512,256]{1,0:T(8,128)S(1)}, f32[512,256]{1,0:T(8,128)S(1)}, f32[512,256]{1,0:T(8,128)S(1)}) custom-call(s32[5]{0:T(128)S(1)} %stack.23.meta, s32[32]{0:T(128)S(1)} %copy-done, bf16[512,512]{1,0:T(8,128)(2,1)S(1)} %pad_maximum_fusion.q_ref, bf16[384,256]{1,0:T(8,128)(2,1)S(1)} %maximum_maximum_fusion.1.refs_0_, ...), custom_call_target="tpu_custom_call" | custom-call | flops 2013265920 | bytes 1048576 | tf_op jit(solution)/shard_map/pallas_call | solution.py:168
  52.9 1.5 %collective-permute-start.18 = (bf16[384,256]{1,0:T(8,128)(2,1)S(1)}, bf16[384,256]{1,0:T(8,128)(2,1)S(1)}, u32[]{:S(2)}, u32[]{:S(2)}) collective-permute-start(bf16[384,256]{1,0:T(8,128)(2,1)S(1)} %collective-permute-done.7.refs_1_), channel_id=1, source_target_pairs={{0,8},{1,9},{2,10},{3,11},{4,12},{5,13},{6,14},{7,15},{8,0},{9,1},... | collective-permute-start | bytes 589832 | tf_op jit(solution)/shard_map/ppermute | solution.py:34
  56.2 9.2 %shard_map.75 = bf16[2,8,80,256]{3,2,1,0:T(8,128)(2,1)S(1)} custom-call(s32[5]{0:T(128)S(1)} %stack.23.meta, s32[32]{0:T(128)S(1)} %copy-done, bf16[512,512]{1,0:T(8,128)(2,1)S(1)} %pad_maximum_fusion.q_ref, bf16[384,256]{1,0:T(8,128)(2,1)S(1)} %collective-permute-done.5.refs_0_, bf16[384,256]{1,0:T(8,128)(2,1)S(1)} %collective-permute-done.7.refs_1_, ...), custom_call_target="tpu_custom_call" | custom-call | flops 2415919104 | bytes 1048576 | tf_op jit(solution)/shard_map/pallas_call | solution.py:168
  65.4 18.1 %all_to_all.10.pieces = bf16[16,80,256]{2,1,0:T(8,128)(2,1)S(1)} all-to-all(bf16[16,80,256]{2,1,0:T(8,128)(2,1)S(1)} %bitcast.9), channel_id=1, replica_groups=mesh['z'=8,'yh'=2,'core'=2,'x'=4,'yl'=2] {'yh','x','yl'}, dimensions={0} | all-to-all | bytes 1310720 | tf_op jit(solution)/shard_map/all_to_all | solution.py:346
  83.5 1.2 shard_map.76.refs_0_
  84.7 1.3 collective-permute-start.24
  86.1 5.9 %collective-permute-done.24.refs_2_ = bf16[64,2048]{1,0:T(8,128)(2,1)S(1)} collective-permute-done((bf16[64,2048]{1,0:T(8,128)(2,1)S(1)}, bf16[64,2048]{1,0:T(8,128)(2,1)S(1)}, u32[]{:S(2)}, u32[]{:S(2)}) %collective-permute-start.24) | collective-permute-done | bytes 262176 | tf_op jit(solution)/shard_map/ppermute | solution.py:34
  92.2 2.7 %collective-permute-start.28 = (bf16[256,1024]{1,0:T(8,128)(2,1)S(1)}, bf16[256,1024]{1,0:T(8,128)(2,1)S(1)}, u32[]{:S(2)}, u32[]{:S(2)}) collective-permute-start(bf16[256,1024]{1,0:T(8,128)(2,1)S(1)} %slice.15), channel_id=1, source_target_pairs={{0,6},{1,7},{2,0},{3,1},{4,2},{5,3},{6,4},{7,5},{8,14},{9,15},{10,... | collective-permute-start | bytes 1572872 | tf_op jit(solution)/shard_map/ppermute | solution.py:34
  94.8 1.2 collective-permute-start.26
  96.0 1.2 collective-permute-done.25.refs_3_
  97.2 1.2 collective-permute-start.31
  98.4 3.1 %collective-permute-done.26.refs_4_ = bf16[64,2048]{1,0:T(8,128)(2,1)S(1)} collective-permute-done((bf16[64,2048]{1,0:T(8,128)(2,1)S(1)}, bf16[64,2048]{1,0:T(8,128)(2,1)S(1)}, u32[]{:S(2)}, u32[]{:S(2)}) %collective-permute-start.26) | collective-permute-done | bytes 262176 | tf_op jit(solution)/shard_map/ppermute | solution.py:34
  101.8 4.4 %collective-permute-done.31.refs_1_ = bf16[64,2048]{1,0:T(8,128)(2,1)S(1)} collective-permute-done((bf16[64,2048]{1,0:T(8,128)(2,1)S(1)}, bf16[64,2048]{1,0:T(8,128)(2,1)S(1)}, u32[]{:S(2)}, u32[]{:S(2)}) %collective-permute-start.31) | collective-permute-done | bytes 262176 | tf_op jit(solution)/shard_map/ppermute | solution.py:34
  106.2 3.0 %shard_map.77 = (f32[320,512]{1,0:T(8,128)S(1)}, bf16[320,512]{1,0:T(8,128)(2,1)S(1)}) custom-call(bf16[64,2048]{1,0:T(8,128)(2,1)S(1)} %shard_map.76.refs_0_, bf16[64,2048]{1,0:T(8,128)(2,1)S(1)} %collective-permute-done.23.refs_1_, bf16[64,2048]{1,0:T(8,128)(2,1)S(1)} %collective-permute-done.24.refs_2_, ...), custom_call_target="tpu_custom_call" | custom-call | flops 1342177280 | bytes 4194304 | tf_op jit(solution)/shard_map/pallas_call | solution.py:243
  109.2 4.8 %collective-permute-start.29 = (bf16[320,512]{1,0:T(8,128)(2,1)S(1)}, bf16[320,512]{1,0:T(8,128)(2,1)S(1)}, u32[]{:S(2)}, u32[]{:S(2)}) collective-permute-start(bf16[320,512]{1,0:T(8,128)(2,1)S(1)} %get-tuple-element.60), channel_id=1, source_target_pairs={{0,8},{1,9},{2,10},{3,11},{4,12},{5,13},{6,14},{7,15},{8,0},{9,1},... | collective-permute-start | bytes 983048 | tf_op jit(solution)/shard_map/ppermute | solution.py:34
  114.0 2.4 %shard_map.78 = (f32[192,512]{1,0:T(8,128)S(1)}, bf16[192,512]{1,0:T(8,128)(2,1)S(1)}) custom-call(bf16[64,2048]{1,0:T(8,128)(2,1)S(1)} %collective-permute-done.30.refs_0_, bf16[64,2048]{1,0:T(8,128)(2,1)S(1)} %collective-permute-done.31.refs_1_, bf16[64,2048]{1,0:T(8,128)(2,1)S(1)} %collective-permute-done.32.refs_2_, ...), custom_call_target="tpu_custom_call" | custom-call | flops 805306368 | bytes 4194304 | tf_op jit(solution)/shard_map/pallas_call | solution.py:243
  116.3 3.8 %collective-permute-start.33 = (bf16[192,512]{1,0:T(8,128)(2,1)S(1)}, bf16[192,512]{1,0:T(8,128)(2,1)S(1)}, u32[]{:S(2)}, u32[]{:S(2)}) collective-permute-start(bf16[192,512]{1,0:T(8,128)(2,1)S(1)} %get-tuple-element.62), channel_id=1, source_target_pairs={{0,8},{1,9},{2,10},{3,11},{4,12},{5,13},{6,14},{7,15},{8,0},{9,1},... | collective-permute-start | bytes 589832 | tf_op jit(solution)/shard_map/ppermute | solution.py:34
  120.2 1.1 collective-permute-done.33.refs_3_
  121.9 15.2 %all_to_all.11 = bf16[16,64,256]{2,1,0:T(8,128)(2,1)S(1)} all-to-all(bf16[16,64,256]{2,1,0:T(8,128)(2,1)S(1)} %bitcast.8), channel_id=1, replica_groups=mesh['z'=8,'yh'=2,'core'=2,'x'=4,'yl'=2] {'yh','x','yl'}, dimensions={0} | all-to-all | bytes 1048576 | tf_op jit(solution)/shard_map/all_to_all | solution.py:368
  (62 shorter events, 12.5 us)
Async XLA Ops:
  1.0 8.2 %collective-permute-start = (bf16[128,512]{1,0:T(8,128)(2,1)S(1)}, bf16[128,512]{1,0:T(8,128)(2,1)S(1)}, u32[]{:S(2)}, u32[]{:S(2)}) collective-permute-start(bf16[128,512]{1,0:T(8,128)(2,1)S(1)} %constant_dynamic-slice_fusion.2), channel_id=1, source_target_pairs={{0,8},{1,9},{2,10},{3,11},{4,12},{5,13},{6,14},{7,15},{8,0},{9,1},... | collective-permute-start | bytes 393224 | tf_op jit(solution)/shard_map/ppermute | solution.py:34
  5.2 9.2 %collective-permute-start.3 = (bf16[384,256]{1,0:T(8,128)(2,1)S(1)}, bf16[384,256]{1,0:T(8,128)(2,1)S(1)}, u32[]{:S(2)}, u32[]{:S(2)}) collective-permute-start(bf16[384,256]{1,0:T(8,128)(2,1)S(1)} %maximum_maximum_fusion.1.refs_0_), channel_id=1, source_target_pairs={{0,224},{1,225},{2,226},{3,227},{4,228},{5,229},{6,230},{7,231},{8... | collective-permute-start | bytes 589832 | tf_op jit(solution)/shard_map/ppermute | solution.py:34
  9.2 6.2 %collective-permute-start.2 = (bf16[384,256]{1,0:T(8,128)(2,1)S(1)}, bf16[384,256]{1,0:T(8,128)(2,1)S(1)}, u32[]{:S(2)}, u32[]{:S(2)}) collective-permute-start(bf16[384,256]{1,0:T(8,128)(2,1)S(1)} %maximum_maximum_fusion.1.refs_0_), channel_id=1, source_target_pairs={{0,32},{1,33},{2,34},{3,35},{4,36},{5,37},{6,38},{7,39},{8,40},{9,... | collective-permute-start | bytes 589832 | tf_op jit(solution)/shard_map/ppermute | solution.py:34
  10.2 9.2 %collective-permute-start.1 = (bf16[256,512]{1,0:T(8,128)(2,1)S(1)}, bf16[256,512]{1,0:T(8,128)(2,1)S(1)}, u32[]{:S(2)}, u32[]{:S(2)}) collective-permute-start(bf16[256,512]{1,0:T(8,128)(2,1)S(1)} %pad_maximum_fusion.1), channel_id=1, source_target_pairs={{0,16},{1,17},{2,18},{3,19},{4,20},{5,21},{6,22},{7,23},{8,24},{9,... | collective-permute-start | bytes 786440 | tf_op jit(solution)/shard_map/ppermute | solution.py:34
  15.4 9.8 %collective-permute-start.13 = (bf16[512,256]{1,0:T(8,128)(2,1)S(1)}, bf16[512,256]{1,0:T(8,128)(2,1)S(1)}, u32[]{:S(2)}, u32[]{:S(2)}) collective-permute-start(bf16[512,256]{1,0:T(8,128)(2,1)S(1)} %get-tuple-element.65), channel_id=1, source_target_pairs={{0,8},{1,9},{2,10},{3,11},{4,12},{5,13},{6,14},{7,15},{8,0},{9,1},... | collective-permute-start | bytes 786440 | tf_op jit(solution)/shard_map/ppermute | solution.py:34
  16.6 7.7 %collective-permute-start.4 = (bf16[384,256]{1,0:T(8,128)(2,1)S(1)}, bf16[384,256]{1,0:T(8,128)(2,1)S(1)}, u32[]{:S(2)}, u32[]{:S(2)}) collective-permute-start(bf16[384,256]{1,0:T(8,128)(2,1)S(1)} %collective-permute-done.2.refs_2_), channel_id=1, source_target_pairs={{0,224},{1,225},{2,226},{3,227},{4,228},{5,229},{6,230},{7,231},{8... | collective-permute-start | bytes 589832 | tf_op jit(solution)/shard_map/ppermute | solution.py:34
  17.8 7.3 %collective-permute-start.6 = (bf16[384,256]{1,0:T(8,128)(2,1)S(1)}, bf16[384,256]{1,0:T(8,128)(2,1)S(1)}, u32[]{:S(2)}, u32[]{:S(2)}) collective-permute-start(bf16[384,256]{1,0:T(8,128)(2,1)S(1)} %collective-permute-done.3.refs_3_), channel_id=1, source_target_pairs={{0,32},{1,33},{2,34},{3,35},{4,36},{5,37},{6,38},{7,39},{8,40},{9,... | collective-permute-start | bytes 589832 | tf_op jit(solution)/shard_map/ppermute | solution.py:34
  17.9 8.0 %collective-permute-start.8 = (bf16[384,256]{1,0:T(8,128)(2,1)S(1)}, bf16[384,256]{1,0:T(8,128)(2,1)S(1)}, u32[]{:S(2)}, u32[]{:S(2)}) collective-permute-start(bf16[384,256]{1,0:T(8,128)(2,1)S(1)} %maximum_maximum_fusion.1.refs_0_), channel_id=1, source_target_pairs={{0,8},{1,9},{2,10},{3,11},{4,12},{5,13},{6,14},{7,15},{8,0},{9,1},... | collective-permute-start | bytes 589832 | tf_op jit(solution)/shard_map/ppermute | solution.py:34
  19.4 6.6 %collective-permute-start.9 = (bf16[384,256]{1,0:T(8,128)(2,1)S(1)}, bf16[384,256]{1,0:T(8,128)(2,1)S(1)}, u32[]{:S(2)}, u32[]{:S(2)}) collective-permute-start(bf16[384,256]{1,0:T(8,128)(2,1)S(1)} %collective-permute-done.2.refs_2_), channel_id=1, source_target_pairs={{0,8},{1,9},{2,10},{3,11},{4,12},{5,13},{6,14},{7,15},{8,0},{9,1},... | collective-permute-start | bytes 589832 | tf_op jit(solution)/shard_map/ppermute | solution.py:34
  24.3 3.0 %collective-permute-start.10 = (bf16[384,256]{1,0:T(8,128)(2,1)S(1)}, bf16[384,256]{1,0:T(8,128)(2,1)S(1)}, u32[]{:S(2)}, u32[]{:S(2)}) collective-permute-start(bf16[384,256]{1,0:T(8,128)(2,1)S(1)} %collective-permute-done.3.refs_3_), channel_id=1, source_target_pairs={{0,8},{1,9},{2,10},{3,11},{4,12},{5,13},{6,14},{7,15},{8,0},{9,1},... | collective-permute-start | bytes 589832 | tf_op jit(solution)/shard_map/ppermute | solution.py:34
  25.2 5.0 %collective-permute-start.12 = (bf16[384,256]{1,0:T(8,128)(2,1)S(1)}, bf16[384,256]{1,0:T(8,128)(2,1)S(1)}, u32[]{:S(2)}, u32[]{:S(2)}) collective-permute-start(bf16[384,256]{1,0:T(8,128)(2,1)S(1)} %collective-permute-done.4.refs_7_), channel_id=1, source_target_pairs={{0,8},{1,9},{2,10},{3,11},{4,12},{5,13},{6,14},{7,15},{8,0},{9,1},... | collective-permute-start | bytes 589832 | tf_op jit(solution)/shard_map/ppermute | solution.py:34
  25.2 5.8 %collective-permute-start.11 = (bf16[384,256]{1,0:T(8,128)(2,1)S(1)}, bf16[384,256]{1,0:T(8,128)(2,1)S(1)}, u32[]{:S(2)}, u32[]{:S(2)}) collective-permute-start(bf16[384,256]{1,0:T(8,128)(2,1)S(1)} %collective-permute-done.6.refs_6_), channel_id=1, source_target_pairs={{0,8},{1,9},{2,10},{3,11},{4,12},{5,13},{6,14},{7,15},{8,0},{9,1},... | collective-permute-start | bytes 589832 | tf_op jit(solution)/shard_map/ppermute | solution.py:34
  25.9 11.7 %collective-permute-start.5 = (bf16[384,256]{1,0:T(8,128)(2,1)S(1)}, bf16[384,256]{1,0:T(8,128)(2,1)S(1)}, u32[]{:S(2)}, u32[]{:S(2)}) collective-permute-start(bf16[384,256]{1,0:T(8,128)(2,1)S(1)} %collective-permute-done.4.refs_7_), channel_id=1, source_target_pairs={{0,32},{1,33},{2,34},{3,35},{4,36},{5,37},{6,38},{7,39},{8,40},{9,... | collective-permute-start | bytes 589832 | tf_op jit(solution)/shard_map/ppermute | solution.py:34
  26.0 11.6 %collective-permute-start.7 = (bf16[384,256]{1,0:T(8,128)(2,1)S(1)}, bf16[384,256]{1,0:T(8,128)(2,1)S(1)}, u32[]{:S(2)}, u32[]{:S(2)}) collective-permute-start(bf16[384,256]{1,0:T(8,128)(2,1)S(1)} %collective-permute-done.6.refs_6_), channel_id=1, source_target_pairs={{0,224},{1,225},{2,226},{3,227},{4,228},{5,229},{6,230},{7,231},{8... | collective-permute-start | bytes 589832 | tf_op jit(solution)/shard_map/ppermute | solution.py:34
  27.3 10.3 %collective-permute-start.14 = (bf16[256,512]{1,0:T(8,128)(2,1)S(1)}, bf16[256,512]{1,0:T(8,128)(2,1)S(1)}, u32[]{:S(2)}, u32[]{:S(2)}) collective-permute-start(bf16[256,512]{1,0:T(8,128)(2,1)S(1)} %get-tuple-element.63), channel_id=1, source_target_pairs={{0,16},{1,17},{2,18},{3,19},{4,20},{5,21},{6,22},{7,23},{8,24},{9,... | collective-permute-start | bytes 786440 | tf_op jit(solution)/shard_map/ppermute | solution.py:34
  30.2 12.4 %collective-permute-start.16 = (bf16[256,512]{1,0:T(8,128)(2,1)S(1)}, bf16[256,512]{1,0:T(8,128)(2,1)S(1)}, u32[]{:S(2)}, u32[]{:S(2)}) collective-permute-start(bf16[256,512]{1,0:T(8,128)(2,1)S(1)} %get-tuple-element.63), channel_id=1, source_target_pairs={{0,17},{1,16},{2,19},{3,18},{4,21},{5,20},{6,23},{7,22},{8,25},{9,... | collective-permute-start | bytes 786440 | tf_op jit(solution)/shard_map/ppermute | solution.py:34
  31.0 11.7 %collective-permute-start.15 = (bf16[256,512]{1,0:T(8,128)(2,1)S(1)}, bf16[256,512]{1,0:T(8,128)(2,1)S(1)}, u32[]{:S(2)}, u32[]{:S(2)}) collective-permute-start(bf16[256,512]{1,0:T(8,128)(2,1)S(1)} %get-tuple-element.52), channel_id=1, source_target_pairs={{0,1},{1,0},{2,3},{3,2},{4,5},{5,4},{6,7},{7,6},{8,9},{9,8},{10,11... | collective-permute-start | bytes 786440 | tf_op jit(solution)/shard_map/ppermute | solution.py:34
  42.6 11.9 %collective-permute-start.19 = (bf16[384,256]{1,0:T(8,128)(2,1)S(1)}, bf16[384,256]{1,0:T(8,128)(2,1)S(1)}, u32[]{:S(2)}, u32[]{:S(2)}) collective-permute-start(bf16[384,256]{1,0:T(8,128)(2,1)S(1)} %collective-permute-done.7.refs_1_), channel_id=1, source_target_pairs={{0,32},{1,33},{2,34},{3,35},{4,36},{5,37},{6,38},{7,39},{8,40},{9,... | collective-permute-start | bytes 589832 | tf_op jit(solution)/shard_map/ppermute | solution.py:34
  43.6 41.0 %collective-permute-start.22 = (bf16[512,1024]{1,0:T(8,128)(2,1)S(1)}, bf16[512,1024]{1,0:T(8,128)(2,1)S(1)}, u32[]{:S(2)}, u32[]{:S(2)}) collective-permute-start(bf16[512,1024]{1,0:T(8,128)(2,1)S(1)} %maximum_maximum_fusion.refs_5_.refs_3_), channel_id=1, source_target_pairs={{0,6},{1,7},{2,0},{3,1},{4,2},{5,3},{6,4},{7,5},{8,14},{9,15},{10,... | collective-permute-start | bytes 3145736 | tf_op jit(solution)/shard_map/ppermute | solution.py:34
  46.2 38.5 %collective-permute-start.21 = (bf16[512,1024]{1,0:T(8,128)(2,1)S(1)}, bf16[512,1024]{1,0:T(8,128)(2,1)S(1)}, u32[]{:S(2)}, u32[]{:S(2)}) collective-permute-start(bf16[512,1024]{1,0:T(8,128)(2,1)S(1)} %maximum_maximum_fusion.refs_5_.refs_3_), channel_id=1, source_target_pairs={{0,2},{1,3},{2,4},{3,5},{4,6},{5,7},{6,0},{7,1},{8,10},{9,11},{10,... | collective-permute-start | bytes 3145736 | tf_op jit(solution)/shard_map/ppermute | solution.py:34
  52.9 3.0 %collective-permute-start.18 = (bf16[384,256]{1,0:T(8,128)(2,1)S(1)}, bf16[384,256]{1,0:T(8,128)(2,1)S(1)}, u32[]{:S(2)}, u32[]{:S(2)}) collective-permute-start(bf16[384,256]{1,0:T(8,128)(2,1)S(1)} %collective-permute-done.7.refs_1_), channel_id=1, source_target_pairs={{0,8},{1,9},{2,10},{3,11},{4,12},{5,13},{6,14},{7,15},{8,0},{9,1},... | collective-permute-start | bytes 589832 | tf_op jit(solution)/shard_map/ppermute | solution.py:34
  84.7 7.3 %collective-permute-start.24 = (bf16[64,2048]{1,0:T(8,128)(2,1)S(1)}, bf16[64,2048]{1,0:T(8,128)(2,1)S(1)}, u32[]{:S(2)}, u32[]{:S(2)}) collective-permute-start(bf16[64,2048]{1,0:T(8,128)(2,1)S(1)} %shard_map.76.refs_0_), channel_id=1, source_target_pairs={{0,224},{1,225},{2,226},{3,227},{4,228},{5,229},{6,230},{7,231},{8... | collective-permute-start | bytes 786440 | tf_op jit(solution)/shard_map/ppermute | solution.py:34
  86.0 8.8 %collective-permute-start.23 = (bf16[64,2048]{1,0:T(8,128)(2,1)S(1)}, bf16[64,2048]{1,0:T(8,128)(2,1)S(1)}, u32[]{:S(2)}, u32[]{:S(2)}) collective-permute-start(bf16[64,2048]{1,0:T(8,128)(2,1)S(1)} %shard_map.76.refs_0_), channel_id=1, source_target_pairs={{0,32},{1,33},{2,34},{3,35},{4,36},{5,37},{6,38},{7,39},{8,40},{9,... | collective-permute-start | bytes 786440 | tf_op jit(solution)/shard_map/ppermute | solution.py:34
  92.0 5.2 %collective-permute-start.25 = (bf16[64,2048]{1,0:T(8,128)(2,1)S(1)}, bf16[64,2048]{1,0:T(8,128)(2,1)S(1)}, u32[]{:S(2)}, u32[]{:S(2)}) collective-permute-start(bf16[64,2048]{1,0:T(8,128)(2,1)S(1)} %collective-permute-done.24.refs_2_), channel_id=1, source_target_pairs={{0,32},{1,33},{2,34},{3,35},{4,36},{5,37},{6,38},{7,39},{8,40},{9,... | collective-permute-start | bytes 786440 | tf_op jit(solution)/shard_map/ppermute | solution.py:34
  92.1 14.1 %collective-permute-start.27 = (bf16[256,1024]{1,0:T(8,128)(2,1)S(1)}, bf16[256,1024]{1,0:T(8,128)(2,1)S(1)}, u32[]{:S(2)}, u32[]{:S(2)}) collective-permute-start(bf16[256,1024]{1,0:T(8,128)(2,1)S(1)} %slice.14), channel_id=1, source_target_pairs={{0,2},{1,3},{2,4},{3,5},{4,6},{5,7},{6,0},{7,1},{8,10},{9,11},{10,... | collective-permute-start | bytes 1572872 | tf_op jit(solution)/shard_map/ppermute | solution.py:34
  92.2 14.0 %collective-permute-start.28 = (bf16[256,1024]{1,0:T(8,128)(2,1)S(1)}, bf16[256,1024]{1,0:T(8,128)(2,1)S(1)}, u32[]{:S(2)}, u32[]{:S(2)}) collective-permute-start(bf16[256,1024]{1,0:T(8,128)(2,1)S(1)} %slice.15), channel_id=1, source_target_pairs={{0,6},{1,7},{2,0},{3,1},{4,2},{5,3},{6,4},{7,5},{8,14},{9,15},{10,... | collective-permute-start | bytes 1572872 | tf_op jit(solution)/shard_map/ppermute | solution.py:34
  94.8 6.7 %collective-permute-start.26 = (bf16[64,2048]{1,0:T(8,128)(2,1)S(1)}, bf16[64,2048]{1,0:T(8,128)(2,1)S(1)}, u32[]{:S(2)}, u32[]{:S(2)}) collective-permute-start(bf16[64,2048]{1,0:T(8,128)(2,1)S(1)} %collective-permute-done.23.refs_1_), channel_id=1, source_target_pairs={{0,224},{1,225},{2,226},{3,227},{4,228},{5,229},{6,230},{7,231},{8... | collective-permute-start | bytes 786440 | tf_op jit(solution)/shard_map/ppermute | solution.py:34
  97.2 9.0 %collective-permute-start.31 = (bf16[64,2048]{1,0:T(8,128)(2,1)S(1)}, bf16[64,2048]{1,0:T(8,128)(2,1)S(1)}, u32[]{:S(2)}, u32[]{:S(2)}) collective-permute-start(bf16[64,2048]{1,0:T(8,128)(2,1)S(1)} %collective-permute-done.25.refs_3_), channel_id=1, source_target_pairs={{0,224},{1,225},{2,226},{3,227},{4,228},{5,229},{6,230},{7,231},{8... | collective-permute-start | bytes 786440 | tf_op jit(solution)/shard_map/ppermute | solution.py:34
  101.6 12.4 %collective-permute-start.30 = (bf16[64,2048]{1,0:T(8,128)(2,1)S(1)}, bf16[64,2048]{1,0:T(8,128)(2,1)S(1)}, u32[]{:S(2)}, u32[]{:S(2)}) collective-permute-start(bf16[64,2048]{1,0:T(8,128)(2,1)S(1)} %collective-permute-done.26.refs_4_), channel_id=1, source_target_pairs={{0,32},{1,33},{2,34},{3,35},{4,36},{5,37},{6,38},{7,39},{8,40},{9,... | collective-permute-start | bytes 786440 | tf_op jit(solution)/shard_map/ppermute | solution.py:34
  106.2 7.8 %collective-permute-start.32 = (bf16[64,2048]{1,0:T(8,128)(2,1)S(1)}, bf16[64,2048]{1,0:T(8,128)(2,1)S(1)}, u32[]{:S(2)}, u32[]{:S(2)}) collective-permute-start(bf16[64,2048]{1,0:T(8,128)(2,1)S(1)} %collective-permute-done.31.refs_1_), channel_id=1, source_target_pairs={{0,32},{1,33},{2,34},{3,35},{4,36},{5,37},{6,38},{7,39},{8,40},{9,... | collective-permute-start | bytes 786440 | tf_op jit(solution)/shard_map/ppermute | solution.py:34
  109.2 11.0 %collective-permute-start.29 = (bf16[320,512]{1,0:T(8,128)(2,1)S(1)}, bf16[320,512]{1,0:T(8,128)(2,1)S(1)}, u32[]{:S(2)}, u32[]{:S(2)}) collective-permute-start(bf16[320,512]{1,0:T(8,128)(2,1)S(1)} %get-tuple-element.60), channel_id=1, source_target_pairs={{0,8},{1,9},{2,10},{3,11},{4,12},{5,13},{6,14},{7,15},{8,0},{9,1},... | collective-permute-start | bytes 983048 | tf_op jit(solution)/shard_map/ppermute | solution.py:34
  116.3 4.9 %collective-permute-start.33 = (bf16[192,512]{1,0:T(8,128)(2,1)S(1)}, bf16[192,512]{1,0:T(8,128)(2,1)S(1)}, u32[]{:S(2)}, u32[]{:S(2)}) collective-permute-start(bf16[192,512]{1,0:T(8,128)(2,1)S(1)} %get-tuple-element.62), channel_id=1, source_target_pairs={{0,8},{1,9},{2,10},{3,11},{4,12},{5,13},{6,14},{7,15},{8,0},{9,1},... | collective-permute-start | bytes 589832 | tf_op jit(solution)/shard_map/ppermute | solution.py:34
  (4 other events, 23.7 us)

commit v5 on v4

--- a/solution.py
+++ b/solution.py
@@ -217,47 +217,36 @@
 
 def project_kernel(count, *refs):
     blocks, weights, (keep, send) = refs[:count], refs[count:-2], refs[-2:]
-    total, at = None, 0
-    for weight in weights:
-        depth = weight.shape[0]
-        a = jnp.concatenate([block[:, at : at + depth] for block in blocks], 0)
-        term = jnp.dot(a, weight[...], preferred_element_type=F32)
-        total = term if total is None else total + term
-        at += depth
-
-    @pl.when(pl.program_id(0) < NY)
-    def _():
-        keep[...] = total
-
-    @pl.when(pl.program_id(0) >= NY)
-    def _():
-        send[...] = total.astype(BF16)
+    tile = weights[0].shape[1] // (NY * NC)
+    for column in range(NY * NC):
+        half, core = column // NC, column % NC
+        total, at = None, 0
+        for weight in weights:
+            depth = weight.shape[0]
+            a = jnp.concatenate([block[:, at : at + depth] for block in blocks], 0)
+            b = weight[:, column * tile : (column + 1) * tile]
+            term = jnp.dot(a, b, preferred_element_type=F32)
+            total = term if total is None else total + term
+            at += depth
+        out = keep if core == 0 else send
+        out[:, half * tile : (half + 1) * tile] = total.astype(out.dtype)
 
 
 def project(blocks, weights):
-    rows = blocks[0].shape[0] * len(blocks)
+    rows, depth = blocks[0].shape[0] * len(blocks), blocks[0].shape[1]
     width = weights[0].shape[1]
-    tile = width // (NY * NC)
-    place = lambda j: j % NY * NC + j // NY
-    whole = pl.BlockSpec(blocks[0].shape, lambda j: (0, 0))
+    whole = pl.BlockSpec(memory_space=pltpu.VMEM)
     return pl.pallas_call(
         functools.partial(project_kernel, len(blocks)),
-        grid=(NC * NY,),
-        in_specs=[whole] * len(blocks)
-        + [pl.BlockSpec((weight.shape[0], tile), lambda j: (0, place(j))) for weight in weights],
-        out_specs=[
-            pl.BlockSpec((rows, tile), lambda j: (0, jnp.minimum(j, NY - 1))),
-            pl.BlockSpec((rows, tile), lambda j: (0, jnp.maximum(j - NY, 0))),
-        ],
+        in_specs=[whole] * (len(blocks) + len(weights)),
+        out_specs=[whole, whole],
         out_shape=[
-            jax.ShapeDtypeStruct((rows, NY * tile), F32),
-            jax.ShapeDtypeStruct((rows, NY * tile), BF16),
+            jax.ShapeDtypeStruct((rows, width // NC), F32),
+            jax.ShapeDtypeStruct((rows, width // NC), BF16),
         ],
         compiler_params=pltpu.CompilerParams(vmem_limit_bytes=VMEM),
         cost_estimate=pl.CostEstimate(
-            flops=2 * rows * blocks[0].shape[1] * width,
-            bytes_accessed=2 * blocks[0].shape[1] * width,
-            transcendentals=0,
+            flops=2 * rows * depth * width, bytes_accessed=2 * depth * width, transcendentals=0
         ),
     )(*blocks, *weights)
 
@@ -330,13 +319,14 @@
     blocks += both(ahead, behind, 2)
     ahead, behind = meet_up(behind), meet_down(ahead)
     low = attend(meta, cache_lengths, q, blocks, 0, None, cache, fresh)
-    ahead, behind, low, quarters = lax.optimization_barrier((ahead, behind, low, quarters))
+    ahead, behind, low = lax.optimization_barrier((ahead, behind, low))
+    last_blocks = both(ahead, behind, 3)
+    ahead = meet_up(behind)
+    low, quarters = lax.optimization_barrier((low, quarters))
     wide = jnp.concatenate(
         [jnp.concatenate(quarters[:2], 1), jnp.concatenate(quarters[2:], 1)], 0
     )
     wide_f, wide_b = shift_x(wide, 1), shift_x(wide, -1)
-    last_blocks = both(ahead, behind, 3)
-    ahead = meet_up(behind)
     high = attend(meta, cache_lengths, q, blocks, 1, None, cache, fresh)
     ahead, high = lax.optimization_barrier((ahead, high))
     last_blocks += [(ahead, 0, 4, 0), (swap(ahead, b=1), 0, 4, 1)]

time: 138 us -> 135 us (0.978)
  starting transfers between devices: 41.5 us -> 47.2 us
  waiting for transfers between devices: 29 us -> 24.5 us
  Pallas kernels: 29.6 us -> 26.6 us
  blocking collectives: 33.3 us -> 31.5 us
    ppermute x34, starting transfers between devices: 41.5 us -> 47.2 us  [permute(): return lax.ppermute(value, AXES, pairs)]
    ppermute x34, waiting for transfers between devices: 29 us -> 24.5 us  [permute(): return lax.ppermute(value, AXES, pairs)]
    pallas_call x2, Pallas kernels: 5.32 us -> 2.5 us  [project(): pl.pallas_call(functools.partial(project_kernel, len(blocks)), in_specs=[...]
    all_to_all x1, blocking collectives: 18.1 us -> 16.7 us  [shards(): lax.all_to_all(pieces.reshape(NY * NZ, group, width), ('yh', 'x', 'yl'),...]
  transfers between devices with their start and end apart: 34 -> 34, of which waited for: 12 -> 13; matrix products, arithmetic and copies ran while one was open for 2% -> 2% of each run, Pallas kernels for 21% -> 19%
where the time goes in v5:
time: 135 us; the launch traced here: 134 us
  starting transfers between devices  47.2 us (35%)
  blocking collectives  31.5 us (23%)
  Pallas kernels  26.6 us (20%)
  waiting for transfers between devices  24.5 us (18%)
  other arithmetic  2.97 us (2%)
    ppermute x34, starting transfers between devices, permute(): return lax.ppermute(value, AXES, pairs)  47.2 us
    ppermute x34, waiting for transfers between devices, permute(): return lax.ppermute(value, AXES, pairs)  24.5 us
    pallas_call x3, Pallas kernels, attend(): pl.pallas_call(functools.partial(attend_kernel, tuple((entry[1:] for entr...  22.3 us
    all_to_all x1, blocking collectives, shards(): lax.all_to_all(pieces.reshape(NY * NZ, group, width), ('yh', 'x', 'yl'),...  16.7 us
    all_to_all x1, blocking collectives, shards(): lax.all_to_all(settled.reshape(NY * NZ, rows, width), ('yh', 'x', 'yl'),...  14.8 us
  transfers between devices with their start and end apart: 34, of which 13 were waited for; matrix products, arithmetic and copies ran while one was open for 2% of the time, Pallas kernels for 19%

profile of v5, /device:TPU:1, one launch (start us, length us, event | category | flops | bytes accessed | tf_op | source)
XLA Modules:
  0.0 134.3 jit_solution(17379533440147666666)
XLA Ops:
  1.0 3.3 %collective-permute-start = (bf16[128,512]{1,0:T(8,128)(2,1)S(1)}, bf16[128,512]{1,0:T(8,128)(2,1)S(1)}, u32[]{:S(2)}, u32[]{:S(2)}) collective-permute-start(bf16[128,512]{1,0:T(8,128)(2,1)S(1)} %constant_dynamic-slice_fusion.2), channel_id=1, source_target_pairs={{0,8},{1,9},{2,10},{3,11},{4,12},{5,13},{6,14},{7,15},{8,0},{9,1},... | collective-permute-start | bytes 393224 | tf_op jit(solution)/shard_map/ppermute | solution.py:34
  5.3 4.6 %collective-permute-start.3 = (bf16[384,256]{1,0:T(8,128)(2,1)S(1)}, bf16[384,256]{1,0:T(8,128)(2,1)S(1)}, u32[]{:S(2)}, u32[]{:S(2)}) collective-permute-start(bf16[384,256]{1,0:T(8,128)(2,1)S(1)} %maximum_maximum_fusion.1.refs_0_), channel_id=1, source_target_pairs={{0,224},{1,225},{2,226},{3,227},{4,228},{5,229},{6,230},{7,231},{8... | collective-permute-start | bytes 589832 | tf_op jit(solution)/shard_map/ppermute | solution.py:34
  10.9 3.0 %collective-permute-start.1 = (bf16[256,512]{1,0:T(8,128)(2,1)S(1)}, bf16[256,512]{1,0:T(8,128)(2,1)S(1)}, u32[]{:S(2)}, u32[]{:S(2)}) collective-permute-start(bf16[256,512]{1,0:T(8,128)(2,1)S(1)} %pad_maximum_fusion.1), channel_id=1, source_target_pairs={{0,16},{1,17},{2,18},{3,19},{4,20},{5,21},{6,22},{7,23},{8,24},{9,... | collective-permute-start | bytes 786440 | tf_op jit(solution)/shard_map/ppermute | solution.py:34
  13.9 1.1 collective-permute-done.3.refs_3_
  15.9 2.7 %collective-permute-start.4 = (bf16[384,256]{1,0:T(8,128)(2,1)S(1)}, bf16[384,256]{1,0:T(8,128)(2,1)S(1)}, u32[]{:S(2)}, u32[]{:S(2)}) collective-permute-start(bf16[384,256]{1,0:T(8,128)(2,1)S(1)} %collective-permute-done.2.refs_2_), channel_id=1, source_target_pairs={{0,224},{1,225},{2,226},{3,227},{4,228},{5,229},{6,230},{7,231},{8... | collective-permute-start | bytes 589832 | tf_op jit(solution)/shard_map/ppermute | solution.py:34
  19.8 1.4 %collective-permute-start.9 = (bf16[384,256]{1,0:T(8,128)(2,1)S(1)}, bf16[384,256]{1,0:T(8,128)(2,1)S(1)}, u32[]{:S(2)}, u32[]{:S(2)}) collective-permute-start(bf16[384,256]{1,0:T(8,128)(2,1)S(1)} %collective-permute-done.2.refs_2_), channel_id=1, source_target_pairs={{0,8},{1,9},{2,10},{3,11},{4,12},{5,13},{6,14},{7,15},{8,0},{9,1},... | collective-permute-start | bytes 589832 | tf_op jit(solution)/shard_map/ppermute | solution.py:34
  21.2 2.4 %collective-permute-done.4.refs_7_ = bf16[384,256]{1,0:T(8,128)(2,1)S(1)} collective-permute-done((bf16[384,256]{1,0:T(8,128)(2,1)S(1)}, bf16[384,256]{1,0:T(8,128)(2,1)S(1)}, u32[]{:S(2)}, u32[]{:S(2)}) %collective-permute-start.4) | collective-permute-done | bytes 196640 | tf_op jit(solution)/shard_map/ppermute | solution.py:34
  24.7 1.2 collective-permute-start.11
  26.2 1.8 %collective-permute-start.7 = (bf16[384,256]{1,0:T(8,128)(2,1)S(1)}, bf16[384,256]{1,0:T(8,128)(2,1)S(1)}, u32[]{:S(2)}, u32[]{:S(2)}) collective-permute-start(bf16[384,256]{1,0:T(8,128)(2,1)S(1)} %collective-permute-done.6.refs_6_), channel_id=1, source_target_pairs={{0,224},{1,225},{2,226},{3,227},{4,228},{5,229},{6,230},{7,231},{8... | collective-permute-start | bytes 589832 | tf_op jit(solution)/shard_map/ppermute | solution.py:34
  28.0 2.9 %collective-permute-start.18 = (bf16[256,512]{1,0:T(8,128)(2,1)S(1)}, bf16[256,512]{1,0:T(8,128)(2,1)S(1)}, u32[]{:S(2)}, u32[]{:S(2)}) collective-permute-start(bf16[256,512]{1,0:T(8,128)(2,1)S(1)} %get-tuple-element.69), channel_id=1, source_target_pairs={{0,16},{1,17},{2,18},{3,19},{4,20},{5,21},{6,22},{7,23},{8,24},{9,... | collective-permute-start | bytes 786440 | tf_op jit(solution)/shard_map/ppermute | solution.py:34
  31.8 6.5 %shard_map.73 = (f32[512,256]{1,0:T(8,128)S(1)}, f32[512,256]{1,0:T(8,128)S(1)}, f32[512,256]{1,0:T(8,128)S(1)}) custom-call(s32[5]{0:T(128)S(1)} %stack.23.meta, s32[32]{0:T(128)S(1)} %copy-done, bf16[512,512]{1,0:T(8,128)(2,1)S(1)} %pad_maximum_fusion.q_ref, bf16[384,256]{1,0:T(8,128)(2,1)S(1)} %maximum_maximum_fusion.1.refs_0_, ...), custom_call_target="tpu_custom_call" | custom-call | flops 2013265920 | bytes 1048576 | tf_op jit(solution)/shard_map/pallas_call | solution.py:168
  39.3 1.1 collective-permute-start.15
  40.8 2.3 %collective-permute-done.19 = bf16[256,512]{1,0:T(8,128)(2,1)S(1)} collective-permute-done((bf16[256,512]{1,0:T(8,128)(2,1)S(1)}, bf16[256,512]{1,0:T(8,128)(2,1)S(1)}, u32[]{:S(2)}, u32[]{:S(2)}) %collective-permute-start.19) | collective-permute-done | bytes 262176 | tf_op jit(solution)/shard_map/ppermute | solution.py:34
  43.5 1.3 collective-permute-start.21
  44.8 1.5 %collective-permute-start.22 = (bf16[512,1024]{1,0:T(8,128)(2,1)S(1)}, bf16[512,1024]{1,0:T(8,128)(2,1)S(1)}, u32[]{:S(2)}, u32[]{:S(2)}) collective-permute-start(bf16[512,1024]{1,0:T(8,128)(2,1)S(1)} %maximum_maximum_fusion.refs_5_.refs_3_), channel_id=1, source_target_pairs={{0,6},{1,7},{2,0},{3,1},{4,2},{5,3},{6,4},{7,5},{8,14},{9,15},{10,... | collective-permute-start | bytes 3145736 | tf_op jit(solution)/shard_map/ppermute | solution.py:34
  46.2 6.6 %shard_map.74 = (f32[512,256]{1,0:T(8,128)S(1)}, f32[512,256]{1,0:T(8,128)S(1)}, f32[512,256]{1,0:T(8,128)S(1)}) custom-call(s32[5]{0:T(128)S(1)} %stack.23.meta, s32[32]{0:T(128)S(1)} %copy-done, bf16[512,512]{1,0:T(8,128)(2,1)S(1)} %pad_maximum_fusion.q_ref, bf16[384,256]{1,0:T(8,128)(2,1)S(1)} %maximum_maximum_fusion.1.refs_0_, ...), custom_call_target="tpu_custom_call" | custom-call | flops 2013265920 | bytes 1048576 | tf_op jit(solution)/shard_map/pallas_call | solution.py:168
  52.9 1.8 %collective-permute-start.16 = (bf16[384,256]{1,0:T(8,128)(2,1)S(1)}, bf16[384,256]{1,0:T(8,128)(2,1)S(1)}, u32[]{:S(2)}, u32[]{:S(2)}) collective-permute-start(bf16[384,256]{1,0:T(8,128)(2,1)S(1)} %collective-permute-done.15.refs_4_), channel_id=1, source_target_pairs={{0,8},{1,9},{2,10},{3,11},{4,12},{5,13},{6,14},{7,15},{8,0},{9,1},... | collective-permute-start | bytes 589832 | tf_op jit(solution)/shard_map/ppermute | solution.py:34
  54.6 1.1 collective-permute-done.16.refs_5_
  55.7 9.2 %shard_map.75 = bf16[2,8,80,256]{3,2,1,0:T(8,128)(2,1)S(1)} custom-call(s32[5]{0:T(128)S(1)} %stack.23.meta, s32[32]{0:T(128)S(1)} %copy-done, bf16[512,512]{1,0:T(8,128)(2,1)S(1)} %pad_maximum_fusion.q_ref, bf16[384,256]{1,0:T(8,128)(2,1)S(1)} %collective-permute-done.5.refs_0_, bf16[384,256]{1,0:T(8,128)(2,1)S(1)} %collective-permute-done.7.refs_1_, ...), custom_call_target="tpu_custom_call" | custom-call | flops 2415919104 | bytes 1048576 | tf_op jit(solution)/shard_map/pallas_call | solution.py:168
  64.9 16.7 %all_to_all.10.pieces = bf16[16,80,256]{2,1,0:T(8,128)(2,1)S(1)} all-to-all(bf16[16,80,256]{2,1,0:T(8,128)(2,1)S(1)} %bitcast.9), channel_id=1, replica_groups=mesh['z'=8,'yh'=2,'core'=2,'x'=4,'yl'=2] {'yh','x','yl'}, dimensions={0} | all-to-all | bytes 1310720 | tf_op jit(solution)/shard_map/all_to_all | solution.py:336
  81.6 1.2 shard_map.76.refs_0_
  83.9 6.1 %collective-permute-done.24.refs_2_ = bf16[64,2048]{1,0:T(8,128)(2,1)S(1)} collective-permute-done((bf16[64,2048]{1,0:T(8,128)(2,1)S(1)}, bf16[64,2048]{1,0:T(8,128)(2,1)S(1)}, u32[]{:S(2)}, u32[]{:S(2)}) %collective-permute-start.24) | collective-permute-done | bytes 262176 | tf_op jit(solution)/shard_map/ppermute | solution.py:34
  90.2 2.7 %collective-permute-start.28 = (bf16[256,1024]{1,0:T(8,128)(2,1)S(1)}, bf16[256,1024]{1,0:T(8,128)(2,1)S(1)}, u32[]{:S(2)}, u32[]{:S(2)}) collective-permute-start(bf16[256,1024]{1,0:T(8,128)(2,1)S(1)} %slice.15), channel_id=1, source_target_pairs={{0,6},{1,7},{2,0},{3,1},{4,2},{5,3},{6,4},{7,5},{8,14},{9,15},{10,... | collective-permute-start | bytes 1572872 | tf_op jit(solution)/shard_map/ppermute | solution.py:34
  93.9 1.4 %collective-permute-done.25.refs_3_ = bf16[64,2048]{1,0:T(8,128)(2,1)S(1)} collective-permute-done((bf16[64,2048]{1,0:T(8,128)(2,1)S(1)}, bf16[64,2048]{1,0:T(8,128)(2,1)S(1)}, u32[]{:S(2)}, u32[]{:S(2)}) %collective-permute-start.25) | collective-permute-done | bytes 262176 | tf_op jit(solution)/shard_map/ppermute | solution.py:34
  95.3 1.1 collective-permute-start.31
  96.4 3.4 %collective-permute-done.26.refs_4_ = bf16[64,2048]{1,0:T(8,128)(2,1)S(1)} collective-permute-done((bf16[64,2048]{1,0:T(8,128)(2,1)S(1)}, bf16[64,2048]{1,0:T(8,128)(2,1)S(1)}, u32[]{:S(2)}, u32[]{:S(2)}) %collective-permute-start.26) | collective-permute-done | bytes 262176 | tf_op jit(solution)/shard_map/ppermute | solution.py:34
  100.0 4.4 %collective-permute-done.31.refs_1_ = bf16[64,2048]{1,0:T(8,128)(2,1)S(1)} collective-permute-done((bf16[64,2048]{1,0:T(8,128)(2,1)S(1)}, bf16[64,2048]{1,0:T(8,128)(2,1)S(1)}, u32[]{:S(2)}, u32[]{:S(2)}) %collective-permute-start.31) | collective-permute-done | bytes 262176 | tf_op jit(solution)/shard_map/ppermute | solution.py:34
  104.4 1.5 %shard_map.77 = (f32[320,512]{1,0:T(8,128)S(1)}, bf16[320,512]{1,0:T(8,128)(2,1)S(1)}) custom-call(bf16[64,2048]{1,0:T(8,128)(2,1)S(1)} %shard_map.76.refs_0_, bf16[64,2048]{1,0:T(8,128)(2,1)S(1)} %collective-permute-done.23.refs_1_, bf16[64,2048]{1,0:T(8,128)(2,1)S(1)} %collective-permute-done.24.refs_2_, ...), custom_call_target="tpu_custom_call" | custom-call | flops 1342177280 | bytes 4194304 | tf_op jit(solution)/shard_map/pallas_call | solution.py:239
  105.9 4.8 %collective-permute-start.29 = (bf16[320,512]{1,0:T(8,128)(2,1)S(1)}, bf16[320,512]{1,0:T(8,128)(2,1)S(1)}, u32[]{:S(2)}, u32[]{:S(2)}) collective-permute-start(bf16[320,512]{1,0:T(8,128)(2,1)S(1)} %get-tuple-element.66), channel_id=1, source_target_pairs={{0,8},{1,9},{2,10},{3,11},{4,12},{5,13},{6,14},{7,15},{8,0},{9,1},... | collective-permute-start | bytes 983048 | tf_op jit(solution)/shard_map/ppermute | solution.py:34
  111.8 5.2 %collective-permute-start.33 = (bf16[192,512]{1,0:T(8,128)(2,1)S(1)}, bf16[192,512]{1,0:T(8,128)(2,1)S(1)}, u32[]{:S(2)}, u32[]{:S(2)}) collective-permute-start(bf16[192,512]{1,0:T(8,128)(2,1)S(1)} %get-tuple-element.68), channel_id=1, source_target_pairs={{0,8},{1,9},{2,10},{3,11},{4,12},{5,13},{6,14},{7,15},{8,0},{9,1},... | collective-permute-start | bytes 589832 | tf_op jit(solution)/shard_map/ppermute | solution.py:34
  117.0 1.1 collective-permute-done.33.refs_3_
  118.7 14.8 %all_to_all.11 = bf16[16,64,256]{2,1,0:T(8,128)(2,1)S(1)} all-to-all(bf16[16,64,256]{2,1,0:T(8,128)(2,1)S(1)} %bitcast.8), channel_id=1, replica_groups=mesh['z'=8,'yh'=2,'core'=2,'x'=4,'yl'=2] {'yh','x','yl'}, dimensions={0} | all-to-all | bytes 1048576 | tf_op jit(solution)/shard_map/all_to_all | solution.py:358
  (62 shorter events, 14.1 us)
Async XLA Ops:
  1.0 8.9 %collective-permute-start = (bf16[128,512]{1,0:T(8,128)(2,1)S(1)}, bf16[128,512]{1,0:T(8,128)(2,1)S(1)}, u32[]{:S(2)}, u32[]{:S(2)}) collective-permute-start(bf16[128,512]{1,0:T(8,128)(2,1)S(1)} %constant_dynamic-slice_fusion.2), channel_id=1, source_target_pairs={{0,8},{1,9},{2,10},{3,11},{4,12},{5,13},{6,14},{7,15},{8,0},{9,1},... | collective-permute-start | bytes 393224 | tf_op jit(solution)/shard_map/ppermute | solution.py:34
  5.2 8.6 %collective-permute-start.2 = (bf16[384,256]{1,0:T(8,128)(2,1)S(1)}, bf16[384,256]{1,0:T(8,128)(2,1)S(1)}, u32[]{:S(2)}, u32[]{:S(2)}) collective-permute-start(bf16[384,256]{1,0:T(8,128)(2,1)S(1)} %maximum_maximum_fusion.1.refs_0_), channel_id=1, source_target_pairs={{0,32},{1,33},{2,34},{3,35},{4,36},{5,37},{6,38},{7,39},{8,40},{9,... | collective-permute-start | bytes 589832 | tf_op jit(solution)/shard_map/ppermute | solution.py:34
  5.3 9.6 %collective-permute-start.3 = (bf16[384,256]{1,0:T(8,128)(2,1)S(1)}, bf16[384,256]{1,0:T(8,128)(2,1)S(1)}, u32[]{:S(2)}, u32[]{:S(2)}) collective-permute-start(bf16[384,256]{1,0:T(8,128)(2,1)S(1)} %maximum_maximum_fusion.1.refs_0_), channel_id=1, source_target_pairs={{0,224},{1,225},{2,226},{3,227},{4,228},{5,229},{6,230},{7,231},{8... | collective-permute-start | bytes 589832 | tf_op jit(solution)/shard_map/ppermute | solution.py:34
  10.9 8.9 %collective-permute-start.1 = (bf16[256,512]{1,0:T(8,128)(2,1)S(1)}, bf16[256,512]{1,0:T(8,128)(2,1)S(1)}, u32[]{:S(2)}, u32[]{:S(2)}) collective-permute-start(bf16[256,512]{1,0:T(8,128)(2,1)S(1)} %pad_maximum_fusion.1), channel_id=1, source_target_pairs={{0,16},{1,17},{2,18},{3,19},{4,20},{5,21},{6,22},{7,23},{8,24},{9,... | collective-permute-start | bytes 786440 | tf_op jit(solution)/shard_map/ppermute | solution.py:34
  15.0 10.9 %collective-permute-start.17 = (bf16[512,256]{1,0:T(8,128)(2,1)S(1)}, bf16[512,256]{1,0:T(8,128)(2,1)S(1)}, u32[]{:S(2)}, u32[]{:S(2)}) collective-permute-start(bf16[512,256]{1,0:T(8,128)(2,1)S(1)} %get-tuple-element.71), channel_id=1, source_target_pairs={{0,8},{1,9},{2,10},{3,11},{4,12},{5,13},{6,14},{7,15},{8,0},{9,1},... | collective-permute-start | bytes 786440 | tf_op jit(solution)/shard_map/ppermute | solution.py:34
  15.9 7.7 %collective-permute-start.4 = (bf16[384,256]{1,0:T(8,128)(2,1)S(1)}, bf16[384,256]{1,0:T(8,128)(2,1)S(1)}, u32[]{:S(2)}, u32[]{:S(2)}) collective-permute-start(bf16[384,256]{1,0:T(8,128)(2,1)S(1)} %collective-permute-done.2.refs_2_), channel_id=1, source_target_pairs={{0,224},{1,225},{2,226},{3,227},{4,228},{5,229},{6,230},{7,231},{8... | collective-permute-start | bytes 589832 | tf_op jit(solution)/shard_map/ppermute | solution.py:34
  18.6 6.1 %collective-permute-start.6 = (bf16[384,256]{1,0:T(8,128)(2,1)S(1)}, bf16[384,256]{1,0:T(8,128)(2,1)S(1)}, u32[]{:S(2)}, u32[]{:S(2)}) collective-permute-start(bf16[384,256]{1,0:T(8,128)(2,1)S(1)} %collective-permute-done.3.refs_3_), channel_id=1, source_target_pairs={{0,32},{1,33},{2,34},{3,35},{4,36},{5,37},{6,38},{7,39},{8,40},{9,... | collective-permute-start | bytes 589832 | tf_op jit(solution)/shard_map/ppermute | solution.py:34
  18.6 7.5 %collective-permute-start.8 = (bf16[384,256]{1,0:T(8,128)(2,1)S(1)}, bf16[384,256]{1,0:T(8,128)(2,1)S(1)}, u32[]{:S(2)}, u32[]{:S(2)}) collective-permute-start(bf16[384,256]{1,0:T(8,128)(2,1)S(1)} %maximum_maximum_fusion.1.refs_0_), channel_id=1, source_target_pairs={{0,8},{1,9},{2,10},{3,11},{4,12},{5,13},{6,14},{7,15},{8,0},{9,1},... | collective-permute-start | bytes 589832 | tf_op jit(solution)/shard_map/ppermute | solution.py:34
  19.8 6.4 %collective-permute-start.9 = (bf16[384,256]{1,0:T(8,128)(2,1)S(1)}, bf16[384,256]{1,0:T(8,128)(2,1)S(1)}, u32[]{:S(2)}, u32[]{:S(2)}) collective-permute-start(bf16[384,256]{1,0:T(8,128)(2,1)S(1)} %collective-permute-done.2.refs_2_), channel_id=1, source_target_pairs={{0,8},{1,9},{2,10},{3,11},{4,12},{5,13},{6,14},{7,15},{8,0},{9,1},... | collective-permute-start | bytes 589832 | tf_op jit(solution)/shard_map/ppermute | solution.py:34
  24.7 6.2 %collective-permute-start.11 = (bf16[384,256]{1,0:T(8,128)(2,1)S(1)}, bf16[384,256]{1,0:T(8,128)(2,1)S(1)}, u32[]{:S(2)}, u32[]{:S(2)}) collective-permute-start(bf16[384,256]{1,0:T(8,128)(2,1)S(1)} %collective-permute-done.6.refs_6_), channel_id=1, source_target_pairs={{0,8},{1,9},{2,10},{3,11},{4,12},{5,13},{6,14},{7,15},{8,0},{9,1},... | collective-permute-start | bytes 589832 | tf_op jit(solution)/shard_map/ppermute | solution.py:34
  25.9 5.8 %collective-permute-start.12 = (bf16[384,256]{1,0:T(8,128)(2,1)S(1)}, bf16[384,256]{1,0:T(8,128)(2,1)S(1)}, u32[]{:S(2)}, u32[]{:S(2)}) collective-permute-start(bf16[384,256]{1,0:T(8,128)(2,1)S(1)} %collective-permute-done.4.refs_7_), channel_id=1, source_target_pairs={{0,8},{1,9},{2,10},{3,11},{4,12},{5,13},{6,14},{7,15},{8,0},{9,1},... | collective-permute-start | bytes 589832 | tf_op jit(solution)/shard_map/ppermute | solution.py:34
  26.1 12.2 %collective-permute-start.5 = (bf16[384,256]{1,0:T(8,128)(2,1)S(1)}, bf16[384,256]{1,0:T(8,128)(2,1)S(1)}, u32[]{:S(2)}, u32[]{:S(2)}) collective-permute-start(bf16[384,256]{1,0:T(8,128)(2,1)S(1)} %collective-permute-done.4.refs_7_), channel_id=1, source_target_pairs={{0,32},{1,33},{2,34},{3,35},{4,36},{5,37},{6,38},{7,39},{8,40},{9,... | collective-permute-start | bytes 589832 | tf_op jit(solution)/shard_map/ppermute | solution.py:34
  26.2 12.1 %collective-permute-start.7 = (bf16[384,256]{1,0:T(8,128)(2,1)S(1)}, bf16[384,256]{1,0:T(8,128)(2,1)S(1)}, u32[]{:S(2)}, u32[]{:S(2)}) collective-permute-start(bf16[384,256]{1,0:T(8,128)(2,1)S(1)} %collective-permute-done.6.refs_6_), channel_id=1, source_target_pairs={{0,224},{1,225},{2,226},{3,227},{4,228},{5,229},{6,230},{7,231},{8... | collective-permute-start | bytes 589832 | tf_op jit(solution)/shard_map/ppermute | solution.py:34
  28.0 12.4 %collective-permute-start.18 = (bf16[256,512]{1,0:T(8,128)(2,1)S(1)}, bf16[256,512]{1,0:T(8,128)(2,1)S(1)}, u32[]{:S(2)}, u32[]{:S(2)}) collective-permute-start(bf16[256,512]{1,0:T(8,128)(2,1)S(1)} %get-tuple-element.69), channel_id=1, source_target_pairs={{0,16},{1,17},{2,18},{3,19},{4,20},{5,21},{6,22},{7,23},{8,24},{9,... | collective-permute-start | bytes 786440 | tf_op jit(solution)/shard_map/ppermute | solution.py:34
  30.9 12.4 %collective-permute-start.20 = (bf16[256,512]{1,0:T(8,128)(2,1)S(1)}, bf16[256,512]{1,0:T(8,128)(2,1)S(1)}, u32[]{:S(2)}, u32[]{:S(2)}) collective-permute-start(bf16[256,512]{1,0:T(8,128)(2,1)S(1)} %get-tuple-element.69), channel_id=1, source_target_pairs={{0,17},{1,16},{2,19},{3,18},{4,21},{5,20},{6,23},{7,22},{8,25},{9,... | collective-permute-start | bytes 786440 | tf_op jit(solution)/shard_map/ppermute | solution.py:34
  31.7 11.3 %collective-permute-start.19 = (bf16[256,512]{1,0:T(8,128)(2,1)S(1)}, bf16[256,512]{1,0:T(8,128)(2,1)S(1)}, u32[]{:S(2)}, u32[]{:S(2)}) collective-permute-start(bf16[256,512]{1,0:T(8,128)(2,1)S(1)} %get-tuple-element.58), channel_id=1, source_target_pairs={{0,1},{1,0},{2,3},{3,2},{4,5},{5,4},{6,7},{7,6},{8,9},{9,8},{10,11... | collective-permute-start | bytes 786440 | tf_op jit(solution)/shard_map/ppermute | solution.py:34
  38.3 16.3 %collective-permute-start.14 = (bf16[384,256]{1,0:T(8,128)(2,1)S(1)}, bf16[384,256]{1,0:T(8,128)(2,1)S(1)}, u32[]{:S(2)}, u32[]{:S(2)}) collective-permute-start(bf16[384,256]{1,0:T(8,128)(2,1)S(1)} %collective-permute-done.7.refs_1_), channel_id=1, source_target_pairs={{0,8},{1,9},{2,10},{3,11},{4,12},{5,13},{6,14},{7,15},{8,0},{9,1},... | collective-permute-start | bytes 589832 | tf_op jit(solution)/shard_map/ppermute | solution.py:34
  39.3 13.6 %collective-permute-start.15 = (bf16[384,256]{1,0:T(8,128)(2,1)S(1)}, bf16[384,256]{1,0:T(8,128)(2,1)S(1)}, u32[]{:S(2)}, u32[]{:S(2)}) collective-permute-start(bf16[384,256]{1,0:T(8,128)(2,1)S(1)} %collective-permute-done.7.refs_1_), channel_id=1, source_target_pairs={{0,32},{1,33},{2,34},{3,35},{4,36},{5,37},{6,38},{7,39},{8,40},{9,... | collective-permute-start | bytes 589832 | tf_op jit(solution)/shard_map/ppermute | solution.py:34
  40.4 14.2 %collective-permute-start.13 = (bf16[384,256]{1,0:T(8,128)(2,1)S(1)}, bf16[384,256]{1,0:T(8,128)(2,1)S(1)}, u32[]{:S(2)}, u32[]{:S(2)}) collective-permute-start(bf16[384,256]{1,0:T(8,128)(2,1)S(1)} %collective-permute-done.5.refs_0_), channel_id=1, source_target_pairs={{0,8},{1,9},{2,10},{3,11},{4,12},{5,13},{6,14},{7,15},{8,0},{9,1},... | collective-permute-start | bytes 589832 | tf_op jit(solution)/shard_map/ppermute | solution.py:34
  43.5 39.3 %collective-permute-start.21 = (bf16[512,1024]{1,0:T(8,128)(2,1)S(1)}, bf16[512,1024]{1,0:T(8,128)(2,1)S(1)}, u32[]{:S(2)}, u32[]{:S(2)}) collective-permute-start(bf16[512,1024]{1,0:T(8,128)(2,1)S(1)} %maximum_maximum_fusion.refs_5_.refs_3_), channel_id=1, source_target_pairs={{0,2},{1,3},{2,4},{3,5},{4,6},{5,7},{6,0},{7,1},{8,10},{9,11},{10,... | collective-permute-start | bytes 3145736 | tf_op jit(solution)/shard_map/ppermute | solution.py:34
  44.8 38.0 %collective-permute-start.22 = (bf16[512,1024]{1,0:T(8,128)(2,1)S(1)}, bf16[512,1024]{1,0:T(8,128)(2,1)S(1)}, u32[]{:S(2)}, u32[]{:S(2)}) collective-permute-start(bf16[512,1024]{1,0:T(8,128)(2,1)S(1)} %maximum_maximum_fusion.refs_5_.refs_3_), channel_id=1, source_target_pairs={{0,6},{1,7},{2,0},{3,1},{4,2},{5,3},{6,4},{7,5},{8,14},{9,15},{10,... | collective-permute-start | bytes 3145736 | tf_op jit(solution)/shard_map/ppermute | solution.py:34
  82.8 7.3 %collective-permute-start.24 = (bf16[64,2048]{1,0:T(8,128)(2,1)S(1)}, bf16[64,2048]{1,0:T(8,128)(2,1)S(1)}, u32[]{:S(2)}, u32[]{:S(2)}) collective-permute-start(bf16[64,2048]{1,0:T(8,128)(2,1)S(1)} %shard_map.76.refs_0_), channel_id=1, source_target_pairs={{0,224},{1,225},{2,226},{3,227},{4,228},{5,229},{6,230},{7,231},{8... | collective-permute-start | bytes 786440 | tf_op jit(solution)/shard_map/ppermute | solution.py:34
  83.8 9.2 %collective-permute-start.23 = (bf16[64,2048]{1,0:T(8,128)(2,1)S(1)}, bf16[64,2048]{1,0:T(8,128)(2,1)S(1)}, u32[]{:S(2)}, u32[]{:S(2)}) collective-permute-start(bf16[64,2048]{1,0:T(8,128)(2,1)S(1)} %shard_map.76.refs_0_), channel_id=1, source_target_pairs={{0,32},{1,33},{2,34},{3,35},{4,36},{5,37},{6,38},{7,39},{8,40},{9,... | collective-permute-start | bytes 786440 | tf_op jit(solution)/shard_map/ppermute | solution.py:34
  90.1 5.2 %collective-permute-start.25 = (bf16[64,2048]{1,0:T(8,128)(2,1)S(1)}, bf16[64,2048]{1,0:T(8,128)(2,1)S(1)}, u32[]{:S(2)}, u32[]{:S(2)}) collective-permute-start(bf16[64,2048]{1,0:T(8,128)(2,1)S(1)} %collective-permute-done.24.refs_2_), channel_id=1, source_target_pairs={{0,32},{1,33},{2,34},{3,35},{4,36},{5,37},{6,38},{7,39},{8,40},{9,... | collective-permute-start | bytes 786440 | tf_op jit(solution)/shard_map/ppermute | solution.py:34
  90.1 14.2 %collective-permute-start.27 = (bf16[256,1024]{1,0:T(8,128)(2,1)S(1)}, bf16[256,1024]{1,0:T(8,128)(2,1)S(1)}, u32[]{:S(2)}, u32[]{:S(2)}) collective-permute-start(bf16[256,1024]{1,0:T(8,128)(2,1)S(1)} %slice.14), channel_id=1, source_target_pairs={{0,2},{1,3},{2,4},{3,5},{4,6},{5,7},{6,0},{7,1},{8,10},{9,11},{10,... | collective-permute-start | bytes 1572872 | tf_op jit(solution)/shard_map/ppermute | solution.py:34
  90.2 14.1 %collective-permute-start.28 = (bf16[256,1024]{1,0:T(8,128)(2,1)S(1)}, bf16[256,1024]{1,0:T(8,128)(2,1)S(1)}, u32[]{:S(2)}, u32[]{:S(2)}) collective-permute-start(bf16[256,1024]{1,0:T(8,128)(2,1)S(1)} %slice.15), channel_id=1, source_target_pairs={{0,6},{1,7},{2,0},{3,1},{4,2},{5,3},{6,4},{7,5},{8,14},{9,15},{10,... | collective-permute-start | bytes 1572872 | tf_op jit(solution)/shard_map/ppermute | solution.py:34
  93.0 6.7 %collective-permute-start.26 = (bf16[64,2048]{1,0:T(8,128)(2,1)S(1)}, bf16[64,2048]{1,0:T(8,128)(2,1)S(1)}, u32[]{:S(2)}, u32[]{:S(2)}) collective-permute-start(bf16[64,2048]{1,0:T(8,128)(2,1)S(1)} %collective-permute-done.23.refs_1_), channel_id=1, source_target_pairs={{0,224},{1,225},{2,226},{3,227},{4,228},{5,229},{6,230},{7,231},{8... | collective-permute-start | bytes 786440 | tf_op jit(solution)/shard_map/ppermute | solution.py:34
  95.3 9.1 %collective-permute-start.31 = (bf16[64,2048]{1,0:T(8,128)(2,1)S(1)}, bf16[64,2048]{1,0:T(8,128)(2,1)S(1)}, u32[]{:S(2)}, u32[]{:S(2)}) collective-permute-start(bf16[64,2048]{1,0:T(8,128)(2,1)S(1)} %collective-permute-done.25.refs_3_), channel_id=1, source_target_pairs={{0,224},{1,225},{2,226},{3,227},{4,228},{5,229},{6,230},{7,231},{8... | collective-permute-start | bytes 786440 | tf_op jit(solution)/shard_map/ppermute | solution.py:34
  99.7 11.0 %collective-permute-start.30 = (bf16[64,2048]{1,0:T(8,128)(2,1)S(1)}, bf16[64,2048]{1,0:T(8,128)(2,1)S(1)}, u32[]{:S(2)}, u32[]{:S(2)}) collective-permute-start(bf16[64,2048]{1,0:T(8,128)(2,1)S(1)} %collective-permute-done.26.refs_4_), channel_id=1, source_target_pairs={{0,32},{1,33},{2,34},{3,35},{4,36},{5,37},{6,38},{7,39},{8,40},{9,... | collective-permute-start | bytes 786440 | tf_op jit(solution)/shard_map/ppermute | solution.py:34
  104.4 6.4 %collective-permute-start.32 = (bf16[64,2048]{1,0:T(8,128)(2,1)S(1)}, bf16[64,2048]{1,0:T(8,128)(2,1)S(1)}, u32[]{:S(2)}, u32[]{:S(2)}) collective-permute-start(bf16[64,2048]{1,0:T(8,128)(2,1)S(1)} %collective-permute-done.31.refs_1_), channel_id=1, source_target_pairs={{0,32},{1,33},{2,34},{3,35},{4,36},{5,37},{6,38},{7,39},{8,40},{9,... | collective-permute-start | bytes 786440 | tf_op jit(solution)/shard_map/ppermute | solution.py:34
  105.9 11.1 %collective-permute-start.29 = (bf16[320,512]{1,0:T(8,128)(2,1)S(1)}, bf16[320,512]{1,0:T(8,128)(2,1)S(1)}, u32[]{:S(2)}, u32[]{:S(2)}) collective-permute-start(bf16[320,512]{1,0:T(8,128)(2,1)S(1)} %get-tuple-element.66), channel_id=1, source_target_pairs={{0,8},{1,9},{2,10},{3,11},{4,12},{5,13},{6,14},{7,15},{8,0},{9,1},... | collective-permute-start | bytes 983048 | tf_op jit(solution)/shard_map/ppermute | solution.py:34
  111.8 6.3 %collective-permute-start.33 = (bf16[192,512]{1,0:T(8,128)(2,1)S(1)}, bf16[192,512]{1,0:T(8,128)(2,1)S(1)}, u32[]{:S(2)}, u32[]{:S(2)}) collective-permute-start(bf16[192,512]{1,0:T(8,128)(2,1)S(1)} %get-tuple-element.68), channel_id=1, source_target_pairs={{0,8},{1,9},{2,10},{3,11},{4,12},{5,13},{6,14},{7,15},{8,0},{9,1},... | collective-permute-start | bytes 589832 | tf_op jit(solution)/shard_map/ppermute | solution.py:34
  (4 other events, 28.0 us)

commit v6 on v5

--- a/solution.py
+++ b/solution.py
@@ -301,7 +301,6 @@
     far = swap(near, a=1)
     q = jnp.concatenate([jnp.where(yh == 0, near, far), jnp.where(yh == 0, far, near)], 0)
 
-    ahead, behind, out_weight = lax.optimization_barrier((ahead, behind, out_weight))
     depth = out_weight.shape[0] // 4
     block = lambda value, at, rows: lax.dynamic_slice_in_dim(value, at * rows, rows, 0)
     wide = jnp.concatenate(

time: 135 us -> 132 us (0.978)
  waiting for transfers between devices: 24.5 us -> 22.3 us
    ppermute x34, waiting for transfers between devices: 24.5 us -> 22.3 us  [permute(): return lax.ppermute(value, AXES, pairs)]
  transfers between devices with their start and end apart: 34 -> 34, of which waited for: 13 -> 10; matrix products, arithmetic and copies ran while one was open for 2% -> 2% of each run, Pallas kernels for 19% -> 20%
where the time goes in v6:
time: 132 us
  starting transfers between devices  47.2 us (36%)
  blocking collectives  30.9 us (23%)
  Pallas kernels  26.6 us (20%)
  waiting for transfers between devices  22.3 us (17%)
  local copies, waits for them, and re-layouts  2.21 us (2%)
  other arithmetic  2.08 us (2%)
    ppermute x34, starting transfers between devices, permute(): return lax.ppermute(value, AXES, pairs)  47.2 us
    pallas_call x3, Pallas kernels, attend(): pl.pallas_call(functools.partial(attend_kernel, tuple((entry[1:] for entr...  22.3 us
    ppermute x34, waiting for transfers between devices, permute(): return lax.ppermute(value, AXES, pairs)  22.3 us
    all_to_all x1, blocking collectives, shards(): lax.all_to_all(pieces.reshape(NY * NZ, group, width), ('yh', 'x', 'yl'),...  17.2 us
    all_to_all x1, blocking collectives, shards(): lax.all_to_all(settled.reshape(NY * NZ, rows, width), ('yh', 'x', 'yl'),...  13.6 us
  transfers between devices with their start and end apart: 34, of which 10 were waited for; matrix products, arithmetic and copies ran while one was open for 2% of the time, Pallas kernels for 20%

profile of v6, /device:TPU:1, one launch (start us, length us, event | category | flops | bytes accessed | tf_op | source)
XLA Modules:
  0.0 131.6 jit_solution(4044541545784086811)
XLA Ops:
  1.0 3.3 %collective-permute-start = (bf16[128,512]{1,0:T(8,128)(2,1)S(1)}, bf16[128,512]{1,0:T(8,128)(2,1)S(1)}, u32[]{:S(2)}, u32[]{:S(2)}) collective-permute-start(bf16[128,512]{1,0:T(8,128)(2,1)S(1)} %constant_dynamic-slice_fusion.2), channel_id=1, source_target_pairs={{0,8},{1,9},{2,10},{3,11},{4,12},{5,13},{6,14},{7,15},{8,0},{9,1},... | collective-permute-start | bytes 393224 | tf_op jit(solution)/shard_map/ppermute | solution.py:34
  5.4 4.6 %collective-permute-start.5 = (bf16[384,256]{1,0:T(8,128)(2,1)S(1)}, bf16[384,256]{1,0:T(8,128)(2,1)S(1)}, u32[]{:S(2)}, u32[]{:S(2)}) collective-permute-start(bf16[384,256]{1,0:T(8,128)(2,1)S(1)} %maximum_maximum_fusion.1.refs_0_), channel_id=1, source_target_pairs={{0,224},{1,225},{2,226},{3,227},{4,228},{5,229},{6,230},{7,231},{8... | collective-permute-start | bytes 589832 | tf_op jit(solution)/shard_map/ppermute | solution.py:34
  11.7 3.0 %collective-permute-start.1 = (bf16[256,512]{1,0:T(8,128)(2,1)S(1)}, bf16[256,512]{1,0:T(8,128)(2,1)S(1)}, u32[]{:S(2)}, u32[]{:S(2)}) collective-permute-start(bf16[256,512]{1,0:T(8,128)(2,1)S(1)} %pad_maximum_fusion.1), channel_id=1, source_target_pairs={{0,16},{1,17},{2,18},{3,19},{4,20},{5,21},{6,22},{7,23},{8,24},{9,... | collective-permute-start | bytes 786440 | tf_op jit(solution)/shard_map/ppermute | solution.py:34
  15.0 2.4 %collective-permute-start.3 = (bf16[384,256]{1,0:T(8,128)(2,1)S(1)}, bf16[384,256]{1,0:T(8,128)(2,1)S(1)}, u32[]{:S(2)}, u32[]{:S(2)}) collective-permute-start(bf16[384,256]{1,0:T(8,128)(2,1)S(1)} %collective-permute-done.2.refs_2_), channel_id=1, source_target_pairs={{0,224},{1,225},{2,226},{3,227},{4,228},{5,229},{6,230},{7,231},{8... | collective-permute-start | bytes 589832 | tf_op jit(solution)/shard_map/ppermute | solution.py:34
  17.3 1.4 %collective-permute-start.8 = (bf16[384,256]{1,0:T(8,128)(2,1)S(1)}, bf16[384,256]{1,0:T(8,128)(2,1)S(1)}, u32[]{:S(2)}, u32[]{:S(2)}) collective-permute-start(bf16[384,256]{1,0:T(8,128)(2,1)S(1)} %maximum_maximum_fusion.1.refs_0_), channel_id=1, source_target_pairs={{0,8},{1,9},{2,10},{3,11},{4,12},{5,13},{6,14},{7,15},{8,0},{9,1},... | collective-permute-start | bytes 589832 | tf_op jit(solution)/shard_map/ppermute | solution.py:34
  18.9 2.3 %collective-permute-done.1 = bf16[256,512]{1,0:T(8,128)(2,1)S(1)} collective-permute-done((bf16[256,512]{1,0:T(8,128)(2,1)S(1)}, bf16[256,512]{1,0:T(8,128)(2,1)S(1)}, u32[]{:S(2)}, u32[]{:S(2)}) %collective-permute-start.1) | collective-permute-done | bytes 262176 | tf_op jit(solution)/shard_map/ppermute | solution.py:34
  22.3 1.2 collective-permute-start.12
  23.6 3.0 %collective-permute-start.18 = (bf16[256,512]{1,0:T(8,128)(2,1)S(1)}, bf16[256,512]{1,0:T(8,128)(2,1)S(1)}, u32[]{:S(2)}, u32[]{:S(2)}) collective-permute-start(bf16[256,512]{1,0:T(8,128)(2,1)S(1)} %get-tuple-element.63), channel_id=1, source_target_pairs={{0,16},{1,17},{2,18},{3,19},{4,20},{5,21},{6,22},{7,23},{8,24},{9,... | collective-permute-start | bytes 786440 | tf_op jit(solution)/shard_map/ppermute | solution.py:34
  27.7 2.4 %collective-permute-start.7 = (bf16[384,256]{1,0:T(8,128)(2,1)S(1)}, bf16[384,256]{1,0:T(8,128)(2,1)S(1)}, u32[]{:S(2)}, u32[]{:S(2)}) collective-permute-start(bf16[384,256]{1,0:T(8,128)(2,1)S(1)} %collective-permute-done.6.refs_6_), channel_id=1, source_target_pairs={{0,224},{1,225},{2,226},{3,227},{4,228},{5,229},{6,230},{7,231},{8... | collective-permute-start | bytes 589832 | tf_op jit(solution)/shard_map/ppermute | solution.py:34
  30.2 6.5 %shard_map.73 = (f32[512,256]{1,0:T(8,128)S(1)}, f32[512,256]{1,0:T(8,128)S(1)}, f32[512,256]{1,0:T(8,128)S(1)}) custom-call(s32[5]{0:T(128)S(1)} %stack.23.meta, s32[32]{0:T(128)S(1)} %copy-done, bf16[512,512]{1,0:T(8,128)(2,1)S(1)} %pad_maximum_fusion.q_ref, bf16[384,256]{1,0:T(8,128)(2,1)S(1)} %maximum_maximum_fusion.1.refs_0_, ...), custom_call_target="tpu_custom_call" | custom-call | flops 2013265920 | bytes 1048576 | tf_op jit(solution)/shard_map/pallas_call | solution.py:168
  36.8 1.2 collective-permute-start.14
  37.9 1.2 collective-permute-done.19
  39.3 1.3 collective-permute-start.21
  40.6 1.5 %collective-permute-start.22 = (bf16[512,1024]{1,0:T(8,128)(2,1)S(1)}, bf16[512,1024]{1,0:T(8,128)(2,1)S(1)}, u32[]{:S(2)}, u32[]{:S(2)}) collective-permute-start(bf16[512,1024]{1,0:T(8,128)(2,1)S(1)} %maximum_maximum_fusion.refs_5_.refs_3_), channel_id=1, source_target_pairs={{0,6},{1,7},{2,0},{3,1},{4,2},{5,3},{6,4},{7,5},{8,14},{9,15},{10,... | collective-permute-start | bytes 3145736 | tf_op jit(solution)/shard_map/ppermute | solution.py:34
  42.0 1.3 %collective-permute-start.13 = (bf16[384,256]{1,0:T(8,128)(2,1)S(1)}, bf16[384,256]{1,0:T(8,128)(2,1)S(1)}, u32[]{:S(2)}, u32[]{:S(2)}) collective-permute-start(bf16[384,256]{1,0:T(8,128)(2,1)S(1)} %collective-permute-done.4.refs_0_), channel_id=1, source_target_pairs={{0,8},{1,9},{2,10},{3,11},{4,12},{5,13},{6,14},{7,15},{8,0},{9,1},... | collective-permute-start | bytes 589832 | tf_op jit(solution)/shard_map/ppermute | solution.py:34
  43.4 6.6 %shard_map.74 = (f32[512,256]{1,0:T(8,128)S(1)}, f32[512,256]{1,0:T(8,128)S(1)}, f32[512,256]{1,0:T(8,128)S(1)}) custom-call(s32[5]{0:T(128)S(1)} %stack.23.meta, s32[32]{0:T(128)S(1)} %copy-done, bf16[512,512]{1,0:T(8,128)(2,1)S(1)} %pad_maximum_fusion.q_ref, bf16[384,256]{1,0:T(8,128)(2,1)S(1)} %maximum_maximum_fusion.1.refs_0_, ...), custom_call_target="tpu_custom_call" | custom-call | flops 2013265920 | bytes 1048576 | tf_op jit(solution)/shard_map/pallas_call | solution.py:168
  50.4 1.4 %collective-permute-done.16.refs_5_ = bf16[384,256]{1,0:T(8,128)(2,1)S(1)} collective-permute-done((bf16[384,256]{1,0:T(8,128)(2,1)S(1)}, bf16[384,256]{1,0:T(8,128)(2,1)S(1)}, u32[]{:S(2)}, u32[]{:S(2)}) %collective-permute-start.16) | collective-permute-done | bytes 196640 | tf_op jit(solution)/shard_map/ppermute | solution.py:34
  51.8 9.2 %shard_map.75 = bf16[2,8,80,256]{3,2,1,0:T(8,128)(2,1)S(1)} custom-call(s32[5]{0:T(128)S(1)} %stack.23.meta, s32[32]{0:T(128)S(1)} %copy-done, bf16[512,512]{1,0:T(8,128)(2,1)S(1)} %pad_maximum_fusion.q_ref, bf16[384,256]{1,0:T(8,128)(2,1)S(1)} %collective-permute-done.4.refs_0_, bf16[384,256]{1,0:T(8,128)(2,1)S(1)} %collective-permute-done.7.refs_1_, ...), custom_call_target="tpu_custom_call" | custom-call | flops 2415919104 | bytes 1048576 | tf_op jit(solution)/shard_map/pallas_call | solution.py:168
  60.9 17.2 %all_to_all.10.pieces = bf16[16,80,256]{2,1,0:T(8,128)(2,1)S(1)} all-to-all(bf16[16,80,256]{2,1,0:T(8,128)(2,1)S(1)} %bitcast.9), channel_id=1, replica_groups=mesh['z'=8,'yh'=2,'core'=2,'x'=4,'yl'=2] {'yh','x','yl'}, dimensions={0} | all-to-all | bytes 1310720 | tf_op jit(solution)/shard_map/all_to_all | solution.py:335
  78.2 1.2 shard_map.76.refs_0_
  79.4 2.5 %collective-permute-start.24 = (bf16[64,2048]{1,0:T(8,128)(2,1)S(1)}, bf16[64,2048]{1,0:T(8,128)(2,1)S(1)}, u32[]{:S(2)}, u32[]{:S(2)}) collective-permute-start(bf16[64,2048]{1,0:T(8,128)(2,1)S(1)} %shard_map.76.refs_0_), channel_id=1, source_target_pairs={{0,224},{1,225},{2,226},{3,227},{4,228},{5,229},{6,230},{7,231},{8... | collective-permute-start | bytes 786440 | tf_op jit(solution)/shard_map/ppermute | solution.py:34
  81.8 5.4 %collective-permute-done.24.refs_2_ = bf16[64,2048]{1,0:T(8,128)(2,1)S(1)} collective-permute-done((bf16[64,2048]{1,0:T(8,128)(2,1)S(1)}, bf16[64,2048]{1,0:T(8,128)(2,1)S(1)}, u32[]{:S(2)}, u32[]{:S(2)}) %collective-permute-start.24) | collective-permute-done | bytes 262176 | tf_op jit(solution)/shard_map/ppermute | solution.py:34
  87.4 2.7 %collective-permute-start.28 = (bf16[256,1024]{1,0:T(8,128)(2,1)S(1)}, bf16[256,1024]{1,0:T(8,128)(2,1)S(1)}, u32[]{:S(2)}, u32[]{:S(2)}) collective-permute-start(bf16[256,1024]{1,0:T(8,128)(2,1)S(1)} %slice.15), channel_id=1, source_target_pairs={{0,6},{1,7},{2,0},{3,1},{4,2},{5,3},{6,4},{7,5},{8,14},{9,15},{10,... | collective-permute-start | bytes 1572872 | tf_op jit(solution)/shard_map/ppermute | solution.py:34
  90.1 2.4 %collective-permute-start.26 = (bf16[64,2048]{1,0:T(8,128)(2,1)S(1)}, bf16[64,2048]{1,0:T(8,128)(2,1)S(1)}, u32[]{:S(2)}, u32[]{:S(2)}) collective-permute-start(bf16[64,2048]{1,0:T(8,128)(2,1)S(1)} %collective-permute-done.23.refs_1_), channel_id=1, source_target_pairs={{0,224},{1,225},{2,226},{3,227},{4,228},{5,229},{6,230},{7,231},{8... | collective-permute-start | bytes 786440 | tf_op jit(solution)/shard_map/ppermute | solution.py:34
  93.3 1.9 %collective-permute-start.31 = (bf16[64,2048]{1,0:T(8,128)(2,1)S(1)}, bf16[64,2048]{1,0:T(8,128)(2,1)S(1)}, u32[]{:S(2)}, u32[]{:S(2)}) collective-permute-start(bf16[64,2048]{1,0:T(8,128)(2,1)S(1)} %collective-permute-done.25.refs_3_), channel_id=1, source_target_pairs={{0,224},{1,225},{2,226},{3,227},{4,228},{5,229},{6,230},{7,231},{8... | collective-permute-start | bytes 786440 | tf_op jit(solution)/shard_map/ppermute | solution.py:34
  95.2 1.6 %collective-permute-done.26.refs_4_ = bf16[64,2048]{1,0:T(8,128)(2,1)S(1)} collective-permute-done((bf16[64,2048]{1,0:T(8,128)(2,1)S(1)}, bf16[64,2048]{1,0:T(8,128)(2,1)S(1)}, u32[]{:S(2)}, u32[]{:S(2)}) %collective-permute-start.26) | collective-permute-done | bytes 262176 | tf_op jit(solution)/shard_map/ppermute | solution.py:34
  97.1 5.8 %collective-permute-done.31.refs_1_ = bf16[64,2048]{1,0:T(8,128)(2,1)S(1)} collective-permute-done((bf16[64,2048]{1,0:T(8,128)(2,1)S(1)}, bf16[64,2048]{1,0:T(8,128)(2,1)S(1)}, u32[]{:S(2)}, u32[]{:S(2)}) %collective-permute-start.31) | collective-permute-done | bytes 262176 | tf_op jit(solution)/shard_map/ppermute | solution.py:34
  102.8 1.5 %shard_map.77 = (f32[320,512]{1,0:T(8,128)S(1)}, bf16[320,512]{1,0:T(8,128)(2,1)S(1)}) custom-call(bf16[64,2048]{1,0:T(8,128)(2,1)S(1)} %shard_map.76.refs_0_, bf16[64,2048]{1,0:T(8,128)(2,1)S(1)} %collective-permute-done.23.refs_1_, bf16[64,2048]{1,0:T(8,128)(2,1)S(1)} %collective-permute-done.24.refs_2_, ...), custom_call_target="tpu_custom_call" | custom-call | flops 1342177280 | bytes 4194304 | tf_op jit(solution)/shard_map/pallas_call | solution.py:239
  104.4 3.4 %collective-permute-start.29 = (bf16[320,512]{1,0:T(8,128)(2,1)S(1)}, bf16[320,512]{1,0:T(8,128)(2,1)S(1)}, u32[]{:S(2)}, u32[]{:S(2)}) collective-permute-start(bf16[320,512]{1,0:T(8,128)(2,1)S(1)} %get-tuple-element.60), channel_id=1, source_target_pairs={{0,8},{1,9},{2,10},{3,11},{4,12},{5,13},{6,14},{7,15},{8,0},{9,1},... | collective-permute-start | bytes 983048 | tf_op jit(solution)/shard_map/ppermute | solution.py:34
  107.8 2.5 %collective-permute-done.32.refs_2_ = bf16[64,2048]{1,0:T(8,128)(2,1)S(1)} collective-permute-done((bf16[64,2048]{1,0:T(8,128)(2,1)S(1)}, bf16[64,2048]{1,0:T(8,128)(2,1)S(1)}, u32[]{:S(2)}, u32[]{:S(2)}) %collective-permute-start.32) | collective-permute-done | bytes 262176 | tf_op jit(solution)/shard_map/ppermute | solution.py:34
  111.3 4.1 %collective-permute-start.33 = (bf16[192,512]{1,0:T(8,128)(2,1)S(1)}, bf16[192,512]{1,0:T(8,128)(2,1)S(1)}, u32[]{:S(2)}, u32[]{:S(2)}) collective-permute-start(bf16[192,512]{1,0:T(8,128)(2,1)S(1)} %get-tuple-element.62), channel_id=1, source_target_pairs={{0,8},{1,9},{2,10},{3,11},{4,12},{5,13},{6,14},{7,15},{8,0},{9,1},... | collective-permute-start | bytes 589832 | tf_op jit(solution)/shard_map/ppermute | solution.py:34
  117.2 13.6 %all_to_all.11 = bf16[16,64,256]{2,1,0:T(8,128)(2,1)S(1)} all-to-all(bf16[16,64,256]{2,1,0:T(8,128)(2,1)S(1)} %bitcast.8), channel_id=1, replica_groups=mesh['z'=8,'yh'=2,'core'=2,'x'=4,'yl'=2] {'yh','x','yl'}, dimensions={0} | all-to-all | bytes 1048576 | tf_op jit(solution)/shard_map/all_to_all | solution.py:357
  (62 shorter events, 11.7 us)
Async XLA Ops:
  1.0 10.7 %collective-permute-start = (bf16[128,512]{1,0:T(8,128)(2,1)S(1)}, bf16[128,512]{1,0:T(8,128)(2,1)S(1)}, u32[]{:S(2)}, u32[]{:S(2)}) collective-permute-start(bf16[128,512]{1,0:T(8,128)(2,1)S(1)} %constant_dynamic-slice_fusion.2), channel_id=1, source_target_pairs={{0,8},{1,9},{2,10},{3,11},{4,12},{5,13},{6,14},{7,15},{8,0},{9,1},... | collective-permute-start | bytes 393224 | tf_op jit(solution)/shard_map/ppermute | solution.py:34
  5.3 9.7 %collective-permute-start.2 = (bf16[384,256]{1,0:T(8,128)(2,1)S(1)}, bf16[384,256]{1,0:T(8,128)(2,1)S(1)}, u32[]{:S(2)}, u32[]{:S(2)}) collective-permute-start(bf16[384,256]{1,0:T(8,128)(2,1)S(1)} %maximum_maximum_fusion.1.refs_0_), channel_id=1, source_target_pairs={{0,32},{1,33},{2,34},{3,35},{4,36},{5,37},{6,38},{7,39},{8,40},{9,... | collective-permute-start | bytes 589832 | tf_op jit(solution)/shard_map/ppermute | solution.py:34
  5.4 9.6 %collective-permute-start.5 = (bf16[384,256]{1,0:T(8,128)(2,1)S(1)}, bf16[384,256]{1,0:T(8,128)(2,1)S(1)}, u32[]{:S(2)}, u32[]{:S(2)}) collective-permute-start(bf16[384,256]{1,0:T(8,128)(2,1)S(1)} %maximum_maximum_fusion.1.refs_0_), channel_id=1, source_target_pairs={{0,224},{1,225},{2,226},{3,227},{4,228},{5,229},{6,230},{7,231},{8... | collective-permute-start | bytes 589832 | tf_op jit(solution)/shard_map/ppermute | solution.py:34
  11.0 7.8 %collective-permute-start.17 = (bf16[512,256]{1,0:T(8,128)(2,1)S(1)}, bf16[512,256]{1,0:T(8,128)(2,1)S(1)}, u32[]{:S(2)}, u32[]{:S(2)}) collective-permute-start(bf16[512,256]{1,0:T(8,128)(2,1)S(1)} %get-tuple-element.65), channel_id=1, source_target_pairs={{0,8},{1,9},{2,10},{3,11},{4,12},{5,13},{6,14},{7,15},{8,0},{9,1},... | collective-permute-start | bytes 786440 | tf_op jit(solution)/shard_map/ppermute | solution.py:34
  11.7 9.5 %collective-permute-start.1 = (bf16[256,512]{1,0:T(8,128)(2,1)S(1)}, bf16[256,512]{1,0:T(8,128)(2,1)S(1)}, u32[]{:S(2)}, u32[]{:S(2)}) collective-permute-start(bf16[256,512]{1,0:T(8,128)(2,1)S(1)} %pad_maximum_fusion.1), channel_id=1, source_target_pairs={{0,16},{1,17},{2,18},{3,19},{4,20},{5,21},{6,22},{7,23},{8,24},{9,... | collective-permute-start | bytes 786440 | tf_op jit(solution)/shard_map/ppermute | solution.py:34
  15.0 7.1 %collective-permute-start.6 = (bf16[384,256]{1,0:T(8,128)(2,1)S(1)}, bf16[384,256]{1,0:T(8,128)(2,1)S(1)}, u32[]{:S(2)}, u32[]{:S(2)}) collective-permute-start(bf16[384,256]{1,0:T(8,128)(2,1)S(1)} %collective-permute-done.5.refs_3_), channel_id=1, source_target_pairs={{0,32},{1,33},{2,34},{3,35},{4,36},{5,37},{6,38},{7,39},{8,40},{9,... | collective-permute-start | bytes 589832 | tf_op jit(solution)/shard_map/ppermute | solution.py:34
  15.0 7.3 %collective-permute-start.3 = (bf16[384,256]{1,0:T(8,128)(2,1)S(1)}, bf16[384,256]{1,0:T(8,128)(2,1)S(1)}, u32[]{:S(2)}, u32[]{:S(2)}) collective-permute-start(bf16[384,256]{1,0:T(8,128)(2,1)S(1)} %collective-permute-done.2.refs_2_), channel_id=1, source_target_pairs={{0,224},{1,225},{2,226},{3,227},{4,228},{5,229},{6,230},{7,231},{8... | collective-permute-start | bytes 589832 | tf_op jit(solution)/shard_map/ppermute | solution.py:34
  17.3 6.3 %collective-permute-start.8 = (bf16[384,256]{1,0:T(8,128)(2,1)S(1)}, bf16[384,256]{1,0:T(8,128)(2,1)S(1)}, u32[]{:S(2)}, u32[]{:S(2)}) collective-permute-start(bf16[384,256]{1,0:T(8,128)(2,1)S(1)} %maximum_maximum_fusion.1.refs_0_), channel_id=1, source_target_pairs={{0,8},{1,9},{2,10},{3,11},{4,12},{5,13},{6,14},{7,15},{8,0},{9,1},... | collective-permute-start | bytes 589832 | tf_op jit(solution)/shard_map/ppermute | solution.py:34
  18.8 7.8 %collective-permute-start.9 = (bf16[384,256]{1,0:T(8,128)(2,1)S(1)}, bf16[384,256]{1,0:T(8,128)(2,1)S(1)}, u32[]{:S(2)}, u32[]{:S(2)}) collective-permute-start(bf16[384,256]{1,0:T(8,128)(2,1)S(1)} %collective-permute-done.2.refs_2_), channel_id=1, source_target_pairs={{0,8},{1,9},{2,10},{3,11},{4,12},{5,13},{6,14},{7,15},{8,0},{9,1},... | collective-permute-start | bytes 589832 | tf_op jit(solution)/shard_map/ppermute | solution.py:34
  21.2 6.2 %collective-permute-start.10 = (bf16[384,256]{1,0:T(8,128)(2,1)S(1)}, bf16[384,256]{1,0:T(8,128)(2,1)S(1)}, u32[]{:S(2)}, u32[]{:S(2)}) collective-permute-start(bf16[384,256]{1,0:T(8,128)(2,1)S(1)} %collective-permute-done.5.refs_3_), channel_id=1, source_target_pairs={{0,8},{1,9},{2,10},{3,11},{4,12},{5,13},{6,14},{7,15},{8,0},{9,1},... | collective-permute-start | bytes 589832 | tf_op jit(solution)/shard_map/ppermute | solution.py:34
  22.1 5.3 %collective-permute-start.11 = (bf16[384,256]{1,0:T(8,128)(2,1)S(1)}, bf16[384,256]{1,0:T(8,128)(2,1)S(1)}, u32[]{:S(2)}, u32[]{:S(2)}) collective-permute-start(bf16[384,256]{1,0:T(8,128)(2,1)S(1)} %collective-permute-done.6.refs_6_), channel_id=1, source_target_pairs={{0,8},{1,9},{2,10},{3,11},{4,12},{5,13},{6,14},{7,15},{8,0},{9,1},... | collective-permute-start | bytes 589832 | tf_op jit(solution)/shard_map/ppermute | solution.py:34
  22.3 5.5 %collective-permute-start.12 = (bf16[384,256]{1,0:T(8,128)(2,1)S(1)}, bf16[384,256]{1,0:T(8,128)(2,1)S(1)}, u32[]{:S(2)}, u32[]{:S(2)}) collective-permute-start(bf16[384,256]{1,0:T(8,128)(2,1)S(1)} %collective-permute-done.3.refs_7_), channel_id=1, source_target_pairs={{0,8},{1,9},{2,10},{3,11},{4,12},{5,13},{6,14},{7,15},{8,0},{9,1},... | collective-permute-start | bytes 589832 | tf_op jit(solution)/shard_map/ppermute | solution.py:34
  23.6 14.3 %collective-permute-start.18 = (bf16[256,512]{1,0:T(8,128)(2,1)S(1)}, bf16[256,512]{1,0:T(8,128)(2,1)S(1)}, u32[]{:S(2)}, u32[]{:S(2)}) collective-permute-start(bf16[256,512]{1,0:T(8,128)(2,1)S(1)} %get-tuple-element.63), channel_id=1, source_target_pairs={{0,16},{1,17},{2,18},{3,19},{4,20},{5,21},{6,22},{7,23},{8,24},{9,... | collective-permute-start | bytes 786440 | tf_op jit(solution)/shard_map/ppermute | solution.py:34
  26.6 12.5 %collective-permute-start.20 = (bf16[256,512]{1,0:T(8,128)(2,1)S(1)}, bf16[256,512]{1,0:T(8,128)(2,1)S(1)}, u32[]{:S(2)}, u32[]{:S(2)}) collective-permute-start(bf16[256,512]{1,0:T(8,128)(2,1)S(1)} %get-tuple-element.63), channel_id=1, source_target_pairs={{0,17},{1,16},{2,19},{3,18},{4,21},{5,20},{6,23},{7,22},{8,25},{9,... | collective-permute-start | bytes 786440 | tf_op jit(solution)/shard_map/ppermute | solution.py:34
  27.4 11.7 %collective-permute-start.19 = (bf16[256,512]{1,0:T(8,128)(2,1)S(1)}, bf16[256,512]{1,0:T(8,128)(2,1)S(1)}, u32[]{:S(2)}, u32[]{:S(2)}) collective-permute-start(bf16[256,512]{1,0:T(8,128)(2,1)S(1)} %get-tuple-element.52), channel_id=1, source_target_pairs={{0,1},{1,0},{2,3},{3,2},{4,5},{5,4},{6,7},{7,6},{8,9},{9,8},{10,11... | collective-permute-start | bytes 786440 | tf_op jit(solution)/shard_map/ppermute | solution.py:34
  27.4 9.3 %collective-permute-start.4 = (bf16[384,256]{1,0:T(8,128)(2,1)S(1)}, bf16[384,256]{1,0:T(8,128)(2,1)S(1)}, u32[]{:S(2)}, u32[]{:S(2)}) collective-permute-start(bf16[384,256]{1,0:T(8,128)(2,1)S(1)} %collective-permute-done.3.refs_7_), channel_id=1, source_target_pairs={{0,32},{1,33},{2,34},{3,35},{4,36},{5,37},{6,38},{7,39},{8,40},{9,... | collective-permute-start | bytes 589832 | tf_op jit(solution)/shard_map/ppermute | solution.py:34
  27.7 9.0 %collective-permute-start.7 = (bf16[384,256]{1,0:T(8,128)(2,1)S(1)}, bf16[384,256]{1,0:T(8,128)(2,1)S(1)}, u32[]{:S(2)}, u32[]{:S(2)}) collective-permute-start(bf16[384,256]{1,0:T(8,128)(2,1)S(1)} %collective-permute-done.6.refs_6_), channel_id=1, source_target_pairs={{0,224},{1,225},{2,226},{3,227},{4,228},{5,229},{6,230},{7,231},{8... | collective-permute-start | bytes 589832 | tf_op jit(solution)/shard_map/ppermute | solution.py:34
  36.8 13.6 %collective-permute-start.14 = (bf16[384,256]{1,0:T(8,128)(2,1)S(1)}, bf16[384,256]{1,0:T(8,128)(2,1)S(1)}, u32[]{:S(2)}, u32[]{:S(2)}) collective-permute-start(bf16[384,256]{1,0:T(8,128)(2,1)S(1)} %collective-permute-done.7.refs_1_), channel_id=1, source_target_pairs={{0,8},{1,9},{2,10},{3,11},{4,12},{5,13},{6,14},{7,15},{8,0},{9,1},... | collective-permute-start | bytes 589832 | tf_op jit(solution)/shard_map/ppermute | solution.py:34
  37.9 12.1 %collective-permute-start.15 = (bf16[384,256]{1,0:T(8,128)(2,1)S(1)}, bf16[384,256]{1,0:T(8,128)(2,1)S(1)}, u32[]{:S(2)}, u32[]{:S(2)}) collective-permute-start(bf16[384,256]{1,0:T(8,128)(2,1)S(1)} %collective-permute-done.7.refs_1_), channel_id=1, source_target_pairs={{0,32},{1,33},{2,34},{3,35},{4,36},{5,37},{6,38},{7,39},{8,40},{9,... | collective-permute-start | bytes 589832 | tf_op jit(solution)/shard_map/ppermute | solution.py:34
  39.3 40.1 %collective-permute-start.21 = (bf16[512,1024]{1,0:T(8,128)(2,1)S(1)}, bf16[512,1024]{1,0:T(8,128)(2,1)S(1)}, u32[]{:S(2)}, u32[]{:S(2)}) collective-permute-start(bf16[512,1024]{1,0:T(8,128)(2,1)S(1)} %maximum_maximum_fusion.refs_5_.refs_3_), channel_id=1, source_target_pairs={{0,2},{1,3},{2,4},{3,5},{4,6},{5,7},{6,0},{7,1},{8,10},{9,11},{10,... | collective-permute-start | bytes 3145736 | tf_op jit(solution)/shard_map/ppermute | solution.py:34
  40.6 38.8 %collective-permute-start.22 = (bf16[512,1024]{1,0:T(8,128)(2,1)S(1)}, bf16[512,1024]{1,0:T(8,128)(2,1)S(1)}, u32[]{:S(2)}, u32[]{:S(2)}) collective-permute-start(bf16[512,1024]{1,0:T(8,128)(2,1)S(1)} %maximum_maximum_fusion.refs_5_.refs_3_), channel_id=1, source_target_pairs={{0,6},{1,7},{2,0},{3,1},{4,2},{5,3},{6,4},{7,5},{8,14},{9,15},{10,... | collective-permute-start | bytes 3145736 | tf_op jit(solution)/shard_map/ppermute | solution.py:34
  42.0 8.3 %collective-permute-start.13 = (bf16[384,256]{1,0:T(8,128)(2,1)S(1)}, bf16[384,256]{1,0:T(8,128)(2,1)S(1)}, u32[]{:S(2)}, u32[]{:S(2)}) collective-permute-start(bf16[384,256]{1,0:T(8,128)(2,1)S(1)} %collective-permute-done.4.refs_0_), channel_id=1, source_target_pairs={{0,8},{1,9},{2,10},{3,11},{4,12},{5,13},{6,14},{7,15},{8,0},{9,1},... | collective-permute-start | bytes 589832 | tf_op jit(solution)/shard_map/ppermute | solution.py:34
  79.4 7.8 %collective-permute-start.24 = (bf16[64,2048]{1,0:T(8,128)(2,1)S(1)}, bf16[64,2048]{1,0:T(8,128)(2,1)S(1)}, u32[]{:S(2)}, u32[]{:S(2)}) collective-permute-start(bf16[64,2048]{1,0:T(8,128)(2,1)S(1)} %shard_map.76.refs_0_), channel_id=1, source_target_pairs={{0,224},{1,225},{2,226},{3,227},{4,228},{5,229},{6,230},{7,231},{8... | collective-permute-start | bytes 786440 | tf_op jit(solution)/shard_map/ppermute | solution.py:34
  81.8 8.3 %collective-permute-start.23 = (bf16[64,2048]{1,0:T(8,128)(2,1)S(1)}, bf16[64,2048]{1,0:T(8,128)(2,1)S(1)}, u32[]{:S(2)}, u32[]{:S(2)}) collective-permute-start(bf16[64,2048]{1,0:T(8,128)(2,1)S(1)} %shard_map.76.refs_0_), channel_id=1, source_target_pairs={{0,32},{1,33},{2,34},{3,35},{4,36},{5,37},{6,38},{7,39},{8,40},{9,... | collective-permute-start | bytes 786440 | tf_op jit(solution)/shard_map/ppermute | solution.py:34
  87.2 6.1 %collective-permute-start.25 = (bf16[64,2048]{1,0:T(8,128)(2,1)S(1)}, bf16[64,2048]{1,0:T(8,128)(2,1)S(1)}, u32[]{:S(2)}, u32[]{:S(2)}) collective-permute-start(bf16[64,2048]{1,0:T(8,128)(2,1)S(1)} %collective-permute-done.24.refs_2_), channel_id=1, source_target_pairs={{0,32},{1,33},{2,34},{3,35},{4,36},{5,37},{6,38},{7,39},{8,40},{9,... | collective-permute-start | bytes 786440 | tf_op jit(solution)/shard_map/ppermute | solution.py:34
  87.2 15.6 %collective-permute-start.27 = (bf16[256,1024]{1,0:T(8,128)(2,1)S(1)}, bf16[256,1024]{1,0:T(8,128)(2,1)S(1)}, u32[]{:S(2)}, u32[]{:S(2)}) collective-permute-start(bf16[256,1024]{1,0:T(8,128)(2,1)S(1)} %slice.14), channel_id=1, source_target_pairs={{0,2},{1,3},{2,4},{3,5},{4,6},{5,7},{6,0},{7,1},{8,10},{9,11},{10,... | collective-permute-start | bytes 1572872 | tf_op jit(solution)/shard_map/ppermute | solution.py:34
  87.4 15.5 %collective-permute-start.28 = (bf16[256,1024]{1,0:T(8,128)(2,1)S(1)}, bf16[256,1024]{1,0:T(8,128)(2,1)S(1)}, u32[]{:S(2)}, u32[]{:S(2)}) collective-permute-start(bf16[256,1024]{1,0:T(8,128)(2,1)S(1)} %slice.15), channel_id=1, source_target_pairs={{0,6},{1,7},{2,0},{3,1},{4,2},{5,3},{6,4},{7,5},{8,14},{9,15},{10,... | collective-permute-start | bytes 1572872 | tf_op jit(solution)/shard_map/ppermute | solution.py:34
  90.1 6.7 %collective-permute-start.26 = (bf16[64,2048]{1,0:T(8,128)(2,1)S(1)}, bf16[64,2048]{1,0:T(8,128)(2,1)S(1)}, u32[]{:S(2)}, u32[]{:S(2)}) collective-permute-start(bf16[64,2048]{1,0:T(8,128)(2,1)S(1)} %collective-permute-done.23.refs_1_), channel_id=1, source_target_pairs={{0,224},{1,225},{2,226},{3,227},{4,228},{5,229},{6,230},{7,231},{8... | collective-permute-start | bytes 786440 | tf_op jit(solution)/shard_map/ppermute | solution.py:34
  93.3 9.5 %collective-permute-start.31 = (bf16[64,2048]{1,0:T(8,128)(2,1)S(1)}, bf16[64,2048]{1,0:T(8,128)(2,1)S(1)}, u32[]{:S(2)}, u32[]{:S(2)}) collective-permute-start(bf16[64,2048]{1,0:T(8,128)(2,1)S(1)} %collective-permute-done.25.refs_3_), channel_id=1, source_target_pairs={{0,224},{1,225},{2,226},{3,227},{4,228},{5,229},{6,230},{7,231},{8... | collective-permute-start | bytes 786440 | tf_op jit(solution)/shard_map/ppermute | solution.py:34
  96.8 11.0 %collective-permute-start.30 = (bf16[64,2048]{1,0:T(8,128)(2,1)S(1)}, bf16[64,2048]{1,0:T(8,128)(2,1)S(1)}, u32[]{:S(2)}, u32[]{:S(2)}) collective-permute-start(bf16[64,2048]{1,0:T(8,128)(2,1)S(1)} %collective-permute-done.26.refs_4_), channel_id=1, source_target_pairs={{0,32},{1,33},{2,34},{3,35},{4,36},{5,37},{6,38},{7,39},{8,40},{9,... | collective-permute-start | bytes 786440 | tf_op jit(solution)/shard_map/ppermute | solution.py:34
  102.8 7.5 %collective-permute-start.32 = (bf16[64,2048]{1,0:T(8,128)(2,1)S(1)}, bf16[64,2048]{1,0:T(8,128)(2,1)S(1)}, u32[]{:S(2)}, u32[]{:S(2)}) collective-permute-start(bf16[64,2048]{1,0:T(8,128)(2,1)S(1)} %collective-permute-done.31.refs_1_), channel_id=1, source_target_pairs={{0,32},{1,33},{2,34},{3,35},{4,36},{5,37},{6,38},{7,39},{8,40},{9,... | collective-permute-start | bytes 786440 | tf_op jit(solution)/shard_map/ppermute | solution.py:34
  104.4 11.1 %collective-permute-start.29 = (bf16[320,512]{1,0:T(8,128)(2,1)S(1)}, bf16[320,512]{1,0:T(8,128)(2,1)S(1)}, u32[]{:S(2)}, u32[]{:S(2)}) collective-permute-start(bf16[320,512]{1,0:T(8,128)(2,1)S(1)} %get-tuple-element.60), channel_id=1, source_target_pairs={{0,8},{1,9},{2,10},{3,11},{4,12},{5,13},{6,14},{7,15},{8,0},{9,1},... | collective-permute-start | bytes 983048 | tf_op jit(solution)/shard_map/ppermute | solution.py:34
  (4 other events, 29.9 us)

commit v7 on v6

--- a/solution.py
+++ b/solution.py
@@ -233,7 +233,7 @@
 
 
 def project(blocks, weights):
-    rows, depth = blocks[0].shape[0] * len(blocks), blocks[0].shape[1]
+    rows, depth = sum(block.shape[0] for block in blocks), blocks[0].shape[1]
     width = weights[0].shape[1]
     whole = pl.BlockSpec(memory_space=pltpu.VMEM)
     return pl.pallas_call(
@@ -343,7 +343,8 @@
         up, down = meet_up(behind[-1]), meet_down(ahead[-1])
         ahead.append(up)
         behind.append(down)
-    ahead.append(meet_up(behind[-1]))
+    middle = a.shape[0] // 2
+    opposite = [meet_up(behind[-1][:middle]), meet_down(ahead[-1][middle:])]
 
     def share(blocks):
         kept, sent = project(blocks, weights)
@@ -351,7 +352,7 @@
 
     order = ((0, 1, -1, 2, -2), (3, -3, 4))
     first = share([a, ahead[1], behind[1], ahead[2], behind[2]])
-    second = share([ahead[3], behind[3], ahead[4]])
+    second = share([ahead[3], behind[3]] + opposite)
     settled = settle(meta, order, (first, second))
     rows, width = settled.shape[2:]
     home = lax.all_to_all(

time: 132 us -> 131 us (level)
  waiting for transfers between devices: 22.3 us -> 19 us
  starting transfers between devices: 47.2 us -> 48.9 us
    ppermute x34 -> x35, waiting for transfers between devices: 22.3 us -> 19 us  [permute(): return lax.ppermute(value, AXES, pairs)]
    ppermute x34 -> x35, starting transfers between devices: 47.2 us -> 48.9 us  [permute(): return lax.ppermute(value, AXES, pairs)]
  transfers between devices with their start and end apart: 34 -> 35, of which waited for: 10 -> 9; matrix products, arithmetic and copies ran while one was open for 2% -> 2% of each run, Pallas kernels for 20% -> 20%
where the time goes in v7:
time: 131 us; the launch traced here: 130 us
  starting transfers between devices  48.9 us (37%)
  blocking collectives  31.3 us (24%)
  Pallas kernels  26.6 us (20%)
  waiting for transfers between devices  19 us (15%)
  local copies, waits for them, and re-layouts  2.23 us (2%)
  other arithmetic  2.08 us (2%)
    ppermute x35, starting transfers between devices, permute(): return lax.ppermute(value, AXES, pairs)  48.9 us
    pallas_call x3, Pallas kernels, attend(): pl.pallas_call(functools.partial(attend_kernel, tuple((entry[1:] for entr...  22.3 us
    ppermute x35, waiting for transfers between devices, permute(): return lax.ppermute(value, AXES, pairs)  19 us
    all_to_all x1, blocking collectives, shards(): lax.all_to_all(pieces.reshape(NY * NZ, group, width), ('yh', 'x', 'yl'),...  17.2 us
    all_to_all x1, blocking collectives, shards(): lax.all_to_all(settled.reshape(NY * NZ, rows, width), ('yh', 'x', 'yl'),...  14.1 us
  transfers between devices with their start and end apart: 35, of which 9 were waited for; matrix products, arithmetic and copies ran while one was open for 2% of the time, Pallas kernels for 20%

profile of v7, /device:TPU:1, one launch (start us, length us, event | category | flops | bytes accessed | tf_op | source)
XLA Modules:
  0.0 130.5 jit_solution(7728566801368658900)
XLA Ops:
  1.0 3.3 %collective-permute-start = (bf16[128,512]{1,0:T(8,128)(2,1)S(1)}, bf16[128,512]{1,0:T(8,128)(2,1)S(1)}, u32[]{:S(2)}, u32[]{:S(2)}) collective-permute-start(bf16[128,512]{1,0:T(8,128)(2,1)S(1)} %constant_dynamic-slice_fusion.2), channel_id=1, source_target_pairs={{0,8},{1,9},{2,10},{3,11},{4,12},{5,13},{6,14},{7,15},{8,0},{9,1},... | collective-permute-start | bytes 393224 | tf_op jit(solution)/shard_map/ppermute | solution.py:34
  5.4 4.6 %collective-permute-start.5 = (bf16[384,256]{1,0:T(8,128)(2,1)S(1)}, bf16[384,256]{1,0:T(8,128)(2,1)S(1)}, u32[]{:S(2)}, u32[]{:S(2)}) collective-permute-start(bf16[384,256]{1,0:T(8,128)(2,1)S(1)} %maximum_maximum_fusion.1.refs_0_), channel_id=1, source_target_pairs={{0,224},{1,225},{2,226},{3,227},{4,228},{5,229},{6,230},{7,231},{8... | collective-permute-start | bytes 589832 | tf_op jit(solution)/shard_map/ppermute | solution.py:34
  11.7 3.0 %collective-permute-start.1 = (bf16[256,512]{1,0:T(8,128)(2,1)S(1)}, bf16[256,512]{1,0:T(8,128)(2,1)S(1)}, u32[]{:S(2)}, u32[]{:S(2)}) collective-permute-start(bf16[256,512]{1,0:T(8,128)(2,1)S(1)} %pad_maximum_fusion.1), channel_id=1, source_target_pairs={{0,16},{1,17},{2,18},{3,19},{4,20},{5,21},{6,22},{7,23},{8,24},{9,... | collective-permute-start | bytes 786440 | tf_op jit(solution)/shard_map/ppermute | solution.py:34
  15.0 2.4 %collective-permute-start.3 = (bf16[384,256]{1,0:T(8,128)(2,1)S(1)}, bf16[384,256]{1,0:T(8,128)(2,1)S(1)}, u32[]{:S(2)}, u32[]{:S(2)}) collective-permute-start(bf16[384,256]{1,0:T(8,128)(2,1)S(1)} %collective-permute-done.2.refs_2_), channel_id=1, source_target_pairs={{0,224},{1,225},{2,226},{3,227},{4,228},{5,229},{6,230},{7,231},{8... | collective-permute-start | bytes 589832 | tf_op jit(solution)/shard_map/ppermute | solution.py:34
  17.3 1.4 %collective-permute-start.8 = (bf16[384,256]{1,0:T(8,128)(2,1)S(1)}, bf16[384,256]{1,0:T(8,128)(2,1)S(1)}, u32[]{:S(2)}, u32[]{:S(2)}) collective-permute-start(bf16[384,256]{1,0:T(8,128)(2,1)S(1)} %maximum_maximum_fusion.1.refs_0_), channel_id=1, source_target_pairs={{0,8},{1,9},{2,10},{3,11},{4,12},{5,13},{6,14},{7,15},{8,0},{9,1},... | collective-permute-start | bytes 589832 | tf_op jit(solution)/shard_map/ppermute | solution.py:34
  18.9 2.3 %collective-permute-done.1 = bf16[256,512]{1,0:T(8,128)(2,1)S(1)} collective-permute-done((bf16[256,512]{1,0:T(8,128)(2,1)S(1)}, bf16[256,512]{1,0:T(8,128)(2,1)S(1)}, u32[]{:S(2)}, u32[]{:S(2)}) %collective-permute-start.1) | collective-permute-done | bytes 262176 | tf_op jit(solution)/shard_map/ppermute | solution.py:34
  22.3 1.2 collective-permute-start.12
  23.6 3.0 %collective-permute-start.18 = (bf16[256,512]{1,0:T(8,128)(2,1)S(1)}, bf16[256,512]{1,0:T(8,128)(2,1)S(1)}, u32[]{:S(2)}, u32[]{:S(2)}) collective-permute-start(bf16[256,512]{1,0:T(8,128)(2,1)S(1)} %get-tuple-element.63), channel_id=1, source_target_pairs={{0,16},{1,17},{2,18},{3,19},{4,20},{5,21},{6,22},{7,23},{8,24},{9,... | collective-permute-start | bytes 786440 | tf_op jit(solution)/shard_map/ppermute | solution.py:34
  27.7 2.4 %collective-permute-start.7 = (bf16[384,256]{1,0:T(8,128)(2,1)S(1)}, bf16[384,256]{1,0:T(8,128)(2,1)S(1)}, u32[]{:S(2)}, u32[]{:S(2)}) collective-permute-start(bf16[384,256]{1,0:T(8,128)(2,1)S(1)} %collective-permute-done.6.refs_6_), channel_id=1, source_target_pairs={{0,224},{1,225},{2,226},{3,227},{4,228},{5,229},{6,230},{7,231},{8... | collective-permute-start | bytes 589832 | tf_op jit(solution)/shard_map/ppermute | solution.py:34
  30.2 6.5 %shard_map.73 = (f32[512,256]{1,0:T(8,128)S(1)}, f32[512,256]{1,0:T(8,128)S(1)}, f32[512,256]{1,0:T(8,128)S(1)}) custom-call(s32[5]{0:T(128)S(1)} %stack.23.meta, s32[32]{0:T(128)S(1)} %copy-done, bf16[512,512]{1,0:T(8,128)(2,1)S(1)} %pad_maximum_fusion.q_ref, bf16[384,256]{1,0:T(8,128)(2,1)S(1)} %maximum_maximum_fusion.1.refs_0_, ...), custom_call_target="tpu_custom_call" | custom-call | flops 2013265920 | bytes 1048576 | tf_op jit(solution)/shard_map/pallas_call | solution.py:168
  36.8 1.2 collective-permute-start.14
  37.9 1.2 collective-permute-done.19
  39.3 1.3 collective-permute-start.21
  40.6 1.5 %collective-permute-start.22 = (bf16[512,1024]{1,0:T(8,128)(2,1)S(1)}, bf16[512,1024]{1,0:T(8,128)(2,1)S(1)}, u32[]{:S(2)}, u32[]{:S(2)}) collective-permute-start(bf16[512,1024]{1,0:T(8,128)(2,1)S(1)} %maximum_maximum_fusion.refs_5_.refs_4_), channel_id=1, source_target_pairs={{0,6},{1,7},{2,0},{3,1},{4,2},{5,3},{6,4},{7,5},{8,14},{9,15},{10,... | collective-permute-start | bytes 3145736 | tf_op jit(solution)/shard_map/ppermute | solution.py:34
  42.0 1.3 %collective-permute-start.13 = (bf16[384,256]{1,0:T(8,128)(2,1)S(1)}, bf16[384,256]{1,0:T(8,128)(2,1)S(1)}, u32[]{:S(2)}, u32[]{:S(2)}) collective-permute-start(bf16[384,256]{1,0:T(8,128)(2,1)S(1)} %collective-permute-done.4.refs_0_), channel_id=1, source_target_pairs={{0,8},{1,9},{2,10},{3,11},{4,12},{5,13},{6,14},{7,15},{8,0},{9,1},... | collective-permute-start | bytes 589832 | tf_op jit(solution)/shard_map/ppermute | solution.py:34
  43.4 6.6 %shard_map.74 = (f32[512,256]{1,0:T(8,128)S(1)}, f32[512,256]{1,0:T(8,128)S(1)}, f32[512,256]{1,0:T(8,128)S(1)}) custom-call(s32[5]{0:T(128)S(1)} %stack.23.meta, s32[32]{0:T(128)S(1)} %copy-done, bf16[512,512]{1,0:T(8,128)(2,1)S(1)} %pad_maximum_fusion.q_ref, bf16[384,256]{1,0:T(8,128)(2,1)S(1)} %maximum_maximum_fusion.1.refs_0_, ...), custom_call_target="tpu_custom_call" | custom-call | flops 2013265920 | bytes 1048576 | tf_op jit(solution)/shard_map/pallas_call | solution.py:168
  50.4 1.4 %collective-permute-done.16.refs_5_ = bf16[384,256]{1,0:T(8,128)(2,1)S(1)} collective-permute-done((bf16[384,256]{1,0:T(8,128)(2,1)S(1)}, bf16[384,256]{1,0:T(8,128)(2,1)S(1)}, u32[]{:S(2)}, u32[]{:S(2)}) %collective-permute-start.16) | collective-permute-done | bytes 196640 | tf_op jit(solution)/shard_map/ppermute | solution.py:34
  51.8 9.2 %shard_map.75 = bf16[2,8,80,256]{3,2,1,0:T(8,128)(2,1)S(1)} custom-call(s32[5]{0:T(128)S(1)} %stack.23.meta, s32[32]{0:T(128)S(1)} %copy-done, bf16[512,512]{1,0:T(8,128)(2,1)S(1)} %pad_maximum_fusion.q_ref, bf16[384,256]{1,0:T(8,128)(2,1)S(1)} %collective-permute-done.4.refs_0_, bf16[384,256]{1,0:T(8,128)(2,1)S(1)} %collective-permute-done.7.refs_1_, ...), custom_call_target="tpu_custom_call" | custom-call | flops 2415919104 | bytes 1048576 | tf_op jit(solution)/shard_map/pallas_call | solution.py:168
  60.9 17.2 %all_to_all.10.pieces = bf16[16,80,256]{2,1,0:T(8,128)(2,1)S(1)} all-to-all(bf16[16,80,256]{2,1,0:T(8,128)(2,1)S(1)} %bitcast.9), channel_id=1, replica_groups=mesh['z'=8,'yh'=2,'core'=2,'x'=4,'yl'=2] {'yh','x','yl'}, dimensions={0} | all-to-all | bytes 1310720 | tf_op jit(solution)/shard_map/all_to_all | solution.py:335
  78.2 1.2 shard_map.76.refs_0_
  79.4 2.5 %collective-permute-start.24 = (bf16[64,2048]{1,0:T(8,128)(2,1)S(1)}, bf16[64,2048]{1,0:T(8,128)(2,1)S(1)}, u32[]{:S(2)}, u32[]{:S(2)}) collective-permute-start(bf16[64,2048]{1,0:T(8,128)(2,1)S(1)} %shard_map.76.refs_0_), channel_id=1, source_target_pairs={{0,224},{1,225},{2,226},{3,227},{4,228},{5,229},{6,230},{7,231},{8... | collective-permute-start | bytes 786440 | tf_op jit(solution)/shard_map/ppermute | solution.py:34
  81.8 5.4 %collective-permute-done.24.refs_2_ = bf16[64,2048]{1,0:T(8,128)(2,1)S(1)} collective-permute-done((bf16[64,2048]{1,0:T(8,128)(2,1)S(1)}, bf16[64,2048]{1,0:T(8,128)(2,1)S(1)}, u32[]{:S(2)}, u32[]{:S(2)}) %collective-permute-start.24) | collective-permute-done | bytes 262176 | tf_op jit(solution)/shard_map/ppermute | solution.py:34
  88.1 1.5 %collective-permute-start.26 = (bf16[64,2048]{1,0:T(8,128)(2,1)S(1)}, bf16[64,2048]{1,0:T(8,128)(2,1)S(1)}, u32[]{:S(2)}, u32[]{:S(2)}) collective-permute-start(bf16[64,2048]{1,0:T(8,128)(2,1)S(1)} %collective-permute-done.23.refs_1_), channel_id=1, source_target_pairs={{0,224},{1,225},{2,226},{3,227},{4,228},{5,229},{6,230},{7,231},{8... | collective-permute-start | bytes 786440 | tf_op jit(solution)/shard_map/ppermute | solution.py:34
  89.8 2.7 %collective-permute-start.28 = (bf16[256,1024]{1,0:T(8,128)(2,1)S(1)}, bf16[256,1024]{1,0:T(8,128)(2,1)S(1)}, u32[]{:S(2)}, u32[]{:S(2)}) collective-permute-start(bf16[256,1024]{1,0:T(8,128)(2,1)S(1)} %slice.21), channel_id=1, source_target_pairs={{0,6},{1,7},{2,0},{3,1},{4,2},{5,3},{6,4},{7,5},{8,14},{9,15},{10,... | collective-permute-start | bytes 1572872 | tf_op jit(solution)/shard_map/ppermute | solution.py:34
  93.3 1.9 %collective-permute-start.31 = (bf16[64,2048]{1,0:T(8,128)(2,1)S(1)}, bf16[64,2048]{1,0:T(8,128)(2,1)S(1)}, u32[]{:S(2)}, u32[]{:S(2)}) collective-permute-start(bf16[64,2048]{1,0:T(8,128)(2,1)S(1)} %collective-permute-done.25.refs_3_), channel_id=1, source_target_pairs={{0,224},{1,225},{2,226},{3,227},{4,228},{5,229},{6,230},{7,231},{8... | collective-permute-start | bytes 786440 | tf_op jit(solution)/shard_map/ppermute | solution.py:34
  95.2 5.6 %collective-permute-done.31.refs_1_ = bf16[64,2048]{1,0:T(8,128)(2,1)S(1)} collective-permute-done((bf16[64,2048]{1,0:T(8,128)(2,1)S(1)}, bf16[64,2048]{1,0:T(8,128)(2,1)S(1)}, u32[]{:S(2)}, u32[]{:S(2)}) %collective-permute-start.31) | collective-permute-done | bytes 262176 | tf_op jit(solution)/shard_map/ppermute | solution.py:34
  101.0 2.2 %collective-permute-start.33 = (bf16[32,2048]{1,0:T(8,128)(2,1)S(1)}, bf16[32,2048]{1,0:T(8,128)(2,1)S(1)}, u32[]{:S(2)}, u32[]{:S(2)}) collective-permute-start(bf16[32,2048]{1,0:T(8,128)(2,1)S(1)} %slice.27), channel_id=1, source_target_pairs={{0,224},{1,225},{2,226},{3,227},{4,228},{5,229},{6,230},{7,231},{8... | collective-permute-start | bytes 393224 | tf_op jit(solution)/shard_map/ppermute | solution.py:34
  103.2 1.5 %shard_map.77 = (f32[320,512]{1,0:T(8,128)S(1)}, bf16[320,512]{1,0:T(8,128)(2,1)S(1)}) custom-call(bf16[64,2048]{1,0:T(8,128)(2,1)S(1)} %shard_map.76.refs_0_, bf16[64,2048]{1,0:T(8,128)(2,1)S(1)} %collective-permute-done.23.refs_1_, bf16[64,2048]{1,0:T(8,128)(2,1)S(1)} %collective-permute-done.24.refs_2_, ...), custom_call_target="tpu_custom_call" | custom-call | flops 1342177280 | bytes 4194304 | tf_op jit(solution)/shard_map/pallas_call | solution.py:239
  104.8 3.8 %collective-permute-start.29 = (bf16[320,512]{1,0:T(8,128)(2,1)S(1)}, bf16[320,512]{1,0:T(8,128)(2,1)S(1)}, u32[]{:S(2)}, u32[]{:S(2)}) collective-permute-start(bf16[320,512]{1,0:T(8,128)(2,1)S(1)} %get-tuple-element.60), channel_id=1, source_target_pairs={{0,8},{1,9},{2,10},{3,11},{4,12},{5,13},{6,14},{7,15},{8,0},{9,1},... | collective-permute-start | bytes 983048 | tf_op jit(solution)/shard_map/ppermute | solution.py:34
  109.6 4.3 %collective-permute-start.34 = (bf16[192,512]{1,0:T(8,128)(2,1)S(1)}, bf16[192,512]{1,0:T(8,128)(2,1)S(1)}, u32[]{:S(2)}, u32[]{:S(2)}) collective-permute-start(bf16[192,512]{1,0:T(8,128)(2,1)S(1)} %get-tuple-element.62), channel_id=1, source_target_pairs={{0,8},{1,9},{2,10},{3,11},{4,12},{5,13},{6,14},{7,15},{8,0},{9,1},... | collective-permute-start | bytes 589832 | tf_op jit(solution)/shard_map/ppermute | solution.py:34
  113.9 1.1 collective-permute-done.34.refs_3_
  115.6 14.1 %all_to_all.11 = bf16[16,64,256]{2,1,0:T(8,128)(2,1)S(1)} all-to-all(bf16[16,64,256]{2,1,0:T(8,128)(2,1)S(1)} %bitcast.8), channel_id=1, replica_groups=mesh['z'=8,'yh'=2,'core'=2,'x'=4,'yl'=2] {'yh','x','yl'}, dimensions={0} | all-to-all | bytes 1048576 | tf_op jit(solution)/shard_map/all_to_all | solution.py:358
  (66 shorter events, 11.4 us)
Async XLA Ops:
  1.0 10.7 %collective-permute-start = (bf16[128,512]{1,0:T(8,128)(2,1)S(1)}, bf16[128,512]{1,0:T(8,128)(2,1)S(1)}, u32[]{:S(2)}, u32[]{:S(2)}) collective-permute-start(bf16[128,512]{1,0:T(8,128)(2,1)S(1)} %constant_dynamic-slice_fusion.2), channel_id=1, source_target_pairs={{0,8},{1,9},{2,10},{3,11},{4,12},{5,13},{6,14},{7,15},{8,0},{9,1},... | collective-permute-start | bytes 393224 | tf_op jit(solution)/shard_map/ppermute | solution.py:34
  5.3 9.7 %collective-permute-start.2 = (bf16[384,256]{1,0:T(8,128)(2,1)S(1)}, bf16[384,256]{1,0:T(8,128)(2,1)S(1)}, u32[]{:S(2)}, u32[]{:S(2)}) collective-permute-start(bf16[384,256]{1,0:T(8,128)(2,1)S(1)} %maximum_maximum_fusion.1.refs_0_), channel_id=1, source_target_pairs={{0,32},{1,33},{2,34},{3,35},{4,36},{5,37},{6,38},{7,39},{8,40},{9,... | collective-permute-start | bytes 589832 | tf_op jit(solution)/shard_map/ppermute | solution.py:34
  5.4 9.6 %collective-permute-start.5 = (bf16[384,256]{1,0:T(8,128)(2,1)S(1)}, bf16[384,256]{1,0:T(8,128)(2,1)S(1)}, u32[]{:S(2)}, u32[]{:S(2)}) collective-permute-start(bf16[384,256]{1,0:T(8,128)(2,1)S(1)} %maximum_maximum_fusion.1.refs_0_), channel_id=1, source_target_pairs={{0,224},{1,225},{2,226},{3,227},{4,228},{5,229},{6,230},{7,231},{8... | collective-permute-start | bytes 589832 | tf_op jit(solution)/shard_map/ppermute | solution.py:34
  11.0 7.8 %collective-permute-start.17 = (bf16[512,256]{1,0:T(8,128)(2,1)S(1)}, bf16[512,256]{1,0:T(8,128)(2,1)S(1)}, u32[]{:S(2)}, u32[]{:S(2)}) collective-permute-start(bf16[512,256]{1,0:T(8,128)(2,1)S(1)} %get-tuple-element.65), channel_id=1, source_target_pairs={{0,8},{1,9},{2,10},{3,11},{4,12},{5,13},{6,14},{7,15},{8,0},{9,1},... | collective-permute-start | bytes 786440 | tf_op jit(solution)/shard_map/ppermute | solution.py:34
  11.7 9.5 %collective-permute-start.1 = (bf16[256,512]{1,0:T(8,128)(2,1)S(1)}, bf16[256,512]{1,0:T(8,128)(2,1)S(1)}, u32[]{:S(2)}, u32[]{:S(2)}) collective-permute-start(bf16[256,512]{1,0:T(8,128)(2,1)S(1)} %pad_maximum_fusion.1), channel_id=1, source_target_pairs={{0,16},{1,17},{2,18},{3,19},{4,20},{5,21},{6,22},{7,23},{8,24},{9,... | collective-permute-start | bytes 786440 | tf_op jit(solution)/shard_map/ppermute | solution.py:34
  15.0 7.1 %collective-permute-start.6 = (bf16[384,256]{1,0:T(8,128)(2,1)S(1)}, bf16[384,256]{1,0:T(8,128)(2,1)S(1)}, u32[]{:S(2)}, u32[]{:S(2)}) collective-permute-start(bf16[384,256]{1,0:T(8,128)(2,1)S(1)} %collective-permute-done.5.refs_3_), channel_id=1, source_target_pairs={{0,32},{1,33},{2,34},{3,35},{4,36},{5,37},{6,38},{7,39},{8,40},{9,... | collective-permute-start | bytes 589832 | tf_op jit(solution)/shard_map/ppermute | solution.py:34
  15.0 7.3 %collective-permute-start.3 = (bf16[384,256]{1,0:T(8,128)(2,1)S(1)}, bf16[384,256]{1,0:T(8,128)(2,1)S(1)}, u32[]{:S(2)}, u32[]{:S(2)}) collective-permute-start(bf16[384,256]{1,0:T(8,128)(2,1)S(1)} %collective-permute-done.2.refs_2_), channel_id=1, source_target_pairs={{0,224},{1,225},{2,226},{3,227},{4,228},{5,229},{6,230},{7,231},{8... | collective-permute-start | bytes 589832 | tf_op jit(solution)/shard_map/ppermute | solution.py:34
  17.3 6.3 %collective-permute-start.8 = (bf16[384,256]{1,0:T(8,128)(2,1)S(1)}, bf16[384,256]{1,0:T(8,128)(2,1)S(1)}, u32[]{:S(2)}, u32[]{:S(2)}) collective-permute-start(bf16[384,256]{1,0:T(8,128)(2,1)S(1)} %maximum_maximum_fusion.1.refs_0_), channel_id=1, source_target_pairs={{0,8},{1,9},{2,10},{3,11},{4,12},{5,13},{6,14},{7,15},{8,0},{9,1},... | collective-permute-start | bytes 589832 | tf_op jit(solution)/shard_map/ppermute | solution.py:34
  18.8 7.8 %collective-permute-start.9 = (bf16[384,256]{1,0:T(8,128)(2,1)S(1)}, bf16[384,256]{1,0:T(8,128)(2,1)S(1)}, u32[]{:S(2)}, u32[]{:S(2)}) collective-permute-start(bf16[384,256]{1,0:T(8,128)(2,1)S(1)} %collective-permute-done.2.refs_2_), channel_id=1, source_target_pairs={{0,8},{1,9},{2,10},{3,11},{4,12},{5,13},{6,14},{7,15},{8,0},{9,1},... | collective-permute-start | bytes 589832 | tf_op jit(solution)/shard_map/ppermute | solution.py:34
  21.2 6.2 %collective-permute-start.10 = (bf16[384,256]{1,0:T(8,128)(2,1)S(1)}, bf16[384,256]{1,0:T(8,128)(2,1)S(1)}, u32[]{:S(2)}, u32[]{:S(2)}) collective-permute-start(bf16[384,256]{1,0:T(8,128)(2,1)S(1)} %collective-permute-done.5.refs_3_), channel_id=1, source_target_pairs={{0,8},{1,9},{2,10},{3,11},{4,12},{5,13},{6,14},{7,15},{8,0},{9,1},... | collective-permute-start | bytes 589832 | tf_op jit(solution)/shard_map/ppermute | solution.py:34
  22.3 5.5 %collective-permute-start.12 = (bf16[384,256]{1,0:T(8,128)(2,1)S(1)}, bf16[384,256]{1,0:T(8,128)(2,1)S(1)}, u32[]{:S(2)}, u32[]{:S(2)}) collective-permute-start(bf16[384,256]{1,0:T(8,128)(2,1)S(1)} %collective-permute-done.3.refs_7_), channel_id=1, source_target_pairs={{0,8},{1,9},{2,10},{3,11},{4,12},{5,13},{6,14},{7,15},{8,0},{9,1},... | collective-permute-start | bytes 589832 | tf_op jit(solution)/shard_map/ppermute | solution.py:34
  23.6 14.3 %collective-permute-start.18 = (bf16[256,512]{1,0:T(8,128)(2,1)S(1)}, bf16[256,512]{1,0:T(8,128)(2,1)S(1)}, u32[]{:S(2)}, u32[]{:S(2)}) collective-permute-start(bf16[256,512]{1,0:T(8,128)(2,1)S(1)} %get-tuple-element.63), channel_id=1, source_target_pairs={{0,16},{1,17},{2,18},{3,19},{4,20},{5,21},{6,22},{7,23},{8,24},{9,... | collective-permute-start | bytes 786440 | tf_op jit(solution)/shard_map/ppermute | solution.py:34
  26.6 12.5 %collective-permute-start.20 = (bf16[256,512]{1,0:T(8,128)(2,1)S(1)}, bf16[256,512]{1,0:T(8,128)(2,1)S(1)}, u32[]{:S(2)}, u32[]{:S(2)}) collective-permute-start(bf16[256,512]{1,0:T(8,128)(2,1)S(1)} %get-tuple-element.63), channel_id=1, source_target_pairs={{0,17},{1,16},{2,19},{3,18},{4,21},{5,20},{6,23},{7,22},{8,25},{9,... | collective-permute-start | bytes 786440 | tf_op jit(solution)/shard_map/ppermute | solution.py:34
  27.4 11.7 %collective-permute-start.19 = (bf16[256,512]{1,0:T(8,128)(2,1)S(1)}, bf16[256,512]{1,0:T(8,128)(2,1)S(1)}, u32[]{:S(2)}, u32[]{:S(2)}) collective-permute-start(bf16[256,512]{1,0:T(8,128)(2,1)S(1)} %get-tuple-element.52), channel_id=1, source_target_pairs={{0,1},{1,0},{2,3},{3,2},{4,5},{5,4},{6,7},{7,6},{8,9},{9,8},{10,11... | collective-permute-start | bytes 786440 | tf_op jit(solution)/shard_map/ppermute | solution.py:34
  27.4 9.3 %collective-permute-start.4 = (bf16[384,256]{1,0:T(8,128)(2,1)S(1)}, bf16[384,256]{1,0:T(8,128)(2,1)S(1)}, u32[]{:S(2)}, u32[]{:S(2)}) collective-permute-start(bf16[384,256]{1,0:T(8,128)(2,1)S(1)} %collective-permute-done.3.refs_7_), channel_id=1, source_target_pairs={{0,32},{1,33},{2,34},{3,35},{4,36},{5,37},{6,38},{7,39},{8,40},{9,... | collective-permute-start | bytes 589832 | tf_op jit(solution)/shard_map/ppermute | solution.py:34
  27.7 9.0 %collective-permute-start.7 = (bf16[384,256]{1,0:T(8,128)(2,1)S(1)}, bf16[384,256]{1,0:T(8,128)(2,1)S(1)}, u32[]{:S(2)}, u32[]{:S(2)}) collective-permute-start(bf16[384,256]{1,0:T(8,128)(2,1)S(1)} %collective-permute-done.6.refs_6_), channel_id=1, source_target_pairs={{0,224},{1,225},{2,226},{3,227},{4,228},{5,229},{6,230},{7,231},{8... | collective-permute-start | bytes 589832 | tf_op jit(solution)/shard_map/ppermute | solution.py:34
  36.8 13.6 %collective-permute-start.14 = (bf16[384,256]{1,0:T(8,128)(2,1)S(1)}, bf16[384,256]{1,0:T(8,128)(2,1)S(1)}, u32[]{:S(2)}, u32[]{:S(2)}) collective-permute-start(bf16[384,256]{1,0:T(8,128)(2,1)S(1)} %collective-permute-done.7.refs_1_), channel_id=1, source_target_pairs={{0,8},{1,9},{2,10},{3,11},{4,12},{5,13},{6,14},{7,15},{8,0},{9,1},... | collective-permute-start | bytes 589832 | tf_op jit(solution)/shard_map/ppermute | solution.py:34
  37.9 12.1 %collective-permute-start.15 = (bf16[384,256]{1,0:T(8,128)(2,1)S(1)}, bf16[384,256]{1,0:T(8,128)(2,1)S(1)}, u32[]{:S(2)}, u32[]{:S(2)}) collective-permute-start(bf16[384,256]{1,0:T(8,128)(2,1)S(1)} %collective-permute-done.7.refs_1_), channel_id=1, source_target_pairs={{0,32},{1,33},{2,34},{3,35},{4,36},{5,37},{6,38},{7,39},{8,40},{9,... | collective-permute-start | bytes 589832 | tf_op jit(solution)/shard_map/ppermute | solution.py:34
  39.3 40.1 %collective-permute-start.21 = (bf16[512,1024]{1,0:T(8,128)(2,1)S(1)}, bf16[512,1024]{1,0:T(8,128)(2,1)S(1)}, u32[]{:S(2)}, u32[]{:S(2)}) collective-permute-start(bf16[512,1024]{1,0:T(8,128)(2,1)S(1)} %maximum_maximum_fusion.refs_5_.refs_4_), channel_id=1, source_target_pairs={{0,2},{1,3},{2,4},{3,5},{4,6},{5,7},{6,0},{7,1},{8,10},{9,11},{10,... | collective-permute-start | bytes 3145736 | tf_op jit(solution)/shard_map/ppermute | solution.py:34
  40.6 38.8 %collective-permute-start.22 = (bf16[512,1024]{1,0:T(8,128)(2,1)S(1)}, bf16[512,1024]{1,0:T(8,128)(2,1)S(1)}, u32[]{:S(2)}, u32[]{:S(2)}) collective-permute-start(bf16[512,1024]{1,0:T(8,128)(2,1)S(1)} %maximum_maximum_fusion.refs_5_.refs_4_), channel_id=1, source_target_pairs={{0,6},{1,7},{2,0},{3,1},{4,2},{5,3},{6,4},{7,5},{8,14},{9,15},{10,... | collective-permute-start | bytes 3145736 | tf_op jit(solution)/shard_map/ppermute | solution.py:34
  42.0 8.3 %collective-permute-start.13 = (bf16[384,256]{1,0:T(8,128)(2,1)S(1)}, bf16[384,256]{1,0:T(8,128)(2,1)S(1)}, u32[]{:S(2)}, u32[]{:S(2)}) collective-permute-start(bf16[384,256]{1,0:T(8,128)(2,1)S(1)} %collective-permute-done.4.refs_0_), channel_id=1, source_target_pairs={{0,8},{1,9},{2,10},{3,11},{4,12},{5,13},{6,14},{7,15},{8,0},{9,1},... | collective-permute-start | bytes 589832 | tf_op jit(solution)/shard_map/ppermute | solution.py:34
  79.4 7.8 %collective-permute-start.24 = (bf16[64,2048]{1,0:T(8,128)(2,1)S(1)}, bf16[64,2048]{1,0:T(8,128)(2,1)S(1)}, u32[]{:S(2)}, u32[]{:S(2)}) collective-permute-start(bf16[64,2048]{1,0:T(8,128)(2,1)S(1)} %shard_map.76.refs_0_), channel_id=1, source_target_pairs={{0,224},{1,225},{2,226},{3,227},{4,228},{5,229},{6,230},{7,231},{8... | collective-permute-start | bytes 786440 | tf_op jit(solution)/shard_map/ppermute | solution.py:34
  81.8 6.3 %collective-permute-start.23 = (bf16[64,2048]{1,0:T(8,128)(2,1)S(1)}, bf16[64,2048]{1,0:T(8,128)(2,1)S(1)}, u32[]{:S(2)}, u32[]{:S(2)}) collective-permute-start(bf16[64,2048]{1,0:T(8,128)(2,1)S(1)} %shard_map.76.refs_0_), channel_id=1, source_target_pairs={{0,32},{1,33},{2,34},{3,35},{4,36},{5,37},{6,38},{7,39},{8,40},{9,... | collective-permute-start | bytes 786440 | tf_op jit(solution)/shard_map/ppermute | solution.py:34
  87.2 6.1 %collective-permute-start.25 = (bf16[64,2048]{1,0:T(8,128)(2,1)S(1)}, bf16[64,2048]{1,0:T(8,128)(2,1)S(1)}, u32[]{:S(2)}, u32[]{:S(2)}) collective-permute-start(bf16[64,2048]{1,0:T(8,128)(2,1)S(1)} %collective-permute-done.24.refs_2_), channel_id=1, source_target_pairs={{0,32},{1,33},{2,34},{3,35},{4,36},{5,37},{6,38},{7,39},{8,40},{9,... | collective-permute-start | bytes 786440 | tf_op jit(solution)/shard_map/ppermute | solution.py:34
  88.1 7.1 %collective-permute-start.26 = (bf16[64,2048]{1,0:T(8,128)(2,1)S(1)}, bf16[64,2048]{1,0:T(8,128)(2,1)S(1)}, u32[]{:S(2)}, u32[]{:S(2)}) collective-permute-start(bf16[64,2048]{1,0:T(8,128)(2,1)S(1)} %collective-permute-done.23.refs_1_), channel_id=1, source_target_pairs={{0,224},{1,225},{2,226},{3,227},{4,228},{5,229},{6,230},{7,231},{8... | collective-permute-start | bytes 786440 | tf_op jit(solution)/shard_map/ppermute | solution.py:34
  89.6 13.6 %collective-permute-start.27 = (bf16[256,1024]{1,0:T(8,128)(2,1)S(1)}, bf16[256,1024]{1,0:T(8,128)(2,1)S(1)}, u32[]{:S(2)}, u32[]{:S(2)}) collective-permute-start(bf16[256,1024]{1,0:T(8,128)(2,1)S(1)} %slice.20), channel_id=1, source_target_pairs={{0,2},{1,3},{2,4},{3,5},{4,6},{5,7},{6,0},{7,1},{8,10},{9,11},{10,... | collective-permute-start | bytes 1572872 | tf_op jit(solution)/shard_map/ppermute | solution.py:34
  89.8 13.5 %collective-permute-start.28 = (bf16[256,1024]{1,0:T(8,128)(2,1)S(1)}, bf16[256,1024]{1,0:T(8,128)(2,1)S(1)}, u32[]{:S(2)}, u32[]{:S(2)}) collective-permute-start(bf16[256,1024]{1,0:T(8,128)(2,1)S(1)} %slice.21), channel_id=1, source_target_pairs={{0,6},{1,7},{2,0},{3,1},{4,2},{5,3},{6,4},{7,5},{8,14},{9,15},{10,... | collective-permute-start | bytes 1572872 | tf_op jit(solution)/shard_map/ppermute | solution.py:34
  93.3 7.5 %collective-permute-start.31 = (bf16[64,2048]{1,0:T(8,128)(2,1)S(1)}, bf16[64,2048]{1,0:T(8,128)(2,1)S(1)}, u32[]{:S(2)}, u32[]{:S(2)}) collective-permute-start(bf16[64,2048]{1,0:T(8,128)(2,1)S(1)} %collective-permute-done.25.refs_3_), channel_id=1, source_target_pairs={{0,224},{1,225},{2,226},{3,227},{4,228},{5,229},{6,230},{7,231},{8... | collective-permute-start | bytes 786440 | tf_op jit(solution)/shard_map/ppermute | solution.py:34
  95.2 5.7 %collective-permute-start.30 = (bf16[64,2048]{1,0:T(8,128)(2,1)S(1)}, bf16[64,2048]{1,0:T(8,128)(2,1)S(1)}, u32[]{:S(2)}, u32[]{:S(2)}) collective-permute-start(bf16[64,2048]{1,0:T(8,128)(2,1)S(1)} %collective-permute-done.26.refs_4_), channel_id=1, source_target_pairs={{0,32},{1,33},{2,34},{3,35},{4,36},{5,37},{6,38},{7,39},{8,40},{9,... | collective-permute-start | bytes 786440 | tf_op jit(solution)/shard_map/ppermute | solution.py:34
  100.9 7.7 %collective-permute-start.32 = (bf16[32,2048]{1,0:T(8,128)(2,1)S(1)}, bf16[32,2048]{1,0:T(8,128)(2,1)S(1)}, u32[]{:S(2)}, u32[]{:S(2)}) collective-permute-start(bf16[32,2048]{1,0:T(8,128)(2,1)S(1)} %slice.26), channel_id=1, source_target_pairs={{0,32},{1,33},{2,34},{3,35},{4,36},{5,37},{6,38},{7,39},{8,40},{9,... | collective-permute-start | bytes 393224 | tf_op jit(solution)/shard_map/ppermute | solution.py:34
  101.0 7.6 %collective-permute-start.33 = (bf16[32,2048]{1,0:T(8,128)(2,1)S(1)}, bf16[32,2048]{1,0:T(8,128)(2,1)S(1)}, u32[]{:S(2)}, u32[]{:S(2)}) collective-permute-start(bf16[32,2048]{1,0:T(8,128)(2,1)S(1)} %slice.27), channel_id=1, source_target_pairs={{0,224},{1,225},{2,226},{3,227},{4,228},{5,229},{6,230},{7,231},{8... | collective-permute-start | bytes 393224 | tf_op jit(solution)/shard_map/ppermute | solution.py:34
  104.8 9.1 %collective-permute-start.29 = (bf16[320,512]{1,0:T(8,128)(2,1)S(1)}, bf16[320,512]{1,0:T(8,128)(2,1)S(1)}, u32[]{:S(2)}, u32[]{:S(2)}) collective-permute-start(bf16[320,512]{1,0:T(8,128)(2,1)S(1)} %get-tuple-element.60), channel_id=1, source_target_pairs={{0,8},{1,9},{2,10},{3,11},{4,12},{5,13},{6,14},{7,15},{8,0},{9,1},... | collective-permute-start | bytes 983048 | tf_op jit(solution)/shard_map/ppermute | solution.py:34
  (5 other events, 35.4 us)
